TPU v7x, 128 devices: a whole 4x4x4 slice. The times are simulated.
128 devices in a mesh: section: 2 (over core), expert: 64 (over z, y, x), dp: 1.
Axes of the slice: x: 4, y: 4, z: 4, core: 2. Of those that a mesh axis runs over, the one named last changes fastest.
Arguments:
- w_up: bfloat16 [2, 32768, 1536], P('section', 'expert'), may hold values from -0.15625 to 0.15625
- saved_rows: bfloat16 [2, 4096, 2048], P('section', ('dp', 'expert')), may hold values from -6 to 6
- hidden_grad: bfloat16 [2, 4096, 8, 1536], P('section', ('dp', 'expert')), may hold values from -6 to 6
- expert_ids: int32 [2, 4096, 8], P('section', ('dp', 'expert')), may hold values from 0 to 15, all different within a row; in each aligned block of 64 rows (0 to 63, 64 to 127, ..., all dimensions but the last counted through in order) at most 48 rows name the same one
- route_weight: float32 [2, 4096, 8], P('section', ('dp', 'expert')), may hold values from 0.1 to 1
Outputs:
- weight_grad: bfloat16 [2, 32768, 1536], P('section', ('dp', 'expert'))
- upstream: bfloat16 [2, 4096, 2048], P('section', ('dp', 'expert'))
Inputs may be any that keep to these rules, and one draw needn't show every extreme that they name: `expert_ids`: each token names 8 different experts. In each aligned block of 64 tokens of a segment (the tokens of one device), no expert is chosen by more than 48 tokens, and in some block one expert is chosen by exactly 48.
All inputs are finite; a program needn't handle non-finite values.
Results may differ from a plain program's by a relative error of at most 0.0057.
Values may be sent and summed in bfloat16 or wider, within the bound.
No kernel may reach another device: no remote copies, remote signals or barrier semaphores. Data moves between devices by JAX's collectives and lax.ppermute only.
A program may use at most 128 MiB of HBM per device.

v0:
```python
import jax
import jax.numpy as jnp
from jax import lax
from jax.sharding import PartitionSpec as P

loss_scale_inverse = 0.0625


def passed_along(x, axis, by):
    size = lax.axis_size(axis)
    pairs = [(i, i + by) for i in range(size) if 0 <= i + by < size]
    return lax.ppermute(x, axis, pairs)


def body(w_up, saved_rows, hidden_grad, expert_ids, route_weight):
    owners = lax.axis_size("expert")
    group_size = min(4, owners)
    experts = owners // group_size
    tokens = saved_rows.shape[1]
    model_width = saved_rows.shape[2]
    top_count = hidden_grad.shape[2]
    hidden = hidden_grad.shape[3]
    slice_width = model_width // group_size
    capacity = 3 * tokens * top_count // (2 * experts)
    routes = tokens * top_count
    chosen = expert_ids[0].reshape(routes)
    onehot = (chosen[:, None] == jnp.arange(experts, dtype=jnp.int32)[None, :]).astype(jnp.int32)
    before = jnp.cumsum(onehot, axis=0) - onehot
    position = jnp.sum(before * onehot, axis=1)
    target = chosen * capacity + position
    placing = (jnp.arange(experts * capacity, dtype=jnp.int32)[:, None] == target[None, :]).astype(
        jnp.bfloat16
    )
    placing_tok = jnp.sum(
        placing.reshape(experts * capacity, tokens, top_count).astype(jnp.float32), axis=2
    ).astype(jnp.bfloat16)
    scaled = (
        (route_weight[0][:, :, None] * hidden_grad[0].astype(jnp.float32))
        .astype(jnp.bfloat16)
        .reshape(routes, hidden)
    )
    packed_grad = jnp.dot(placing, scaled, preferred_element_type=jnp.float32).astype(jnp.bfloat16)
    packed_rows = jnp.dot(placing_tok, saved_rows[0], preferred_element_type=jnp.float32).astype(
        jnp.bfloat16
    )
    rows_out = packed_rows.reshape(experts, capacity, group_size, slice_width)
    rows_out = rows_out.transpose(0, 2, 1, 3).reshape(owners, capacity, slice_width)
    rows_in = lax.all_to_all(rows_out, "expert", split_axis=0, concat_axis=0, tiled=True)
    grad_out = jnp.broadcast_to(
        packed_grad.reshape(experts, 1, capacity, hidden), (experts, group_size, capacity, hidden)
    )
    grad_in = lax.all_to_all(
        grad_out.reshape(owners, capacity, hidden),
        "expert",
        split_axis=0,
        concat_axis=0,
        tiled=True,
    )
    weight_local = w_up[0]
    flat_grad = grad_in.reshape(owners * capacity, hidden)
    part_grad = lax.dot_general(
        flat_grad, weight_local, (((1,), (1,)), ((), ())), preferred_element_type=jnp.float32
    ).astype(jnp.bfloat16)
    flat_rows = rows_in.reshape(owners * capacity, slice_width)
    summed = lax.dot_general(
        flat_rows, flat_grad, (((0,), (0,)), ((), ())), preferred_element_type=jnp.float32
    )
    weight_grad = (summed * loss_scale_inverse).astype(jnp.bfloat16)
    returned = lax.all_to_all(
        part_grad.reshape(owners, capacity, slice_width),
        "expert",
        split_axis=0,
        concat_axis=0,
        tiled=True,
    )
    assembled = returned.reshape(experts, group_size, capacity, slice_width)
    assembled = assembled.transpose(0, 2, 1, 3).reshape(experts * capacity, model_width)
    row_grad = lax.dot_general(
        placing_tok, assembled, (((0,), (0,)), ((), ())), preferred_element_type=jnp.float32
    ).astype(jnp.bfloat16)
    upstream = passed_along(row_grad[None], "section", -1)
    return (weight_grad[None], upstream)


def solution(mesh):
    return jax.shard_map(
        body,
        mesh=mesh,
        in_specs=(
            P("section", "expert", None),
            P("section", ("dp", "expert"), None),
            P("section", ("dp", "expert"), None, None),
            P("section", ("dp", "expert"), None),
            P("section", ("dp", "expert"), None),
        ),
        out_specs=(P("section", ("dp", "expert"), None), P("section", ("dp", "expert"), None)),
        check_vma=False,
    )
```

profile of v0, /device:TPU:0, one launch (start us, length us, event | category | flops | bytes accessed | tf_op | source)
XLA Modules:
  0.0 246.7 jit_solution(14034292750912324187)
XLA Ops:
  0.6 0.0 copy-start
  0.6 0.9 copy.36
  1.5 0.1 eq.50
  1.6 0.1 eq.46
  1.7 1.2 reduce-window.6
  2.9 0.2 slice_reduce_fusion
  3.1 0.1 fusion.15
  3.3 0.8 copy.41
  4.0 0.1 mul.44
  4.1 2.9 %convolution_convert_fusion.2 = bf16[768,1536]{1,0:T(8,128)(2,1)S(1)} fusion(bf16[1,64,8,1536]{3,2,1,0:T(8,128)(2,1)} %param.7, f32[512]{0:T(512)S(1)} %mul.44, s32[512]{0:T(512)S(1)} %multiply_add_fusion), kind=kOutput, calls=%fused_computation.2 | convolution fusion | flops 1211891712 | bytes 3936256 | tf_op jit(solution)/shard_map/dot_general | solution.py:42
  7.0 4.8 %broadcast_in_dim.17 = bf16[16,4,48,1536]{3,2,1,0:T(8,128)(2,1)} broadcast(bf16[16,48,1536]{2,1,0:T(8,128)(2,1)S(1)} %bitcast.70), dimensions={0,2,3} | broadcast | bytes 11796480 | tf_op jit(solution)/shard_map/broadcast_in_dim | solution.py:49
  11.9 123.5 %all_to_all.15 = bf16[64,48,1536]{2,1,0:T(8,128)(2,1)S(1)} all-to-all(bf16[64,48,1536]{2,1,0:T(8,128)(2,1)} %bitcast.63), channel_id=1, replica_groups=mesh['section'=2,'expert'=64,'dp'=1] {'expert'}, dimensions={0} | all-to-all | bytes 18874368 | tf_op jit(solution)/shard_map/all_to_all | solution.py:52
  135.4 0.0 copy-done
  135.4 6.8 %convolution_convert_fusion = bf16[3072,512]{1,0:T(8,128)(2,1)} fusion(bf16[3072,1536]{1,0:T(8,128)(2,1)S(1)} %bitcast.68, bf16[1,512,1536]{2,1,0:T(8,128)(2,1)S(1)} %copy-done), kind=kOutput, calls=%fused_computation | convolution fusion | flops 4833411072 | bytes 14155776 | tf_op jit(solution)/shard_map/dot_general | solution.py:61
  142.2 0.0 copy-done.1
  142.2 5.7 %all-to-all-start.2 = ((bf16[64,48,512]{2,1,0:T(8,128)(2,1)}), bf16[64,48,512]{2,1,0:T(8,128)(2,1)}, u32[]{:S(2)}, u32[]{:S(2)}) async-start(bf16[64,48,512]{2,1,0:T(8,128)(2,1)} %bitcast.69), calls=%async_computation.2 | async-start | bytes 6291456 | tf_op jit(solution)/shard_map/all_to_all | solution.py:69
  147.9 0.1 reduce_sum.24
  148.0 0.5 fusion.10
  148.6 0.0 copy-done.2
  148.6 2.7 %convolution_convert_fusion.1 = bf16[768,2048]{1,0:T(8,128)(2,1)} fusion(bf16[768,64]{0,1:T(8,128)(2,1)S(1)} %fusion.10, bf16[1,64,2048]{2,1,0:T(8,128)(2,1)S(1)} %copy-done.2), kind=kOutput, calls=%fused_computation.1 | convolution fusion | flops 202899456 | bytes 3506176 | tf_op jit(solution)/shard_map/dot_general | solution.py:43
  151.3 6.2 %reshape.74 = bf16[16,48,4,512]{3,2,1,0:T(4,128)(2,1)} reshape(bf16[768,2048]{1,0:T(8,128)(2,1)} %convolution_convert_fusion.1) | data formatting | bytes 6291456 | tf_op jit(solution)/shard_map/reshape | solution.py:46
  157.4 4.4 %copy.40 = bf16[16,4,48,512]{3,2,1,0:T(8,128)(2,1)} copy(bf16[16,4,48,512]{3,1,2,0:T(4,128)(2,1)} %bitcast.66) | data formatting | bytes 6291456 | tf_op jit(solution)/shard_map/transpose | solution.py:47
  161.9 26.1 %all-to-all-done.2 = bf16[64,48,512]{2,1,0:T(8,128)(2,1)} async-done(((bf16[64,48,512]{2,1,0:T(8,128)(2,1)}), bf16[64,48,512]{2,1,0:T(8,128)(2,1)}, u32[]{:S(2)}, u32[]{:S(2)}) %all-to-all-start.2) | async-done | bytes 3145760 | tf_op jit(solution)/shard_map/all_to_all | solution.py:69
  188.0 6.5 %all-to-all-start = ((bf16[64,48,512]{2,1,0:T(8,128)(2,1)}), bf16[64,48,512]{2,1,0:T(8,128)(2,1)}, u32[]{:S(2)}, u32[]{:S(2)}) async-start(bf16[64,48,512]{2,1,0:T(8,128)(2,1)} %bitcast.64), calls=%async_computation | async-start | bytes 6291456 | tf_op jit(solution)/shard_map/all_to_all | solution.py:48
  194.5 4.5 %copy.42 = bf16[16,48,4,512]{3,2,1,0:T(4,128)(2,1)S(1)} copy(bf16[16,48,4,512]{3,1,2,0:T(8,128)(2,1)} %bitcast.14) | data formatting | bytes 6291456 | tf_op jit(solution)/shard_map/transpose | solution.py:77
  199.0 1.0 copy.44
  200.1 0.7 fusion.4
  200.7 1.3 collective-permute-start
  202.0 33.7 %all-to-all-done = bf16[64,48,512]{2,1,0:T(8,128)(2,1)} async-done(((bf16[64,48,512]{2,1,0:T(8,128)(2,1)}), bf16[64,48,512]{2,1,0:T(8,128)(2,1)}, u32[]{:S(2)}, u32[]{:S(2)}) %all-to-all-start) | async-done | bytes 3145760 | tf_op jit(solution)/shard_map/all_to_all | solution.py:48
  235.7 10.3 %fusion.3 = bf16[1,512,1536]{2,1,0:T(8,128)(2,1)} fusion(bf16[64,48,512]{2,1,0:T(8,128)(2,1)} %all-to-all-done, bf16[64,48,1536]{2,1,0:T(8,128)(2,1)} %copy-done.1), kind=kOutput, calls=%fused_computation.8 | convolution fusion | flops 4833411072 | bytes 14155776 | tf_op jit(solution)/shard_map/dot_general | solution.py:65
  246.0 0.0 collective-permute-done
  246.0 0.7 copy.47
  (7 shorter events, 0.1 us)
Async XLA Ops:
  0.6 134.8 %copy-start = (bf16[1,512,1536]{2,1,0:T(8,128)(2,1)S(1)}, bf16[1,512,1536]{2,1,0:T(8,128)(2,1)}, u32[]{:S(2)}) copy-start(bf16[1,512,1536]{2,1,0:T(8,128)(2,1)} %param.5) | copy-start | bytes 4718596
  135.4 6.8 %copy-start.1 = (bf16[64,48,1536]{2,1,0:T(8,128)(2,1)}, bf16[64,48,1536]{2,1,0:T(8,128)(2,1)S(1)}, u32[]{:S(2)}) copy-start(bf16[64,48,1536]{2,1,0:T(8,128)(2,1)S(1)} %all_to_all.15) | copy-start | bytes 28311556
  142.2 6.4 %copy-start.2 = (bf16[1,64,2048]{2,1,0:T(8,128)(2,1)S(1)}, bf16[1,64,2048]{2,1,0:T(8,128)(2,1)}, u32[]{:S(2)}) copy-start(bf16[1,64,2048]{2,1,0:T(8,128)(2,1)} %param.6) | copy-start | bytes 786436
  142.2 45.8 %all-to-all-start.2 = ((bf16[64,48,512]{2,1,0:T(8,128)(2,1)}), bf16[64,48,512]{2,1,0:T(8,128)(2,1)}, u32[]{:S(2)}, u32[]{:S(2)}) async-start(bf16[64,48,512]{2,1,0:T(8,128)(2,1)} %bitcast.69), calls=%async_computation.2 | async-start | bytes 6291456 | tf_op jit(solution)/shard_map/all_to_all | solution.py:69
  188.0 47.7 %all-to-all-start = ((bf16[64,48,512]{2,1,0:T(8,128)(2,1)}), bf16[64,48,512]{2,1,0:T(8,128)(2,1)}, u32[]{:S(2)}, u32[]{:S(2)}) async-start(bf16[64,48,512]{2,1,0:T(8,128)(2,1)} %bitcast.64), calls=%async_computation | async-start | bytes 6291456 | tf_op jit(solution)/shard_map/all_to_all | solution.py:48
  200.7 45.3 %collective-permute-start = (bf16[1,64,2048]{2,1,0:T(8,128)(2,1)S(1)}, bf16[1,64,2048]{2,1,0:T(8,128)(2,1)S(1)}, u32[]{:S(2)}, u32[]{:S(2)}) collective-permute-start(bf16[1,64,2048]{2,1,0:T(8,128)(2,1)S(1)} %fusion.4), channel_id=1, source_target_pairs={{64,0},{65,1},{66,2},{67,3},{68,4},{69,5},{70,6},{71,7},{72,8},{73... | collective-permute-start | bytes 786440 | tf_op jit(solution)/shard_map/ppermute | solution.py:12
where the time goes:
time: 247 us
  blocking collectives  124 us (50%)
  waiting for transfers between devices  59.8 us (24%)
  local copies, waits for them, and re-layouts  23.9 us (10%)
  matrix products  23.3 us (9%)
  starting transfers between devices  13.5 us (5%)
    all_to_all x1, blocking collectives, body(): lax.all_to_all(grad_out.reshape(owners, capacity, hidden), 'expert', spli...  124 us
    all_to_all x1, waiting for transfers between devices, body(): lax.all_to_all(rows_out, 'expert', split_axis=0, concat_axis=0, tiled=True)  33.7 us
    all_to_all x1, waiting for transfers between devices, body(): lax.all_to_all(part_grad.reshape(owners, capacity, slice_width), 'expert'...  26.1 us
    dot_general x1, matrix products, body(): lax.dot_general(flat_rows, flat_grad, (((0,), (0,)), ((), ())), preferred...  10.3 us
    dot_general x1, matrix products, body(): lax.dot_general(flat_grad, weight_local, (((1,), (1,)), ((), ())), prefer...  6.82 us
    all_to_all x1, starting transfers between devices, body(): lax.all_to_all(rows_out, 'expert', split_axis=0, concat_axis=0, tiled=True)  6.5 us
    reshape x1, local copies, waits for them, and re-layouts, body(): rows_out = packed_rows.reshape(experts, capacity, group_size, slice_width)  6.17 us
    all_to_all x1, starting transfers between devices, body(): lax.all_to_all(part_grad.reshape(owners, capacity, slice_width), 'expert'...  5.71 us
  transfers between devices with their start and end apart: 3, of which 2 were waited for; matrix products, arithmetic and copies ran while one was open for 12% of the time, Pallas kernels for 0%

commit v1 on v0

v1 whole, which is shorter than its diff:
```python
import jax
import jax.numpy as jnp
from jax import lax
from jax.sharding import Mesh, PartitionSpec as P

loss_scale_inverse = 0.0625
bf16 = jnp.bfloat16
f32 = jnp.float32
ZY = ("z", "y")
CHUNKS = 2
TOKEN_PAIRS = [(0, 1), (1, 0), (2, 3), (3, 2)]
FEATURE_PAIRS = [(0, 3), (3, 0), (1, 2), (2, 1)]


def dot(a, b, dims):
    return lax.dot_general(a, b, (dims, ((), ())), preferred_element_type=f32)


def positions(ids, experts):
    chosen = jnp.any(ids[:, None, :, :] == jnp.arange(experts, dtype=ids.dtype)[None, :, None, None], axis=3)
    tokens = ids.shape[1]
    row = lax.broadcasted_iota(jnp.int32, (tokens, tokens), 0)
    col = lax.broadcasted_iota(jnp.int32, (tokens, tokens), 1)
    earlier = (row < col).astype(bf16)
    slot = dot(chosen.astype(bf16), earlier, ((2,), (0,)))
    return chosen, slot.astype(jnp.int32)


def body(w_up, saved_rows, hidden_grad, expert_ids, route_weight):
    experts = lax.axis_size("z") * lax.axis_size("y")
    x = lax.axis_index("x")
    me = lax.axis_index("z") * lax.axis_size("y") + lax.axis_index("y")
    tokens = saved_rows.shape[1]
    width = saved_rows.shape[2]
    top = hidden_grad.shape[2]
    hidden = hidden_grad.shape[3]
    quarter = width // 4
    half = width // 2
    capacity = 3 * tokens * top // (2 * experts)
    part = hidden // CHUNKS

    w_own = w_up[0]
    w_other = lax.ppermute(w_own, "x", FEATURE_PAIRS)

    def features(a, q):
        return lax.dynamic_slice_in_dim(a, q * quarter, quarter, 1)

    rows = saved_rows[0]
    ids = expert_ids[0]
    mate = jnp.bitwise_xor(x, 1)
    for_mate = jnp.concatenate(
        [features(rows, mate), features(rows, 3 - mate)], axis=1
    )
    id_wide = jnp.pad(ids.T.astype(bf16), ((0, 0), (0, half - tokens)))
    out_rows = jnp.concatenate([for_mate, id_wide], axis=0)
    mate_rows = lax.ppermute(out_rows, "x", TOKEN_PAIRS)
    mine = jnp.concatenate([features(rows, x), features(rows, 3 - x)], axis=1)
    mate_ids_t = mate_rows[tokens:, :tokens]
    id_both = jnp.concatenate(
        [ids.T.astype(bf16), mate_ids_t], axis=1
    )
    id_both = jnp.pad(id_both, ((0, 0), (0, half - 2 * tokens)))
    block = jnp.concatenate([mine, mate_rows[:tokens], id_both], axis=0)
    gathered = lax.all_gather(block, ZY, tiled=False)
    gathered = gathered.reshape(experts, 2 * tokens + top, half)

    both_ids = jnp.stack([ids, mate_ids_t.T.astype(jnp.int32)])
    chosen, slot = positions(both_ids, experts)
    slots = jnp.arange(capacity, dtype=jnp.int32)
    place_tok = jnp.logical_and(
        chosen[:, :, None, :], slot[:, :, None, :] == slots[None, None, :, None]
    ).astype(bf16)
    place_tok = place_tok.reshape(2, experts * capacity, tokens)
    hit = ids[None, :, :] == jnp.arange(experts, dtype=jnp.int32)[:, None, None]
    place = jnp.logical_and(
        hit[:, None, :, :], (slot[0][:, None, :] == slots[None, :, None])[:, :, :, None]
    ).astype(bf16)
    place = place.reshape(experts * capacity, tokens * top)
    scaled = (route_weight[0][:, :, None] * hidden_grad[0].astype(f32)).astype(bf16)
    scaled = scaled.reshape(tokens * top, hidden)

    own_grad, mate_grad = [], []
    for c in range(CHUNKS):
        packed = dot(place, scaled[:, c * part : (c + 1) * part], ((1,), (0,))).astype(bf16)
        got = lax.all_to_all(
            packed.reshape(experts, capacity, part), ZY, 0, 0, tiled=True
        ).reshape(experts * capacity, part)
        own_grad.append(got)
        mate_grad.append(lax.ppermute(got, "x", TOKEN_PAIRS))

    def route_grad(grads):
        outs = []
        for w in (w_own, w_other):
            total = dot(grads[0], w[:, :part], ((1,), (1,)))
            for c in range(1, CHUNKS):
                total = total + dot(grads[c], w[:, c * part : (c + 1) * part], ((1,), (1,)))
            outs.append(total.astype(bf16))
        out = jnp.concatenate(outs, axis=1).reshape(experts, capacity, half)
        back = lax.all_to_all(out, ZY, 0, 0, tiled=True)
        return back.reshape(experts * capacity, half)

    back_own = route_grad(own_grad)
    sum_own = dot(place_tok[0], back_own, ((0,), (0,))).astype(bf16)
    back_mate = route_grad(mate_grad)
    sum_mate = dot(place_tok[1], back_mate, ((0,), (0,))).astype(bf16)

    to_own = [(4 + i, i) for i in range(4)]
    to_mate = [(4 + i, j) for i, j in TOKEN_PAIRS]
    up_own = lax.ppermute(sum_own, ("section", "x"), to_own)
    up_mate = lax.ppermute(sum_mate, ("section", "x"), to_mate)
    pieces = []
    for q in range(4):
        pieces.append(
            jnp.where(
                q == x,
                up_own[:, :quarter],
                jnp.where(
                    q == 3 - x,
                    up_own[:, quarter:],
                    jnp.where(q == mate, up_mate[:, :quarter], up_mate[:, quarter:]),
                ),
            )
        )
    upstream = jnp.concatenate(pieces, axis=1)

    all_ids = gathered[:, 2 * tokens :, : 2 * tokens]
    named = jnp.any(all_ids == me.astype(bf16), axis=1).reshape(experts, 2, tokens)
    row = lax.broadcasted_iota(jnp.int32, (tokens, tokens), 0)
    col = lax.broadcasted_iota(jnp.int32, (tokens, tokens), 1)
    where = dot(named.astype(bf16), (row < col).astype(bf16), ((2,), (0,))).astype(jnp.int32)
    pick = jnp.logical_and(
        named[:, :, None, :], where[:, :, None, :] == slots[None, None, :, None]
    ).astype(bf16)
    plane_rows = []
    for p in range(2):
        plane = gathered[:, p * tokens : (p + 1) * tokens]
        plane_rows.append(
            lax.dot_general(
                pick[:, p], plane, (((2,), (1,)), ((0,), (0,))), preferred_element_type=f32
            )
            .astype(bf16)
            .reshape(experts * capacity, half)
        )
    outs = []
    for c in range(CHUNKS):
        def partial(lo):
            total = dot(plane_rows[0][:, lo : lo + quarter], own_grad[c], ((0,), (0,)))
            return total + dot(plane_rows[1][:, lo : lo + quarter], mate_grad[c], ((0,), (0,)))

        theirs = lax.ppermute(partial(quarter).astype(bf16), "x", FEATURE_PAIRS)
        summed = partial(0) + theirs.astype(f32)
        outs.append((summed * loss_scale_inverse).astype(bf16))
    weight_grad = jnp.concatenate(outs, axis=1)
    return weight_grad[None], upstream[None]


def solution(mesh):
    grid = Mesh(mesh.devices.reshape(2, 4, 4, 4), ("section", "z", "y", "x"))
    expert = ("z", "y", "x")
    return jax.shard_map(
        body,
        mesh=grid,
        in_specs=(
            P("section", expert, None),
            P("section", expert, None),
            P("section", expert, None, None),
            P("section", expert, None),
            P("section", expert, None),
        ),
        out_specs=(P("section", expert, None), P("section", expert, None)),
        check_vma=False,
    )
```

time: 247 us -> 216 us (0.87)
  blocking collectives: 124 us -> 0 us
  waiting for transfers between devices: 59.8 us -> 109 us
  starting transfers between devices: 13.5 us -> 34.9 us
  matrix products: 23.3 us -> 39.5 us
  local copies, waits for them, and re-layouts: 23.9 us -> 7.97 us
  between operations: 0.74 us -> 14.5 us
  other arithmetic: 1.83 us -> 8.97 us
    all_to_all x1 -> x0, blocking collectives: 124 us -> none  [body(): lax.all_to_all(grad_out.reshape(owners, capacity, hidden), 'expert', spli...]
    ppermute x1 -> x8, waiting for transfers between devices: 0.01 us -> 35.5 us  [the longest x2 24.5 us: body(): theirs = lax.ppermute(partial(quarter).astype(bf16), 'x', FEATURE_PAIRS)]
    dot_general x5 -> x24, matrix products: 23.3 us -> 39.5 us  [the longest x22 35.2 us: dot(): return lax.dot_general(a, b, (dims, ((), ())), preferred_element_type=f32)]
    all_to_all x2 -> x4, waiting for transfers between devices: 59.8 us -> 73.1 us  [the longest x2 44.4 us: body(): lax.all_to_all(packed.reshape(experts, capacity, part), ZY, 0, 0, tiled=T...]
    ppermute x1 -> x8, starting transfers between devices: 1.29 us -> 12 us  [the longest x2 3.42 us: body(): theirs = lax.ppermute(partial(quarter).astype(bf16), 'x', FEATURE_PAIRS)]
    all_to_all x2 -> x4, starting transfers between devices: 12.2 us -> 22.8 us  [the longest x2 12 us: body(): lax.all_to_all(packed.reshape(experts, capacity, part), ZY, 0, 0, tiled=T...]
    transpose x2 -> x0, local copies, waits for them, and re-layouts: 8.97 us -> none  [the longest x1 4.53 us: body(): assembled.transpose(0, 2, 1, 3).reshape(experts * capacity, model_width)]
    reshape x1 -> x0, local copies, waits for them, and re-layouts: 6.17 us -> none  [body(): rows_out = packed_rows.reshape(experts, capacity, group_size, slice_width)]
  transfers between devices with their start and end apart: 3 -> 13, of which waited for: 2 -> 10; matrix products, arithmetic and copies ran while one was open for 12% -> 18% of each run, Pallas kernels for 0% -> 0%
where the time goes in v1:
time: 216 us; the launch traced here: 214 us
  waiting for transfers between devices  109 us (50%)
  matrix products  39.5 us (18%)
  starting transfers between devices  34.9 us (16%)
  between operations  14.5 us (7%)
  other arithmetic  8.97 us (4%)
  local copies, waits for them, and re-layouts  7.97 us (4%)
    all_to_all x2, waiting for transfers between devices, body(): lax.all_to_all(packed.reshape(experts, capacity, part), ZY, 0, 0, tiled=T...  44.4 us
    dot_general x22, matrix products, dot(): return lax.dot_general(a, b, (dims, ((), ())), preferred_element_type=f32)  35.2 us
    all_to_all x2, waiting for transfers between devices, route_grad(): back = lax.all_to_all(out, ZY, 0, 0, tiled=True)  28.7 us
    ppermute x2, waiting for transfers between devices, body(): theirs = lax.ppermute(partial(quarter).astype(bf16), 'x', FEATURE_PAIRS)  24.5 us
    all_to_all x2, starting transfers between devices, body(): lax.all_to_all(packed.reshape(experts, capacity, part), ZY, 0, 0, tiled=T...  12 us
    all_to_all x2, starting transfers between devices, route_grad(): back = lax.all_to_all(out, ZY, 0, 0, tiled=True)  10.8 us
    ppermute x1, waiting for transfers between devices, body(): up_mate = lax.ppermute(sum_mate, ('section', 'x'), to_mate)  4.93 us
    ppermute x1, waiting for transfers between devices, body(): w_other = lax.ppermute(w_own, 'x', FEATURE_PAIRS)  4.81 us
  transfers between devices with their start and end apart: 13, of which 10 were waited for; matrix products, arithmetic and copies ran while one was open for 18% of the time, Pallas kernels for 0%

profile of v1, /device:TPU:0, one launch (start us, length us, event | category | flops | bytes accessed | tf_op | source)
XLA Modules:
  0.0 214.4 jit_solution(5439548231689453290)
XLA Ops:
  17.2 1.9 and.44
  19.1 1.8 convolution_convert_fusion
  20.9 8.3 %all-to-all-start.1 = ((bf16[16,48,768]{2,1,0:T(8,128)(2,1)}), bf16[16,48,768]{2,1,0:T(8,128)(2,1)}, u32[]{:S(2)}, u32[]{:S(2)}) async-start(bf16[16,48,768]{2,1,0:T(8,128)(2,1)} %bitcast.96), calls=%async_computation.1 | async-start | bytes 2359296 | tf_op jit(solution)/shard_map/all_to_all | solution.py:85
  29.3 1.9 convolution_convert_fusion.1
  31.2 20.5 %all-to-all-done.1 = bf16[16,48,768]{2,1,0:T(8,128)(2,1)} async-done(((bf16[16,48,768]{2,1,0:T(8,128)(2,1)}), bf16[16,48,768]{2,1,0:T(8,128)(2,1)}, u32[]{:S(2)}, u32[]{:S(2)}) %all-to-all-start.1) | async-done | bytes 1179680 | tf_op jit(solution)/shard_map/all_to_all | solution.py:85
  51.7 3.7 %all-to-all-start = ((bf16[16,48,768]{2,1,0:T(8,128)(2,1)}), bf16[16,48,768]{2,1,0:T(8,128)(2,1)S(1)}, u32[]{:S(2)}, u32[]{:S(2)}) async-start(bf16[16,48,768]{2,1,0:T(8,128)(2,1)} %bitcast.95), calls=%async_computation | async-start | bytes 2359296 | tf_op jit(solution)/shard_map/all_to_all | solution.py:85
  55.4 2.8 %collective-permute-start.5 = (bf16[512,1536]{1,0:T(8,128)(2,1)S(1)}, bf16[512,1536]{1,0:T(8,128)(2,1)}, u32[]{:S(2)}, u32[]{:S(2)}) collective-permute-start(bf16[512,1536]{1,0:T(8,128)(2,1)S(1)} %bitcast.100), channel_id=1, source_target_pairs={{0,3},{3,0},{1,2},{2,1},{4,7},{7,4},{5,6},{6,5},{8,11},{11,8},{9,1... | collective-permute-start | bytes 4718600 | tf_op jit(solution)/shard_map/ppermute | solution.py:43
  58.4 23.9 %all-to-all-done = bf16[16,48,768]{2,1,0:T(8,128)(2,1)S(1)} async-done(((bf16[16,48,768]{2,1,0:T(8,128)(2,1)}), bf16[16,48,768]{2,1,0:T(8,128)(2,1)S(1)}, u32[]{:S(2)}, u32[]{:S(2)}) %all-to-all-start) | async-done | bytes 1179680 | tf_op jit(solution)/shard_map/all_to_all | solution.py:85
  84.5 2.1 add_convert_fusion.3
  86.6 4.8 %collective-permute-done.5 = bf16[512,1536]{1,0:T(8,128)(2,1)} collective-permute-done((bf16[512,1536]{1,0:T(8,128)(2,1)S(1)}, bf16[512,1536]{1,0:T(8,128)(2,1)}, u32[]{:S(2)}, u32[]{:S(2)}) %collective-permute-start.5) | collective-permute-done | bytes 1572896 | tf_op jit(solution)/shard_map/ppermute | solution.py:43
  91.4 2.3 %fusion.17 = f32[768,512]{0,1:T(8,128)S(1)} fusion(bf16[768,768]{1,0:T(8,128)(2,1)} %bitcast.19, bf16[512,1536]{1,0:T(8,128)(2,1)} %collective-permute-done.5), kind=kOutput, calls=%fused_computation.34 | convolution fusion | flops 603979776 | bytes 3538944 | tf_op jit(solution)/shard_map/dot_general | solution.py:16
  93.7 1.9 add_convert_fusion.2
  97.4 6.9 %all-to-all-start.2 = ((bf16[16,48,1024]{2,1,0:T(8,128)(2,1)}), bf16[16,48,1024]{2,1,0:T(8,128)(2,1)S(1)}, u32[]{:S(2)}, u32[]{:S(2)}) async-start(bf16[16,48,1024]{2,1,0:T(8,128)(2,1)} %bitcast.23), calls=%async_computation.2 | async-start | bytes 3145728 | tf_op jit(solution)/shard_map/all_to_all | solution.py:99
  104.3 2.4 %fusion.15 = f32[768,512]{0,1:T(8,128)S(1)} fusion(bf16[768,768]{1,0:T(8,128)(2,1)} %collective-permute-done.3, bf16[512,1536]{1,0:T(8,128)(2,1)} %collective-permute-done.5), kind=kOutput, calls=%fused_computation.32 | convolution fusion | flops 603979776 | bytes 3538944 | tf_op jit(solution)/shard_map/dot_general | solution.py:16
  106.7 2.1 fusion.21
  109.6 2.3 %add_convert_fusion = bf16[768,512]{0,1:T(8,128)(2,1)S(1)} fusion(f32[768,512]{0,1:T(8,128)S(1)} %fusion.15, bf16[768,768]{1,0:T(8,128)(2,1)} %collective-permute-done.1, bf16[512,1536]{1,0:T(8,128)(2,1)} %collective-permute-done.5), kind=kOutput, calls=%fused_computation.12 | convolution fusion | flops 604766208 | bytes 4325376 | tf_op jit(solution)/shard_map/dot_general | solution.py:16
  112.0 2.1 add_convert_fusion.1
  115.8 9.7 %all-to-all-done.2 = bf16[16,48,1024]{2,1,0:T(8,128)(2,1)S(1)} async-done(((bf16[16,48,1024]{2,1,0:T(8,128)(2,1)}), bf16[16,48,1024]{2,1,0:T(8,128)(2,1)S(1)}, u32[]{:S(2)}, u32[]{:S(2)}) %all-to-all-start.2) | async-done | bytes 1572896 | tf_op jit(solution)/shard_map/all_to_all | solution.py:99
  125.5 3.9 %all-to-all-start.3 = ((bf16[16,48,1024]{2,1,0:T(8,128)(2,1)}), bf16[16,48,1024]{2,1,0:T(8,128)(2,1)S(1)}, u32[]{:S(2)}, u32[]{:S(2)}) async-start(bf16[16,48,1024]{2,1,0:T(8,128)(2,1)} %bitcast.26), calls=%async_computation.3 | async-start | bytes 3145728 | tf_op jit(solution)/shard_map/all_to_all | solution.py:99
  131.3 19.0 %all-to-all-done.3 = bf16[16,48,1024]{2,1,0:T(8,128)(2,1)S(1)} async-done(((bf16[16,48,1024]{2,1,0:T(8,128)(2,1)}), bf16[16,48,1024]{2,1,0:T(8,128)(2,1)S(1)}, u32[]{:S(2)}, u32[]{:S(2)}) %all-to-all-start.3) | async-done | bytes 1572896 | tf_op jit(solution)/shard_map/all_to_all | solution.py:99
  152.1 4.9 %collective-permute-done.7 = bf16[64,1024]{1,0:T(8,128)(2,1)S(1)} collective-permute-done((bf16[64,1024]{1,0:T(8,128)(2,1)S(1)}, bf16[64,1024]{1,0:T(8,128)(2,1)S(1)}, u32[]{:S(2)}, u32[]{:S(2)}) %collective-permute-start.7) | collective-permute-done | bytes 131104 | tf_op jit(solution)/shard_map/ppermute | solution.py:110
  159.0 2.1 %fusion.5 = bf16[16,48,1024]{2,1,0:T(8,128)(2,1)S(1)} fusion(bf16[16,136,1024]{2,1,0:T(8,128)(2,1)} %bitcast.80, pred[16,2,48,64]{3,2,0,1:T(8,128)(4,1)S(1)} %fusion.13), kind=kOutput, calls=%fused_computation.7 | convolution fusion | flops 101449728 | bytes 3768320 | tf_op jit(solution)/shard_map/dot_general | solution.py:138
  161.2 2.1 %fusion.8 = bf16[16,48,1024]{2,1,0:T(8,128)(2,1)S(1)} fusion(bf16[16,136,1024]{2,1,0:T(8,128)(2,1)} %bitcast.81, pred[16,2,48,64]{3,2,0,1:T(8,128)(4,1)S(1)} %fusion.13), kind=kOutput, calls=%fused_computation.8 | convolution fusion | flops 101449728 | bytes 3768320 | tf_op jit(solution)/shard_map/dot_general | solution.py:138
  163.3 2.1 fusion.29
  165.4 2.2 %fusion.37 = f32[512,768]{1,0:T(8,128)S(1)} fusion(bf16[768,768]{1,0:T(8,128)(2,1)} %bitcast.19, bf16[768,1024]{1,0:T(8,128)(2,1)S(1)} %bitcast.87), kind=kOutput, calls=%fused_computation.54 | convolution fusion | flops 603979776 | bytes 3538944 | tf_op jit(solution)/shard_map/dot_general | solution.py:16
  168.5 2.1 add_convert_fusion.4
  170.6 2.8 %collective-permute-start.4 = (bf16[512,768]{1,0:T(8,128)(2,1)S(1)}, bf16[512,768]{1,0:T(8,128)(2,1)S(1)}, u32[]{:S(2)}, u32[]{:S(2)}) collective-permute-start(bf16[512,768]{1,0:T(8,128)(2,1)S(1)} %add_convert_fusion.4), channel_id=1, source_target_pairs={{0,3},{3,0},{1,2},{2,1},{4,7},{7,4},{5,6},{6,5},{8,11},{11,8},{9,1... | collective-permute-start | bytes 2359304 | tf_op jit(solution)/shard_map/ppermute | solution.py:150
  173.4 2.1 add_convert_fusion.5
  177.0 2.1 fusion.33
  179.1 2.1 fusion.35
  181.2 11.2 %collective-permute-done.4 = bf16[512,768]{1,0:T(8,128)(2,1)S(1)} collective-permute-done((bf16[512,768]{1,0:T(8,128)(2,1)S(1)}, bf16[512,768]{1,0:T(8,128)(2,1)S(1)}, u32[]{:S(2)}, u32[]{:S(2)}) %collective-permute-start.4) | collective-permute-done | bytes 786464 | tf_op jit(solution)/shard_map/ppermute | solution.py:150
  192.7 13.3 %collective-permute-done.2 = bf16[512,768]{1,0:T(8,128)(2,1)S(1)} collective-permute-done((bf16[512,768]{1,0:T(8,128)(2,1)S(1)}, bf16[512,768]{1,0:T(8,128)(2,1)S(1)}, u32[]{:S(2)}, u32[]{:S(2)}) %collective-permute-start.2) | collective-permute-done | bytes 786464 | tf_op jit(solution)/shard_map/ppermute | solution.py:150
  (64 shorter events, 26.3 us)
Async XLA Ops:
  7.2 150.7 %all-gather.3.cloned.1.call-start = ((), (), s32[]{:S(2)}) async-start(), calls=%async_computation.4 | async-start | bytes 4734976 | tf_op jit(solution)/shard_map/all_gather | solution.py:64
  8.9 5.5 %collective-permute-start = (bf16[72,1024]{1,0:T(8,128)(2,1)S(1)}, bf16[72,1024]{1,0:T(8,128)(2,1)S(1)}, u32[]{:S(2)}, u32[]{:S(2)}) collective-permute-start(bf16[72,1024]{1,0:T(8,128)(2,1)S(1)} %fusion.42), channel_id=1, source_target_pairs={{0,1},{1,0},{2,3},{3,2},{4,5},{5,4},{6,7},{7,6},{8,9},{9,8},{10,11... | collective-permute-start | bytes 442376 | tf_op jit(solution)/shard_map/ppermute | solution.py:56
  12.2 2.2 %copy-start.2 = (s32[1,64,8]{1,2,0:T(8,128)S(1)}, s32[1,64,8]{1,2,0:T(8,128)}, u32[]{:S(2)}) copy-start(s32[1,64,8]{1,2,0:T(8,128)} %param.8) | copy-start | bytes 6148
  20.9 30.7 %all-to-all-start.1 = ((bf16[16,48,768]{2,1,0:T(8,128)(2,1)}), bf16[16,48,768]{2,1,0:T(8,128)(2,1)}, u32[]{:S(2)}, u32[]{:S(2)}) async-start(bf16[16,48,768]{2,1,0:T(8,128)(2,1)} %bitcast.96), calls=%async_computation.1 | async-start | bytes 2359296 | tf_op jit(solution)/shard_map/all_to_all | solution.py:85
  31.2 24.2 %copy-start.3 = (bf16[1,512,1536]{2,1,0:T(8,128)(2,1)S(1)}, bf16[1,512,1536]{2,1,0:T(8,128)(2,1)}, u32[]{:S(2)}) copy-start(bf16[1,512,1536]{2,1,0:T(8,128)(2,1)} %param.5) | copy-start | bytes 4718596
  51.7 30.6 %all-to-all-start = ((bf16[16,48,768]{2,1,0:T(8,128)(2,1)}), bf16[16,48,768]{2,1,0:T(8,128)(2,1)S(1)}, u32[]{:S(2)}, u32[]{:S(2)}) async-start(bf16[16,48,768]{2,1,0:T(8,128)(2,1)} %bitcast.95), calls=%async_computation | async-start | bytes 2359296 | tf_op jit(solution)/shard_map/all_to_all | solution.py:85
  55.4 36.0 %collective-permute-start.5 = (bf16[512,1536]{1,0:T(8,128)(2,1)S(1)}, bf16[512,1536]{1,0:T(8,128)(2,1)}, u32[]{:S(2)}, u32[]{:S(2)}) collective-permute-start(bf16[512,1536]{1,0:T(8,128)(2,1)S(1)} %bitcast.100), channel_id=1, source_target_pairs={{0,3},{3,0},{1,2},{2,1},{4,7},{7,4},{5,6},{6,5},{8,11},{11,8},{9,1... | collective-permute-start | bytes 4718600 | tf_op jit(solution)/shard_map/ppermute | solution.py:43
  58.2 46.1 %collective-permute-start.3 = (bf16[768,768]{1,0:T(8,128)(2,1)}, bf16[768,768]{1,0:T(8,128)(2,1)}, u32[]{:S(2)}, u32[]{:S(2)}) collective-permute-start(bf16[768,768]{1,0:T(8,128)(2,1)} %bitcast.19), channel_id=1, source_target_pairs={{0,1},{1,0},{2,3},{3,2},{4,5},{5,4},{6,7},{7,6},{8,9},{9,8},{10,11... | collective-permute-start | bytes 3538952 | tf_op jit(solution)/shard_map/ppermute | solution.py:89
  82.3 11.4 %copy-start = (bf16[16,48,768]{2,1,0:T(8,128)(2,1)}, bf16[16,48,768]{2,1,0:T(8,128)(2,1)S(1)}, u32[]{:S(2)}) copy-start(bf16[16,48,768]{2,1,0:T(8,128)(2,1)S(1)} %all-to-all-done) | copy-start | bytes 3538948
  82.3 27.4 %collective-permute-start.1 = (bf16[768,768]{1,0:T(8,128)(2,1)S(1)}, bf16[768,768]{1,0:T(8,128)(2,1)}, u32[]{:S(2)}, u32[]{:S(2)}) collective-permute-start(bf16[768,768]{1,0:T(8,128)(2,1)S(1)} %bitcast.90), channel_id=1, source_target_pairs={{0,1},{1,0},{2,3},{3,2},{4,5},{5,4},{6,7},{7,6},{8,9},{9,8},{10,11... | collective-permute-start | bytes 3538952 | tf_op jit(solution)/shard_map/ppermute | solution.py:89
  97.4 28.1 %all-to-all-start.2 = ((bf16[16,48,1024]{2,1,0:T(8,128)(2,1)}), bf16[16,48,1024]{2,1,0:T(8,128)(2,1)S(1)}, u32[]{:S(2)}, u32[]{:S(2)}) async-start(bf16[16,48,1024]{2,1,0:T(8,128)(2,1)} %bitcast.23), calls=%async_computation.2 | async-start | bytes 3145728 | tf_op jit(solution)/shard_map/all_to_all | solution.py:99
  104.2 2.4 %copy-start.4 = (bf16[1,512,1536]{2,1,0:T(8,128)(2,1)S(1)}, bf16[1,512,1536]{2,1,0:T(8,128)(2,1)}, u32[]{:S(2)}) copy-start(bf16[1,512,1536]{2,1,0:T(8,128)(2,1)} %param.5) | copy-start | bytes 4718596
  125.5 24.8 %all-to-all-start.3 = ((bf16[16,48,1024]{2,1,0:T(8,128)(2,1)}), bf16[16,48,1024]{2,1,0:T(8,128)(2,1)S(1)}, u32[]{:S(2)}, u32[]{:S(2)}) async-start(bf16[16,48,1024]{2,1,0:T(8,128)(2,1)} %bitcast.26), calls=%async_computation.3 | async-start | bytes 3145728 | tf_op jit(solution)/shard_map/all_to_all | solution.py:99
  130.0 22.1 %collective-permute-start.6 = (bf16[64,1024]{1,0:T(8,128)(2,1)S(1)}, bf16[64,1024]{1,0:T(8,128)(2,1)S(1)}, u32[]{:S(2)}, u32[]{:S(2)}) collective-permute-start(bf16[64,1024]{1,0:T(8,128)(2,1)S(1)} %convolution_convert_fusion.3), channel_id=1, source_target_pairs={{64,0},{65,1},{66,2},{67,3},{68,4},{69,5},{70,6},{71,7},{72,8},{73... | collective-permute-start | bytes 393224 | tf_op jit(solution)/shard_map/ppermute | solution.py:109
  150.8 6.3 %collective-permute-start.7 = (bf16[64,1024]{1,0:T(8,128)(2,1)S(1)}, bf16[64,1024]{1,0:T(8,128)(2,1)S(1)}, u32[]{:S(2)}, u32[]{:S(2)}) collective-permute-start(bf16[64,1024]{1,0:T(8,128)(2,1)S(1)} %convolution_convert_fusion.2), channel_id=1, source_target_pairs={{64,1},{65,0},{66,3},{67,2},{68,5},{69,4},{70,7},{71,6},{72,9},{73... | collective-permute-start | bytes 393224 | tf_op jit(solution)/shard_map/ppermute | solution.py:110
  165.4 2.2 %copy-start.1 = (bf16[16,48,768]{2,1,0:T(8,128)(2,1)S(1)}, bf16[16,48,768]{2,1,0:T(8,128)(2,1)}, u32[]{:S(2)}) copy-start(bf16[16,48,768]{2,1,0:T(8,128)(2,1)} %copy-done) | copy-start | bytes 3538948
  170.6 21.8 %collective-permute-start.4 = (bf16[512,768]{1,0:T(8,128)(2,1)S(1)}, bf16[512,768]{1,0:T(8,128)(2,1)S(1)}, u32[]{:S(2)}, u32[]{:S(2)}) collective-permute-start(bf16[512,768]{1,0:T(8,128)(2,1)S(1)} %add_convert_fusion.4), channel_id=1, source_target_pairs={{0,3},{3,0},{1,2},{2,1},{4,7},{7,4},{5,6},{6,5},{8,11},{11,8},{9,1... | collective-permute-start | bytes 2359304 | tf_op jit(solution)/shard_map/ppermute | solution.py:150
  175.5 30.5 %collective-permute-start.2 = (bf16[512,768]{1,0:T(8,128)(2,1)S(1)}, bf16[512,768]{1,0:T(8,128)(2,1)S(1)}, u32[]{:S(2)}, u32[]{:S(2)}) collective-permute-start(bf16[512,768]{1,0:T(8,128)(2,1)S(1)} %add_convert_fusion.5), channel_id=1, source_target_pairs={{0,3},{3,0},{1,2},{2,1},{4,7},{7,4},{5,6},{6,5},{8,11},{11,8},{9,1... | collective-permute-start | bytes 2359304 | tf_op jit(solution)/shard_map/ppermute | solution.py:150
Sparse Core Ops, SparseCore 0:
  15.7 73.5 all-gather.2

commit v2 on v0

v2 whole, which is shorter than its diff:
```python
import jax
import jax.numpy as jnp
from jax import lax
from jax.sharding import Mesh, PartitionSpec as P

loss_scale_inverse = 0.0625
bf16 = jnp.bfloat16
f32 = jnp.float32
ZY = ("z", "y")
STEPS = (
    (("z", 1), ("z", 3), ("y", 1), ("y", 3)),
    (("y", 3), ("y", 1), ("z", 3), ("z", 1)),
)
TO_RIGHT = [(i, (i + 1) % 4) for i in range(4)]
TO_LEFT = [(i, (i + 3) % 4) for i in range(4)]


def dot(a, b, dims):
    return lax.dot_general(a, b, (dims, ((), ())), preferred_element_type=f32)


def gather_plane(block, steps):
    kept = block[None]
    for i, (axis, flip) in enumerate(steps):
        got = lax.ppermute(kept, axis, [(j, j ^ flip) for j in range(4)])
        if i == len(steps) - 1:
            return kept, got
        kept = jnp.concatenate([kept, got], axis=0)


def sources(steps):
    out = [0]
    for axis, flip in steps:
        mask = flip * 4 if axis == "z" else flip
        out = out + [o ^ mask for o in out]
    return out


def body(w_up, saved_rows, hidden_grad, expert_ids, route_weight):
    experts = lax.axis_size("z") * lax.axis_size("y")
    x = lax.axis_index("x")
    me = lax.axis_index("z") * lax.axis_size("y") + lax.axis_index("y")
    tokens = saved_rows.shape[1]
    width = saved_rows.shape[2]
    top = hidden_grad.shape[2]
    hidden = hidden_grad.shape[3]
    quarter = width // 4
    half = width // 2
    capacity = 3 * tokens * top // (2 * experts)
    slots = experts * capacity

    w = w_up[0]
    w_right = lax.ppermute(w, "x", TO_LEFT)
    w_left = lax.ppermute(w, "x", TO_RIGHT)
    mid = quarter // 2
    w_far_a = lax.ppermute(w_right[:mid], "x", TO_LEFT)
    w_far_b = lax.ppermute(w_left[mid:], "x", TO_RIGHT)

    rows = saved_rows[0]
    ids = expert_ids[0]
    ids_t = ids.T
    id_rows = jnp.pad(ids_t.astype(bf16), ((0, 0), (0, half - tokens)))
    first = gather_plane(jnp.concatenate([rows[:, :half], id_rows], axis=0), STEPS[0])
    second = gather_plane(rows[:, half:], STEPS[1])

    names = jnp.arange(experts, dtype=jnp.int32)
    row = lax.broadcasted_iota(jnp.int32, (tokens, tokens), 0)
    col = lax.broadcasted_iota(jnp.int32, (tokens, tokens), 1)
    earlier = (row < col).astype(bf16)
    chosen = jnp.any(ids_t[:, None, :] == names[None, :, None], axis=0)
    slot = dot(chosen.astype(bf16), earlier, ((1,), (0,))).astype(jnp.int32)
    target_t = jnp.where(chosen, slot, -1)
    target = jnp.sum(
        jnp.where(ids_t[:, None, :] == names[None, :, None], slot[None] + capacity * names[None, :, None], 0), axis=1
    )
    target = target.T.reshape(1, tokens * top)
    place = (lax.broadcasted_iota(jnp.int32, (slots, 1), 0) == target).astype(bf16)
    scaled = (route_weight[0][:, :, None] * hidden_grad[0].astype(f32)).astype(bf16)
    scaled = scaled.reshape(tokens * top, hidden)
    packed = dot(place, scaled, ((1,), (0,))).astype(bf16).reshape(experts, capacity, hidden)
    grads = lax.all_to_all(packed, ZY, 0, 0, tiled=True).reshape(slots, hidden)

    outs = [
        dot(grads, piece, ((1,), (1,))).astype(bf16)
        for piece in (w, w_right, w_far_a, w_far_b, w_left)
    ]
    routed = jnp.concatenate(outs, axis=1).reshape(experts, capacity, width)
    back = lax.all_to_all(routed, ZY, 0, 0, tiled=True).reshape(slots, width)
    place_tok = (
        (lax.broadcasted_iota(jnp.int32, (1, capacity, 1), 1) == target_t[:, None, :])
        .astype(bf16)
        .reshape(slots, tokens)
    )
    turned = dot(place_tok, back, ((0,), (0,))).astype(bf16)
    turned = lax.ppermute(turned, "section", [(1, 0)])
    upstream = lax.dynamic_slice_in_dim(
        jnp.concatenate([turned, turned], axis=1), (4 - x) * quarter, width, 1
    )

    ids_in = jnp.concatenate([a[:, tokens:, :tokens] for a in first], axis=0)
    named = jnp.any(ids_in == me.astype(bf16), axis=1)
    where = dot(named.astype(bf16), earlier, ((1,), (0,))).astype(jnp.int32)
    froms = [sources(steps) for steps in STEPS]
    base = (jnp.array(froms[0], jnp.int32) ^ me) * capacity
    goal = jnp.where(named, where + base[:, None], -1)
    goals = [goal, jnp.stack([goal[froms[0].index(s)] for s in froms[1]])]
    picked = []
    for goal_h, pieces in zip(goals, (first, second)):
        total = 0.0
        for i, piece in enumerate(pieces):
            n = piece.shape[0]
            line = goal_h[i * n : (i + 1) * n].reshape(1, n * tokens)
            pick = (lax.broadcasted_iota(jnp.int32, (slots, 1), 0) == line).astype(bf16)
            total = total + dot(pick, piece[:, :tokens].reshape(n * tokens, half), ((1,), (0,)))
        picked.append(total.astype(bf16))
    picked = jnp.concatenate(picked + picked, axis=1)
    turned_rows = lax.dynamic_slice_in_dim(picked, x * quarter, width, 1)

    def partial(lo, hi):
        return dot(turned_rows[:, lo:hi], grads, ((0,), (0,)))

    a, b = 2 * quarter, 2 * quarter + mid
    far_a = lax.ppermute(partial(a, b).astype(bf16), "x", TO_RIGHT)
    far_b = lax.ppermute(partial(b, b + mid).astype(bf16), "x", TO_LEFT)
    right_b = lax.ppermute(partial(quarter + mid, 2 * quarter).astype(bf16), "x", TO_RIGHT)
    left_a = lax.ppermute(partial(3 * quarter, 3 * quarter + mid).astype(bf16), "x", TO_LEFT)
    right_a = partial(quarter, quarter + mid) + far_a.astype(f32)
    left_b = partial(3 * quarter + mid, width) + far_b.astype(f32)
    right_a = lax.ppermute(right_a.astype(bf16), "x", TO_RIGHT)
    left_b = lax.ppermute(left_b.astype(bf16), "x", TO_LEFT)
    top_half = partial(0, mid) + left_a.astype(f32) + right_a.astype(f32)
    low_half = partial(mid, quarter) + left_b.astype(f32) + right_b.astype(f32)
    weight_grad = jnp.concatenate([top_half, low_half], axis=0) * loss_scale_inverse
    return weight_grad.astype(bf16)[None], upstream[None]


def solution(mesh):
    grid = Mesh(mesh.devices.reshape(2, 4, 4, 4), ("section", "z", "y", "x"))
    expert = ("z", "y", "x")
    return jax.shard_map(
        body,
        mesh=grid,
        in_specs=(
            P("section", expert, None),
            P("section", expert, None),
            P("section", expert, None, None),
            P("section", expert, None),
            P("section", expert, None),
        ),
        out_specs=(P("section", expert, None), P("section", expert, None)),
        check_vma=False,
    )
```

time: 247 us -> 216 us (0.87)
  blocking collectives: 124 us -> 0 us
  starting transfers between devices: 13.5 us -> 54.9 us
  waiting for transfers between devices: 59.8 us -> 87.5 us
  matrix products: 23.3 us -> 40.4 us
  other arithmetic: 1.83 us -> 15.2 us
  local copies, waits for them, and re-layouts: 23.9 us -> 14.5 us
    all_to_all x1 -> x0, blocking collectives: 124 us -> none  [body(): lax.all_to_all(grad_out.reshape(owners, capacity, hidden), 'expert', spli...]
    ppermute x1 -> x19, waiting for transfers between devices: 0.01 us -> 87.5 us  [the longest x8 50.1 us: gather_plane(): got = lax.ppermute(kept, axis, [(j, j ^ flip) for j in range(4)])]
    all_to_all x2, waiting for transfers between devices: 59.8 us -> 0.01 us  [the longest x1 0.01 us: body(): back = lax.all_to_all(routed, ZY, 0, 0, tiled=True).reshape(slots, width)]
    ppermute x1 -> x19, starting transfers between devices: 1.29 us -> 40.1 us  [the longest x8 24.7 us: gather_plane(): got = lax.ppermute(kept, axis, [(j, j ^ flip) for j in range(4)])]
    dot_general x5 -> x21, matrix products: 23.3 us -> 40.4 us  [dot(): return lax.dot_general(a, b, (dims, ((), ())), preferred_element_type=f32)]
    concatenate x0 -> x9, other arithmetic: none -> 11.3 us  [the longest x6 6.61 us: gather_plane(): kept = jnp.concatenate([kept, got], axis=0)]
    transpose x2 -> x1, local copies, waits for them, and re-layouts: 8.97 us -> 0.08 us  [body(): target = target.T.reshape(1, tokens * top)]
    slice x1 -> x8, local copies, waits for them, and re-layouts: 0.22 us -> 7.37 us  [the longest x2 2.39 us: body(): piece[:, :tokens].reshape(n * tokens, half)]
  transfers between devices with their start and end apart: 3 -> 21, of which waited for: 2 -> 11; matrix products, arithmetic and copies ran while one was open for 12% -> 30% of each run, Pallas kernels for 0% -> 0%
where the time goes in v2:
time: 216 us; the launch traced here: 213 us
  waiting for transfers between devices  87.5 us (41%)
  starting transfers between devices  54.9 us (25%)
  matrix products  40.4 us (19%)
  other arithmetic  15.2 us (7%)
  local copies, waits for them, and re-layouts  14.5 us (7%)
    ppermute x8, waiting for transfers between devices, gather_plane(): got = lax.ppermute(kept, axis, [(j, j ^ flip) for j in range(4)])  50.1 us
    dot_general x21, matrix products, dot(): return lax.dot_general(a, b, (dims, ((), ())), preferred_element_type=f32)  40.4 us
    ppermute x8, starting transfers between devices, gather_plane(): got = lax.ppermute(kept, axis, [(j, j ^ flip) for j in range(4)])  24.7 us
    ppermute x1, waiting for transfers between devices, body(): far_b = lax.ppermute(partial(b, b + mid).astype(bf16), 'x', TO_LEFT)  12.6 us
    ppermute x1, waiting for transfers between devices, body(): lax.ppermute(partial(3 * quarter, 3 * quarter + mid).astype(bf16), 'x', T...  12 us
    ppermute x1, waiting for transfers between devices, body(): left_b = lax.ppermute(left_b.astype(bf16), 'x', TO_LEFT)  10.1 us
    all_to_all x1, starting transfers between devices, body(): back = lax.all_to_all(routed, ZY, 0, 0, tiled=True).reshape(slots, width)  8.11 us
    all_to_all x1, starting transfers between devices, body(): grads = lax.all_to_all(packed, ZY, 0, 0, tiled=True).reshape(slots, hidden)  6.68 us
  transfers between devices with their start and end apart: 21, of which 11 were waited for; matrix products, arithmetic and copies ran while one was open for 30% of the time, Pallas kernels for 0%

profile of v2, /device:TPU:0, one launch (start us, length us, event | category | flops | bytes accessed | tf_op | source)
XLA Modules:
  0.0 213.5 jit_solution(6185865245105846673)
XLA Ops:
  5.1 2.8 %collective-permute-start.14 = (bf16[512,1536]{1,0:T(8,128)(2,1)}, bf16[512,1536]{1,0:T(8,128)(2,1)}, u32[]{:S(2)}, u32[]{:S(2)}) collective-permute-start(bf16[512,1536]{1,0:T(8,128)(2,1)} %bitcast.81), channel_id=1, source_target_pairs={{0,3},{1,0},{2,1},{3,2},{4,7},{5,4},{6,5},{7,6},{8,11},{9,8},{10,9... | collective-permute-start | bytes 4718600 | tf_op jit(solution)/shard_map/ppermute | solution.py:53
  9.0 3.9 %collective-permute-start.1 = (bf16[2,72,1024]{2,1,0:T(8,128)(2,1)S(1)}, bf16[2,72,1024]{2,1,0:T(8,128)(2,1)S(1)}, u32[]{:S(2)}, u32[]{:S(2)}) collective-permute-start(bf16[2,72,1024]{2,1,0:T(8,128)(2,1)S(1)} %pad_maximum_fusion.4), channel_id=1, source_target_pairs={{0,48},{16,32},{32,16},{48,0},{1,49},{17,33},{33,17},{49,1},{2,50}... | collective-permute-start | bytes 884744 | tf_op jit(solution)/shard_map/ppermute | solution.py:25
  13.0 6.2 %collective-permute-done.1 = bf16[2,72,1024]{2,1,0:T(8,128)(2,1)S(1)} collective-permute-done((bf16[2,72,1024]{2,1,0:T(8,128)(2,1)S(1)}, bf16[2,72,1024]{2,1,0:T(8,128)(2,1)S(1)}, u32[]{:S(2)}, u32[]{:S(2)}) %collective-permute-start.1) | collective-permute-done | bytes 294944 | tf_op jit(solution)/shard_map/ppermute | solution.py:25
  21.3 4.3 %convolution_convert_fusion = bf16[768,1536]{1,0:T(8,128)(2,1)} fusion(bf16[1,64,8,1536]{3,2,1,0:T(8,128)(2,1)} %param.8, f32[512]{0:T(512)S(1)} %mul.48, s32[512]{0:T(512)S(1)} %eq.136), kind=kOutput, calls=%fused_computation.4 | convolution fusion | flops 1211891712 | bytes 3936256 | tf_op jit(solution)/shard_map/dot_general | solution.py:19
  25.6 6.7 %all-to-all-start = ((bf16[16,48,1536]{2,1,0:T(8,128)(2,1)}), bf16[16,48,1536]{2,1,0:T(8,128)(2,1)S(1)}, u32[]{:S(2)}, u32[]{:S(2)}) async-start(bf16[16,48,1536]{2,1,0:T(8,128)(2,1)} %bitcast.74), calls=%async_computation | async-start | bytes 4718592 | tf_op jit(solution)/shard_map/all_to_all | solution.py:81
  32.3 3.2 %collective-permute-start.4 = (bf16[1,64,1024]{2,1,0:T(8,128)(2,1)}, bf16[1,64,1024]{2,1,0:T(8,128)(2,1)S(1)}, u32[]{:S(2)}, u32[]{:S(2)}) collective-permute-start(bf16[1,64,1024]{2,1,0:T(8,128)(2,1)} %get-tuple-element.2), channel_id=1, source_target_pairs={{0,12},{4,8},{8,4},{12,0},{1,13},{5,9},{9,5},{13,1},{2,14},{6,10},... | collective-permute-start | bytes 393224 | tf_op jit(solution)/shard_map/ppermute | solution.py:25
  38.9 23.2 %collective-permute-done.4 = bf16[1,64,1024]{2,1,0:T(8,128)(2,1)S(1)} collective-permute-done((bf16[1,64,1024]{2,1,0:T(8,128)(2,1)}, bf16[1,64,1024]{2,1,0:T(8,128)(2,1)S(1)}, u32[]{:S(2)}, u32[]{:S(2)}) %collective-permute-start.4) | collective-permute-done | bytes 131104 | tf_op jit(solution)/shard_map/ppermute | solution.py:25
  63.1 3.2 %collective-permute-start.5 = (bf16[2,64,1024]{2,1,0:T(8,128)(2,1)S(1)}, bf16[2,64,1024]{2,1,0:T(8,128)(2,1)S(1)}, u32[]{:S(2)}, u32[]{:S(2)}) collective-permute-start(bf16[2,64,1024]{2,1,0:T(8,128)(2,1)S(1)} %pad_maximum_fusion.5), channel_id=1, source_target_pairs={{0,4},{4,0},{8,12},{12,8},{1,5},{5,1},{9,13},{13,9},{2,6},{6,2},{1... | collective-permute-start | bytes 786440 | tf_op jit(solution)/shard_map/ppermute | solution.py:25
  66.2 4.4 %collective-permute-done.5 = bf16[2,64,1024]{2,1,0:T(8,128)(2,1)S(1)} collective-permute-done((bf16[2,64,1024]{2,1,0:T(8,128)(2,1)S(1)}, bf16[2,64,1024]{2,1,0:T(8,128)(2,1)S(1)}, u32[]{:S(2)}, u32[]{:S(2)}) %collective-permute-start.5) | collective-permute-done | bytes 262176 | tf_op jit(solution)/shard_map/ppermute | solution.py:25
  72.4 4.7 %collective-permute-start.6 = (bf16[4,64,1024]{2,1,0:T(8,128)(2,1)}, bf16[4,64,1024]{2,1,0:T(8,128)(2,1)}, u32[]{:S(2)}, u32[]{:S(2)}) collective-permute-start(bf16[4,64,1024]{2,1,0:T(8,128)(2,1)} %pad_maximum_fusion.3), channel_id=1, source_target_pairs={{0,48},{16,32},{32,16},{48,0},{1,49},{17,33},{33,17},{49,1},{2,50}... | collective-permute-start | bytes 1572872 | tf_op jit(solution)/shard_map/ppermute | solution.py:25
  77.1 7.5 %collective-permute-done.6 = bf16[4,64,1024]{2,1,0:T(8,128)(2,1)} collective-permute-done((bf16[4,64,1024]{2,1,0:T(8,128)(2,1)}, bf16[4,64,1024]{2,1,0:T(8,128)(2,1)}, u32[]{:S(2)}, u32[]{:S(2)}) %collective-permute-start.6) | collective-permute-done | bytes 524320 | tf_op jit(solution)/shard_map/ppermute | solution.py:25
  84.6 2.4 %pad_maximum_fusion.1 = bf16[8,64,1024]{2,1,0:T(8,128)(2,1)} fusion(bf16[4,64,1024]{2,1,0:T(8,128)(2,1)} %collective-permute-done.6, bf16[2,64,1024]{2,1,0:T(8,128)(2,1)} %copy-done.9, bf16[1,64,1024]{2,1,0:T(8,128)(2,1)} %copy-done.7, bf16[1,64,1024]{2,1,0:T(8,128)(2,1)} %get-tuple-element.2), kind=kLoop, calls=%fused_computation.48 | loop fusion | flops 1572864 | bytes 2097152 | tf_op jit(solution)/shard_map/concatenate | solution.py:28
  86.9 4.0 %collective-permute-start.7 = (bf16[8,64,1024]{2,1,0:T(8,128)(2,1)}, bf16[8,64,1024]{2,1,0:T(8,128)(2,1)}, u32[]{:S(2)}, u32[]{:S(2)}) collective-permute-start(bf16[8,64,1024]{2,1,0:T(8,128)(2,1)} %pad_maximum_fusion.1), channel_id=1, source_target_pairs={{0,16},{16,0},{32,48},{48,32},{1,17},{17,1},{33,49},{49,33},{2,18}... | collective-permute-start | bytes 3145736 | tf_op jit(solution)/shard_map/ppermute | solution.py:25
  94.1 2.4 %collective-permute-start.15 = (bf16[256,1536]{1,0:T(8,128)(2,1)}, bf16[256,1536]{1,0:T(8,128)(2,1)}, u32[]{:S(2)}, u32[]{:S(2)}) collective-permute-start(bf16[256,1536]{1,0:T(8,128)(2,1)} %slice.172), channel_id=1, source_target_pairs={{0,3},{1,0},{2,1},{3,2},{4,7},{5,4},{6,5},{7,6},{8,11},{9,8},{10,9... | collective-permute-start | bytes 2359304 | tf_op jit(solution)/shard_map/ppermute | solution.py:56
  99.8 3.7 %fusion.13 = bf16[768,2048]{0,1:T(8,128)(2,1)} fusion(bf16[768,1536]{1,0:T(8,128)(2,1)S(1)} %bitcast.60, bf16[1,512,1536]{2,1,0:T(8,128)(2,1)} %param.6), kind=kOutput, calls=%fused_computation.38 | convolution fusion | flops 1208352768 | bytes 4718592 | tf_op jit(solution)/shard_map/dot_general | solution.py:19
  103.5 8.5 %collective-permute-done.7 = bf16[8,64,1024]{2,1,0:T(8,128)(2,1)} collective-permute-done((bf16[8,64,1024]{2,1,0:T(8,128)(2,1)}, bf16[8,64,1024]{2,1,0:T(8,128)(2,1)}, u32[]{:S(2)}, u32[]{:S(2)}) %collective-permute-start.7) | collective-permute-done | bytes 1048608 | tf_op jit(solution)/shard_map/ppermute | solution.py:25
  112.0 2.2 %fusion.10 = f32[768,1024]{1,0:T(8,128)S(1)} fusion(bf16[512,1024]{1,0:T(8,128)(2,1)} %bitcast.8, s32[512]{0:T(512)S(1)} %eq.129), kind=kOutput, calls=%fused_computation.32 | convolution fusion | flops 805699584 | bytes 4196352 | tf_op jit(solution)/shard_map/dot_general | solution.py:19
  116.6 2.3 %add_convert_fusion = bf16[768,1024]{1,0:T(8,128)(2,1)S(1)} fusion(f32[768,1024]{1,0:T(8,128)S(1)} %fusion.10, bf16[512,1024]{1,0:T(8,128)(2,1)} %bitcast.7, s32[512]{0:T(512)S(1)} %eq.125), kind=kOutput, calls=%fused_computation.12 | convolution fusion | flops 807272448 | bytes 5769216 | tf_op jit(solution)/shard_map/dot_general | solution.py:19
  120.0 3.0 %fusion.2 = bf16[768,2048]{1,0:T(8,128)(2,1)S(1)} fusion(s32[]{:T(128)S(6)} %select_n.18, bf16[768,1024]{1,0:T(8,128)(2,1)S(1)} %add_convert_fusion.1, bf16[768,1024]{1,0:T(8,128)(2,1)S(1)} %add_convert_fusion), kind=kLoop, calls=%fused_computation.7 | loop fusion | flops 12582912 | bytes 6291460 | tf_op jit(solution)/shard_map/concatenate | solution.py:116
  127.2 3.7 %fusion.12 = bf16[768,2048]{0,1:T(8,128)(2,1)} fusion(bf16[768,2048]{0,1:T(8,128)(2,1)} %fusion.13, bf16[768,1536]{1,0:T(8,128)(2,1)S(1)} %bitcast.63, bf16[512,1536]{1,0:T(8,128)(2,1)} %collective-permute-done.14), kind=kOutput, calls=%fused_computation.36 | convolution fusion | flops 1208352768 | bytes 4718592 | tf_op jit(solution)/shard_map/dot_general | solution.py:19
  131.0 2.7 %fusion.14 = bf16[768,2048]{0,1:T(8,128)(2,1)} fusion(bf16[768,2048]{0,1:T(8,128)(2,1)} %fusion.12, bf16[768,1536]{1,0:T(8,128)(2,1)S(1)} %bitcast.64, bf16[256,1536]{1,0:T(8,128)(2,1)} %collective-permute-done.15), kind=kOutput, calls=%fused_computation.41 | convolution fusion | flops 604176384 | bytes 3538944 | tf_op jit(solution)/shard_map/dot_general | solution.py:19
  133.7 2.7 %fusion.15 = bf16[768,2048]{0,1:T(8,128)(2,1)} fusion(bf16[768,2048]{0,1:T(8,128)(2,1)} %fusion.14, bf16[768,1536]{1,0:T(8,128)(2,1)S(1)} %bitcast.65, bf16[256,1536]{1,0:T(8,128)(2,1)} %collective-permute-done.17), kind=kOutput, calls=%fused_computation.42 | convolution fusion | flops 604176384 | bytes 3538944 | tf_op jit(solution)/shard_map/dot_general | solution.py:19
  136.4 3.7 %fusion.11 = bf16[768,2048]{0,1:T(8,128)(2,1)} fusion(bf16[768,2048]{0,1:T(8,128)(2,1)} %fusion.15, bf16[768,1536]{1,0:T(8,128)(2,1)S(1)} %bitcast.66, bf16[512,1536]{1,0:T(8,128)(2,1)} %collective-permute-done.16), kind=kOutput, calls=%fused_computation.34 | convolution fusion | flops 1208352768 | bytes 4718592 | tf_op jit(solution)/shard_map/dot_general | solution.py:19
  140.1 4.7 %copy.13 = bf16[768,2048]{1,0:T(8,128)(2,1)} copy(bf16[768,2048]{0,1:T(8,128)(2,1)} %fusion.11) | data formatting | bytes 6291456 | tf_op jit(solution)/shard_map/concatenate | solution.py:87
  144.8 8.1 %all-to-all-start.1 = ((bf16[16,48,2048]{2,1,0:T(8,128)(2,1)}), bf16[16,48,2048]{2,1,0:T(8,128)(2,1)}, u32[]{:S(2)}, u32[]{:S(2)}) async-start(bf16[16,48,2048]{2,1,0:T(8,128)(2,1)} %bitcast.73), calls=%async_computation.1 | async-start | bytes 6291456 | tf_op jit(solution)/shard_map/all_to_all | solution.py:88
  154.9 2.2 %collective-permute-start.11 = (bf16[256,1536]{1,0:T(8,128)(2,1)S(1)}, bf16[256,1536]{1,0:T(8,128)(2,1)S(1)}, u32[]{:S(2)}, u32[]{:S(2)}) collective-permute-start(bf16[256,1536]{1,0:T(8,128)(2,1)S(1)} %convolution_convert_fusion.2), channel_id=1, source_target_pairs={{0,3},{1,0},{2,1},{3,2},{4,7},{5,4},{6,5},{7,6},{8,11},{9,8},{10,9... | collective-permute-start | bytes 2359304 | tf_op jit(solution)/shard_map/ppermute | solution.py:124
  163.0 12.6 %collective-permute-done.11 = bf16[256,1536]{1,0:T(8,128)(2,1)S(1)} collective-permute-done((bf16[256,1536]{1,0:T(8,128)(2,1)S(1)}, bf16[256,1536]{1,0:T(8,128)(2,1)S(1)}, u32[]{:S(2)}, u32[]{:S(2)}) %collective-permute-start.11) | collective-permute-done | bytes 786464 | tf_op jit(solution)/shard_map/ppermute | solution.py:124
  176.5 3.2 %collective-permute-start.12 = (bf16[256,1536]{1,0:T(8,128)(2,1)S(1)}, bf16[256,1536]{1,0:T(8,128)(2,1)S(1)}, u32[]{:S(2)}, u32[]{:S(2)}) collective-permute-start(bf16[256,1536]{1,0:T(8,128)(2,1)S(1)} %add_convert_fusion.2), channel_id=1, source_target_pairs={{0,3},{1,0},{2,1},{3,2},{4,7},{5,4},{6,5},{7,6},{8,11},{9,8},{10,9... | collective-permute-start | bytes 2359304 | tf_op jit(solution)/shard_map/ppermute | solution.py:130
  180.5 12.0 %collective-permute-done.8 = bf16[256,1536]{1,0:T(8,128)(2,1)S(1)} collective-permute-done((bf16[256,1536]{1,0:T(8,128)(2,1)S(1)}, bf16[256,1536]{1,0:T(8,128)(2,1)S(1)}, u32[]{:S(2)}, u32[]{:S(2)}) %collective-permute-start.8) | collective-permute-done | bytes 786464 | tf_op jit(solution)/shard_map/ppermute | solution.py:126
  192.8 2.2 %collective-permute-done.13 = bf16[256,1536]{1,0:T(8,128)(2,1)S(1)} collective-permute-done((bf16[256,1536]{1,0:T(8,128)(2,1)S(1)}, bf16[256,1536]{1,0:T(8,128)(2,1)S(1)}, u32[]{:S(2)}, u32[]{:S(2)}) %collective-permute-start.13) | collective-permute-done | bytes 786464 | tf_op jit(solution)/shard_map/ppermute | solution.py:125
  195.0 10.1 %collective-permute-done.12 = bf16[256,1536]{1,0:T(8,128)(2,1)S(1)} collective-permute-done((bf16[256,1536]{1,0:T(8,128)(2,1)S(1)}, bf16[256,1536]{1,0:T(8,128)(2,1)S(1)}, u32[]{:S(2)}, u32[]{:S(2)}) %collective-permute-start.12) | collective-permute-done | bytes 786464 | tf_op jit(solution)/shard_map/ppermute | solution.py:130
  206.5 2.7 %fusion.5 = bf16[64,2048]{1,0:T(8,128)(2,1)S(1)} fusion(bf16[16,48,2048]{2,1,0:T(8,128)(2,1)} %all-to-all-done.1, s32[16,64]{1,0:T(8,128)S(1)} %get-tuple-element.4), kind=kOutput, calls=%fused_computation.19 | convolution fusion | flops 201506816 | bytes 3411968 | tf_op jit(solution)/shard_map/dot_general | solution.py:19
  (95 shorter events, 43.5 us)
Async XLA Ops:
  0.6 20.3 %copy-start.10 = (s32[1,64,8]{1,2,0:T(8,128)S(1)}, s32[1,64,8]{1,2,0:T(8,128)}, u32[]{:S(2)}) copy-start(s32[1,64,8]{1,2,0:T(8,128)} %param.9) | copy-start | bytes 6148
  0.6 20.4 %copy-start.11 = (f32[1,64,8]{1,2,0:T(8,128)S(1)}, f32[1,64,8]{1,2,0:T(8,128)}, u32[]{:S(2)}) copy-start(f32[1,64,8]{1,2,0:T(8,128)} %param.10) | copy-start | bytes 6148
  3.0 22.6 %copy-start.4 = (bf16[1,72,1024]{2,1,0:T(8,128)(2,1)}, bf16[1,72,1024]{2,1,0:T(8,128)(2,1)S(1)}, u32[]{:S(2)}) copy-start(bf16[1,72,1024]{2,1,0:T(8,128)(2,1)S(1)} %fusion.44) | copy-start | bytes 442372
  3.0 5.9 %collective-permute-start = (bf16[1,72,1024]{2,1,0:T(8,128)(2,1)S(1)}, bf16[1,72,1024]{2,1,0:T(8,128)(2,1)S(1)}, u32[]{:S(2)}, u32[]{:S(2)}) collective-permute-start(bf16[1,72,1024]{2,1,0:T(8,128)(2,1)S(1)} %fusion.44), channel_id=1, source_target_pairs={{0,16},{16,0},{32,48},{48,32},{1,17},{17,1},{33,49},{49,33},{2,18}... | collective-permute-start | bytes 442376 | tf_op jit(solution)/shard_map/ppermute | solution.py:25
  5.1 86.9 %collective-permute-start.14 = (bf16[512,1536]{1,0:T(8,128)(2,1)}, bf16[512,1536]{1,0:T(8,128)(2,1)}, u32[]{:S(2)}, u32[]{:S(2)}) collective-permute-start(bf16[512,1536]{1,0:T(8,128)(2,1)} %bitcast.81), channel_id=1, source_target_pairs={{0,3},{1,0},{2,1},{3,2},{4,7},{5,4},{6,5},{7,6},{8,11},{9,8},{10,9... | collective-permute-start | bytes 4718600 | tf_op jit(solution)/shard_map/ppermute | solution.py:53
  7.9 88.6 %collective-permute-start.16 = (bf16[512,1536]{1,0:T(8,128)(2,1)}, bf16[512,1536]{1,0:T(8,128)(2,1)}, u32[]{:S(2)}, u32[]{:S(2)}) collective-permute-start(bf16[512,1536]{1,0:T(8,128)(2,1)} %bitcast.82), channel_id=1, source_target_pairs={{0,1},{1,2},{2,3},{3,0},{4,5},{5,6},{6,7},{7,4},{8,9},{9,10},{10,1... | collective-permute-start | bytes 4718600 | tf_op jit(solution)/shard_map/ppermute | solution.py:54
  8.9 16.7 %copy-start.5 = (bf16[1,72,1024]{2,1,0:T(8,128)(2,1)}, bf16[1,72,1024]{2,1,0:T(8,128)(2,1)S(1)}, u32[]{:S(2)}) copy-start(bf16[1,72,1024]{2,1,0:T(8,128)(2,1)S(1)} %collective-permute-done) | copy-start | bytes 442372
  9.0 10.2 %collective-permute-start.1 = (bf16[2,72,1024]{2,1,0:T(8,128)(2,1)S(1)}, bf16[2,72,1024]{2,1,0:T(8,128)(2,1)S(1)}, u32[]{:S(2)}, u32[]{:S(2)}) collective-permute-start(bf16[2,72,1024]{2,1,0:T(8,128)(2,1)S(1)} %pad_maximum_fusion.4), channel_id=1, source_target_pairs={{0,48},{16,32},{32,16},{48,0},{1,49},{17,33},{33,17},{49,1},{2,50}... | collective-permute-start | bytes 884744 | tf_op jit(solution)/shard_map/ppermute | solution.py:25
  19.2 6.5 %copy-start.6 = (bf16[2,72,1024]{2,1,0:T(8,128)(2,1)}, bf16[2,72,1024]{2,1,0:T(8,128)(2,1)S(1)}, u32[]{:S(2)}) copy-start(bf16[2,72,1024]{2,1,0:T(8,128)(2,1)S(1)} %collective-permute-done.1) | copy-start | bytes 884740
  19.2 16.3 %collective-permute-start.2 = (bf16[4,72,1024]{2,1,0:T(8,128)(2,1)S(1)}, bf16[4,72,1024]{2,1,0:T(8,128)(2,1)}, u32[]{:S(2)}, u32[]{:S(2)}) collective-permute-start(bf16[4,72,1024]{2,1,0:T(8,128)(2,1)S(1)} %pad_maximum_fusion.2), channel_id=1, source_target_pairs={{0,4},{4,0},{8,12},{12,8},{1,5},{5,1},{9,13},{13,9},{2,6},{6,2},{1... | collective-permute-start | bytes 1769480 | tf_op jit(solution)/shard_map/ppermute | solution.py:25
  25.6 74.2 %all-to-all-start = ((bf16[16,48,1536]{2,1,0:T(8,128)(2,1)}), bf16[16,48,1536]{2,1,0:T(8,128)(2,1)S(1)}, u32[]{:S(2)}, u32[]{:S(2)}) async-start(bf16[16,48,1536]{2,1,0:T(8,128)(2,1)} %bitcast.74), calls=%async_computation | async-start | bytes 4718592 | tf_op jit(solution)/shard_map/all_to_all | solution.py:81
  32.3 44.8 %copy-start.12 = (s32[16]{0:T(128)S(1)}, s32[16]{0:T(128)}, u32[]{:S(2)}) copy-start(s32[16]{0:T(128)} %constant.32.clone) | copy-start | bytes 196
  32.3 29.8 %collective-permute-start.4 = (bf16[1,64,1024]{2,1,0:T(8,128)(2,1)}, bf16[1,64,1024]{2,1,0:T(8,128)(2,1)S(1)}, u32[]{:S(2)}, u32[]{:S(2)}) collective-permute-start(bf16[1,64,1024]{2,1,0:T(8,128)(2,1)} %get-tuple-element.2), channel_id=1, source_target_pairs={{0,12},{4,8},{8,4},{12,0},{1,13},{5,9},{9,5},{13,1},{2,14},{6,10},... | collective-permute-start | bytes 393224 | tf_op jit(solution)/shard_map/ppermute | solution.py:25
  36.9 61.7 %collective-permute-start.3 = (bf16[8,72,1024]{2,1,0:T(8,128)(2,1)S(1)}, bf16[8,72,1024]{2,1,0:T(8,128)(2,1)}, u32[]{:S(2)}, u32[]{:S(2)}) collective-permute-start(bf16[8,72,1024]{2,1,0:T(8,128)(2,1)S(1)} %pad_maximum_fusion), channel_id=1, source_target_pairs={{0,12},{4,8},{8,4},{12,0},{1,13},{5,9},{9,5},{13,1},{2,14},{6,10},... | collective-permute-start | bytes 3538952 | tf_op jit(solution)/shard_map/ppermute | solution.py:25
  62.1 8.5 %copy-start.7 = (bf16[1,64,1024]{2,1,0:T(8,128)(2,1)}, bf16[1,64,1024]{2,1,0:T(8,128)(2,1)S(1)}, u32[]{:S(2)}) copy-start(bf16[1,64,1024]{2,1,0:T(8,128)(2,1)S(1)} %collective-permute-done.4) | copy-start | bytes 393220
  63.1 7.5 %collective-permute-start.5 = (bf16[2,64,1024]{2,1,0:T(8,128)(2,1)S(1)}, bf16[2,64,1024]{2,1,0:T(8,128)(2,1)S(1)}, u32[]{:S(2)}, u32[]{:S(2)}) collective-permute-start(bf16[2,64,1024]{2,1,0:T(8,128)(2,1)S(1)} %pad_maximum_fusion.5), channel_id=1, source_target_pairs={{0,4},{4,0},{8,12},{12,8},{1,5},{5,1},{9,13},{13,9},{2,6},{6,2},{1... | collective-permute-start | bytes 786440 | tf_op jit(solution)/shard_map/ppermute | solution.py:25
  72.4 12.1 %collective-permute-start.6 = (bf16[4,64,1024]{2,1,0:T(8,128)(2,1)}, bf16[4,64,1024]{2,1,0:T(8,128)(2,1)}, u32[]{:S(2)}, u32[]{:S(2)}) collective-permute-start(bf16[4,64,1024]{2,1,0:T(8,128)(2,1)} %pad_maximum_fusion.3), channel_id=1, source_target_pairs={{0,48},{16,32},{32,16},{48,0},{1,49},{17,33},{33,17},{49,1},{2,50}... | collective-permute-start | bytes 1572872 | tf_op jit(solution)/shard_map/ppermute | solution.py:25
  86.9 25.1 %collective-permute-start.7 = (bf16[8,64,1024]{2,1,0:T(8,128)(2,1)}, bf16[8,64,1024]{2,1,0:T(8,128)(2,1)}, u32[]{:S(2)}, u32[]{:S(2)}) collective-permute-start(bf16[8,64,1024]{2,1,0:T(8,128)(2,1)} %pad_maximum_fusion.1), channel_id=1, source_target_pairs={{0,16},{16,0},{32,48},{48,32},{1,17},{17,1},{33,49},{49,33},{2,18}... | collective-permute-start | bytes 3145736 | tf_op jit(solution)/shard_map/ppermute | solution.py:25
  94.1 36.9 %collective-permute-start.15 = (bf16[256,1536]{1,0:T(8,128)(2,1)}, bf16[256,1536]{1,0:T(8,128)(2,1)}, u32[]{:S(2)}, u32[]{:S(2)}) collective-permute-start(bf16[256,1536]{1,0:T(8,128)(2,1)} %slice.172), channel_id=1, source_target_pairs={{0,3},{1,0},{2,1},{3,2},{4,7},{5,4},{6,5},{7,6},{8,11},{9,8},{10,9... | collective-permute-start | bytes 2359304 | tf_op jit(solution)/shard_map/ppermute | solution.py:56
  98.5 35.1 %collective-permute-start.17 = (bf16[256,1536]{1,0:T(8,128)(2,1)}, bf16[256,1536]{1,0:T(8,128)(2,1)}, u32[]{:S(2)}, u32[]{:S(2)}) collective-permute-start(bf16[256,1536]{1,0:T(8,128)(2,1)} %slice.173), channel_id=1, source_target_pairs={{0,1},{1,2},{2,3},{3,0},{4,5},{5,6},{6,7},{7,4},{8,9},{9,10},{10,1... | collective-permute-start | bytes 2359304 | tf_op jit(solution)/shard_map/ppermute | solution.py:57
  122.9 3.0 %copy-start = (bf16[768,2048]{1,0:T(8,128)(2,1)}, bf16[768,2048]{1,0:T(8,128)(2,1)S(1)}, u32[]{:S(2)}) copy-start(bf16[768,2048]{1,0:T(8,128)(2,1)S(1)} %fusion.2) | copy-start | bytes 9437188
  125.9 33.3 %collective-permute-start.9 = (bf16[256,1536]{1,0:T(8,128)(2,1)S(1)}, bf16[256,1536]{1,0:T(8,128)(2,1)}, u32[]{:S(2)}, u32[]{:S(2)}) collective-permute-start(bf16[256,1536]{1,0:T(8,128)(2,1)S(1)} %convolution_convert_fusion.3), channel_id=1, source_target_pairs={{0,1},{1,2},{2,3},{3,0},{4,5},{5,6},{6,7},{7,4},{8,9},{9,10},{10,1... | collective-permute-start | bytes 2359304 | tf_op jit(solution)/shard_map/ppermute | solution.py:123
  144.8 61.7 %all-to-all-start.1 = ((bf16[16,48,2048]{2,1,0:T(8,128)(2,1)}), bf16[16,48,2048]{2,1,0:T(8,128)(2,1)}, u32[]{:S(2)}, u32[]{:S(2)}) async-start(bf16[16,48,2048]{2,1,0:T(8,128)(2,1)} %bitcast.73), calls=%async_computation.1 | async-start | bytes 6291456 | tf_op jit(solution)/shard_map/all_to_all | solution.py:88
  152.9 4.2 %copy-start.1 = (bf16[768,2048]{1,0:T(8,128)(2,1)S(1)}, bf16[768,2048]{1,0:T(8,128)(2,1)}, u32[]{:S(2)}) copy-start(bf16[768,2048]{1,0:T(8,128)(2,1)} %copy-done) | copy-start | bytes 9437188
  154.9 20.8 %collective-permute-start.11 = (bf16[256,1536]{1,0:T(8,128)(2,1)S(1)}, bf16[256,1536]{1,0:T(8,128)(2,1)S(1)}, u32[]{:S(2)}, u32[]{:S(2)}) collective-permute-start(bf16[256,1536]{1,0:T(8,128)(2,1)S(1)} %convolution_convert_fusion.2), channel_id=1, source_target_pairs={{0,3},{1,0},{2,1},{3,2},{4,7},{5,4},{6,5},{7,6},{8,11},{9,8},{10,9... | collective-permute-start | bytes 2359304 | tf_op jit(solution)/shard_map/ppermute | solution.py:124
  157.9 34.5 %collective-permute-start.8 = (bf16[256,1536]{1,0:T(8,128)(2,1)S(1)}, bf16[256,1536]{1,0:T(8,128)(2,1)S(1)}, u32[]{:S(2)}, u32[]{:S(2)}) collective-permute-start(bf16[256,1536]{1,0:T(8,128)(2,1)S(1)} %convolution_convert_fusion.4), channel_id=1, source_target_pairs={{0,3},{1,0},{2,1},{3,2},{4,7},{5,4},{6,5},{7,6},{8,11},{9,8},{10,9... | collective-permute-start | bytes 2359304 | tf_op jit(solution)/shard_map/ppermute | solution.py:126
  161.2 31.3 %collective-permute-start.10 = (bf16[256,1536]{1,0:T(8,128)(2,1)S(1)}, bf16[256,1536]{1,0:T(8,128)(2,1)S(1)}, u32[]{:S(2)}, u32[]{:S(2)}) collective-permute-start(bf16[256,1536]{1,0:T(8,128)(2,1)S(1)} %add_convert_fusion.3), channel_id=1, source_target_pairs={{0,1},{1,2},{2,3},{3,0},{4,5},{5,6},{6,7},{7,4},{8,9},{9,10},{10,1... | collective-permute-start | bytes 2359304 | tf_op jit(solution)/shard_map/ppermute | solution.py:129
  162.9 32.1 %collective-permute-start.13 = (bf16[256,1536]{1,0:T(8,128)(2,1)S(1)}, bf16[256,1536]{1,0:T(8,128)(2,1)S(1)}, u32[]{:S(2)}, u32[]{:S(2)}) collective-permute-start(bf16[256,1536]{1,0:T(8,128)(2,1)S(1)} %convolution_convert_fusion.1), channel_id=1, source_target_pairs={{0,1},{1,2},{2,3},{3,0},{4,5},{5,6},{6,7},{7,4},{8,9},{9,10},{10,1... | collective-permute-start | bytes 2359304 | tf_op jit(solution)/shard_map/ppermute | solution.py:125
  176.5 16.0 %copy-start.2 = (f32[256,1536]{1,0:T(8,128)S(1)}, f32[256,1536]{1,0:T(8,128)}, u32[]{:S(2)}) copy-start(f32[256,1536]{1,0:T(8,128)} %fusion.37) | copy-start | bytes 4718596
  176.5 28.6 %collective-permute-start.12 = (bf16[256,1536]{1,0:T(8,128)(2,1)S(1)}, bf16[256,1536]{1,0:T(8,128)(2,1)S(1)}, u32[]{:S(2)}, u32[]{:S(2)}) collective-permute-start(bf16[256,1536]{1,0:T(8,128)(2,1)S(1)} %add_convert_fusion.2), channel_id=1, source_target_pairs={{0,3},{1,0},{2,1},{3,2},{4,7},{5,4},{6,5},{7,6},{8,11},{9,8},{10,9... | collective-permute-start | bytes 2359304 | tf_op jit(solution)/shard_map/ppermute | solution.py:130
  206.5 4.0 %copy-start.3 = (f32[1,256,1536]{2,1,0:T(8,128)S(1)}, f32[1,256,1536]{2,1,0:T(8,128)}, u32[]{:S(2)}) copy-start(f32[1,256,1536]{2,1,0:T(8,128)} %add_bitcast_fusion) | copy-start | bytes 4718596
  209.2 3.4 %collective-permute-start.18 = (bf16[64,2048]{1,0:T(8,128)(2,1)S(1)}, bf16[64,2048]{1,0:T(8,128)(2,1)S(1)}, u32[]{:S(2)}, u32[]{:S(2)}) collective-permute-start(bf16[64,2048]{1,0:T(8,128)(2,1)S(1)} %fusion.5), channel_id=1, source_target_pairs={{64,0},{65,1},{66,2},{67,3},{68,4},{69,5},{70,6},{71,7},{72,8},{73... | collective-permute-start | bytes 786440 | tf_op jit(solution)/shard_map/ppermute | solution.py:95
  (2 other events, 4.2 us)

commit v3 on v2

v3 whole, which is shorter than its diff:
```python
import jax
import jax.numpy as jnp
from jax import lax
from jax.sharding import Mesh, PartitionSpec as P

loss_scale_inverse = 0.0625
bf16 = jnp.bfloat16
f32 = jnp.float32
ZY = ("z", "y")
TO_RIGHT = [(i, (i + 1) % 4) for i in range(4)]
TO_LEFT = [(i, (i + 3) % 4) for i in range(4)]


FLIP_1 = [(i, i ^ 1) for i in range(4)]
FLIP_3 = [(i, i ^ 3) for i in range(4)]
MATES = [(4 * z + i, 4 * z + (i ^ (1 if z < 2 else 3))) for z in range(4) for i in range(4)]


def dot(a, b, dims):
    return lax.dot_general(a, b, (dims, ((), ())), preferred_element_type=f32)


def body(w_up, saved_rows, hidden_grad, expert_ids, route_weight):
    experts = lax.axis_size("z") * lax.axis_size("y")
    x = lax.axis_index("x")
    me = lax.axis_index("z") * lax.axis_size("y") + lax.axis_index("y")
    tokens = saved_rows.shape[1]
    width = saved_rows.shape[2]
    top = hidden_grad.shape[2]
    hidden = hidden_grad.shape[3]
    quarter = width // 4
    half = width // 2
    capacity = 3 * tokens * top // (2 * experts)
    slots = experts * capacity

    w = w_up[0]
    mid = quarter // 2
    right_a = lax.ppermute(w[:mid], "x", TO_LEFT)
    left_b = lax.ppermute(w[mid:], "x", TO_RIGHT)
    right_b = lax.ppermute(w[mid:], "x", TO_LEFT)
    left_a = lax.ppermute(w[:mid], "x", TO_RIGHT)
    far_a = lax.ppermute(right_a, "x", TO_LEFT)
    far_b = lax.ppermute(left_b, "x", TO_RIGHT)

    low = lax.axis_index("z") < 2
    other = jnp.where(low, x ^ 3, x ^ 1)
    mate = jnp.where(low, x ^ 1, x ^ 3)

    def features(q, r):
        parts = [lax.dynamic_slice_in_dim(saved_rows[0], i * quarter, quarter, 1) for i in (q, r)]
        return jnp.concatenate(parts, axis=1)

    ids = expert_ids[0]
    ids_t = ids.T
    ids_16 = ids_t.astype(bf16)
    lent = jnp.concatenate([features(mate, x ^ 2), jnp.pad(ids_16, ((0, 0), (0, half - tokens)))], axis=0)
    lent = lax.ppermute(lent, ("z", "x"), MATES)
    ids_pair = jnp.concatenate([ids_16, lent[tokens:, :tokens]], axis=1)
    ids_pair = jnp.pad(ids_pair, ((0, 0), (0, half - 2 * tokens)))
    gathered = lax.all_gather(
        jnp.concatenate([features(x, other), lent[:tokens], ids_pair], axis=0), ZY
    )

    names = jnp.arange(experts, dtype=jnp.int32)
    row = lax.broadcasted_iota(jnp.int32, (tokens, tokens), 0)
    col = lax.broadcasted_iota(jnp.int32, (tokens, tokens), 1)
    earlier = (row < col).astype(bf16)
    chosen = jnp.any(ids_t[:, None, :] == names[None, :, None], axis=0)
    slot = dot(chosen.astype(bf16), earlier, ((1,), (0,))).astype(jnp.int32)
    target_t = jnp.where(chosen, slot, -1)
    target = jnp.sum(
        jnp.where(ids_t[:, None, :] == names[None, :, None], slot[None] + capacity * names[None, :, None], 0), axis=1
    )
    target = target.T.reshape(1, tokens * top)
    place = (lax.broadcasted_iota(jnp.int32, (slots, 1), 0) == target).astype(bf16)
    scaled = (route_weight[0][:, :, None] * hidden_grad[0].astype(f32)).astype(bf16)
    scaled = scaled.reshape(tokens * top, hidden)
    packed = dot(place, scaled, ((1,), (0,))).astype(bf16).reshape(experts, capacity, hidden)
    arrived = lax.all_to_all(packed, ZY, 0, 0, tiled=True).reshape(slots, hidden)

    weights = jnp.concatenate([w, right_a, right_b, far_a, far_b, left_a, left_b], axis=0)
    weights, grads = lax.optimization_barrier((weights, arrived))
    routed = dot(grads, weights, ((1,), (1,))).astype(bf16).reshape(experts, capacity, width)
    back = lax.all_to_all(routed, ZY, 0, 0, tiled=True).reshape(slots, width)
    place_tok = (
        (lax.broadcasted_iota(jnp.int32, (1, capacity, 1), 1) == target_t[:, None, :])
        .astype(bf16)
        .reshape(slots, tokens)
    )
    turned = dot(place_tok, back, ((0,), (0,))).astype(bf16)
    turned = lax.ppermute(turned, "section", [(1, 0)])
    upstream = lax.dynamic_slice_in_dim(
        jnp.concatenate([turned, turned], axis=1), (4 - x) * quarter, width, 1
    )

    named = jnp.any(gathered[:, 2 * tokens :, : 2 * tokens] == me.astype(bf16), axis=1)
    where = dot(named.reshape(2 * experts, tokens).astype(bf16), earlier, ((1,), (0,))).astype(jnp.int32)
    where = where.reshape(experts, 2 * tokens)
    where = where + capacity * (lax.broadcasted_iota(jnp.int32, (1, 2 * tokens), 1) // tokens)
    where = jnp.pad(jnp.where(named, where, -1), ((0, 0), (0, top)), constant_values=-1)
    pick = (lax.broadcasted_iota(jnp.int32, (1, 2 * capacity, 1), 1) == where[:, None, :]).astype(bf16)
    picked = lax.dot_general(
        pick, gathered, (((2,), (1,)), ((0,), (0,))), preferred_element_type=f32
    ).astype(bf16)
    own = 0.0
    fars = []
    for s, flips in ((0, (FLIP_1, FLIP_3)), (1, (FLIP_3, FLIP_1))):
        held = arrived[s * slots // 2 : (s + 1) * slots // 2]
        both = jnp.concatenate(
            [a.reshape(experts // 2, capacity, hidden) for a in (held, lax.ppermute(held, "x", flips[0]))], axis=1
        ).reshape(slots, hidden)
        mine = picked[s * experts // 2 : (s + 1) * experts // 2].reshape(slots, half)
        far = dot(mine[:, quarter:], both, ((0,), (0,))).astype(bf16)
        fars.append(lax.ppermute(far, "x", flips[1]))
        own = own + dot(mine[:, :quarter], both, ((0,), (0,)))
    weight_grad = (own + fars[0].astype(f32) + fars[1].astype(f32)) * loss_scale_inverse
    return weight_grad.astype(bf16)[None], upstream[None]


def solution(mesh):
    grid = Mesh(mesh.devices.reshape(2, 4, 4, 4), ("section", "z", "y", "x"))
    expert = ("z", "y", "x")
    return jax.shard_map(
        body,
        mesh=grid,
        in_specs=(
            P("section", expert, None),
            P("section", expert, None),
            P("section", expert, None, None),
            P("section", expert, None),
            P("section", expert, None),
        ),
        out_specs=(P("section", expert, None), P("section", expert, None)),
        check_vma=False,
    )
```

time: 216 us -> 181 us (0.84)
  starting transfers between devices: 54.9 us -> 29.8 us
  between operations: 0.93 us -> 14.3 us
  waiting for transfers between devices: 87.5 us -> 75.9 us
  matrix products: 40.4 us -> 31.9 us
  other arithmetic: 15.2 us -> 8.06 us
  local copies, waits for them, and re-layouts: 14.5 us -> 20.7 us
    ppermute x18 -> x11, starting transfers between devices: 38.9 us -> 12.3 us  [the longest x1 3.69 us: body(): far_a = lax.ppermute(right_a, 'x', TO_LEFT)]
    ppermute x18 -> x11, waiting for transfers between devices: 86.9 us -> 60.9 us  [the longest x1 13.9 us: body(): far_b = lax.ppermute(left_b, 'x', TO_RIGHT)]
    unnamed x27 -> x29, local copies, waits for them, and re-layouts: 0.15 us -> 15.4 us
    all_to_all x1, waiting for transfers between devices: 0.01 us -> 12.9 us  [body(): back = lax.all_to_all(routed, ZY, 0, 0, tiled=True).reshape(slots, width)]
    dot_general x21 -> x9, matrix products: 40.4 us -> 28 us  [dot(): return lax.dot_general(a, b, (dims, ((), ())), preferred_element_type=f32)]
    concatenate x9 -> x5, other arithmetic: 11.3 us -> 5.57 us  [the longest x2 4.74 us: body(): jnp.concatenate([a.reshape(experts // 2, capacity, hidden) for a in (held...]
    slice x8 -> x5, local copies, waits for them, and re-layouts: 7.37 us -> 2.9 us  [the longest x1 1.26 us: body(): right_b = lax.ppermute(w[mid:], 'x', TO_LEFT)]
    dot_general x0 -> x1, matrix products: none -> 3.87 us  [body(): lax.dot_general(pick, gathered, (((2,), (1,)), ((0,), (0,))), preferred_e...]
  transfers between devices with their start and end apart: 21 -> 15, of which waited for: 11 -> 10; matrix products, arithmetic and copies ran while one was open for 30% -> 28% of each run, Pallas kernels for 0% -> 0%
where the time goes in v3:
time: 181 us
  waiting for transfers between devices  75.9 us (42%)
  matrix products  31.9 us (18%)
  starting transfers between devices  29.8 us (16%)
  local copies, waits for them, and re-layouts  20.7 us (11%)
  between operations  14.3 us (8%)
  other arithmetic  8.06 us (4%)
    dot_general x9, matrix products, dot(): return lax.dot_general(a, b, (dims, ((), ())), preferred_element_type=f32)  28 us
    unnamed x29, local copies, waits for them, and re-layouts  15.4 us
    ppermute x1, waiting for transfers between devices, body(): far_b = lax.ppermute(left_b, 'x', TO_RIGHT)  13.9 us
    all_to_all x1, waiting for transfers between devices, body(): back = lax.all_to_all(routed, ZY, 0, 0, tiled=True).reshape(slots, width)  12.9 us
    ppermute x1, waiting for transfers between devices, body(): left_b = lax.ppermute(w[mid:], 'x', TO_RIGHT)  10.7 us
    ppermute x1, waiting for transfers between devices, body(): far_a = lax.ppermute(right_a, 'x', TO_LEFT)  10.7 us
    ppermute x2, waiting for transfers between devices, body(): fars.append(lax.ppermute(far, 'x', flips[1]))  10.3 us
    ppermute x2, waiting for transfers between devices, body(): lax.ppermute(held, 'x', flips[0])  9.81 us
  transfers between devices with their start and end apart: 15, of which 10 were waited for; matrix products, arithmetic and copies ran while one was open for 28% of the time, Pallas kernels for 0%

profile of v3, /device:TPU:0, one launch (start us, length us, event | category | flops | bytes accessed | tf_op | source)
XLA Modules:
  0.0 180.6 jit_solution(10083493610702347097)
XLA Ops:
  9.1 1.7 collective-permute-start
  10.7 3.8 %collective-permute-done = bf16[72,1024]{1,0:T(8,128)(2,1)S(1)} collective-permute-done((bf16[72,1024]{1,0:T(8,128)(2,1)S(1)}, bf16[72,1024]{1,0:T(8,128)(2,1)S(1)}, u32[]{:S(2)}, u32[]{:S(2)}) %collective-permute-start) | collective-permute-done | bytes 147488 | tf_op jit(solution)/shard_map/ppermute | solution.py:57
  16.7 3.0 %collective-permute-start.5 = (bf16[256,1536]{1,0:T(8,128)(2,1)}, bf16[256,1536]{1,0:T(8,128)(2,1)}, u32[]{:S(2)}, u32[]{:S(2)}) collective-permute-start(bf16[256,1536]{1,0:T(8,128)(2,1)} %get-tuple-element.11), channel_id=1, source_target_pairs={{0,3},{1,0},{2,1},{3,2},{4,7},{5,4},{6,5},{7,6},{8,11},{9,8},{10,9... | collective-permute-start | bytes 2359304 | tf_op jit(solution)/shard_map/ppermute | solution.py:38
  20.3 3.0 %convolution_convert_fusion = bf16[768,1536]{1,0:T(8,128)(2,1)} fusion(bf16[1,64,8,1536]{3,2,1,0:T(8,128)(2,1)S(1)} %copy-done.10, f32[512]{0:T(512)S(1)} %mul.62, s32[512]{0:T(512)S(1)} %eq.76), kind=kOutput, calls=%fused_computation | convolution fusion | flops 1211891712 | bytes 3936256 | tf_op jit(solution)/shard_map/dot_general | solution.py:20
  23.3 9.3 %all-to-all-start = ((bf16[16,48,1536]{2,1,0:T(8,128)(2,1)}), bf16[16,48,1536]{2,1,0:T(8,128)(2,1)S(1)}, u32[]{:S(2)}, u32[]{:S(2)}) async-start(bf16[16,48,1536]{2,1,0:T(8,128)(2,1)} %bitcast.68), calls=%async_computation | async-start | bytes 4718592 | tf_op jit(solution)/shard_map/all_to_all | solution.py:79
  32.7 3.2 %collective-permute-start.6 = (bf16[256,1536]{1,0:T(8,128)(2,1)}, bf16[256,1536]{1,0:T(8,128)(2,1)}, u32[]{:S(2)}, u32[]{:S(2)}) collective-permute-start(bf16[256,1536]{1,0:T(8,128)(2,1)} %get-tuple-element.10), channel_id=1, source_target_pairs={{0,3},{1,0},{2,1},{3,2},{4,7},{5,4},{6,5},{7,6},{8,11},{9,8},{10,9... | collective-permute-start | bytes 2359304 | tf_op jit(solution)/shard_map/ppermute | solution.py:40
  37.4 3.7 %collective-permute-start.7 = (bf16[256,1536]{1,0:T(8,128)(2,1)}, bf16[256,1536]{1,0:T(8,128)(2,1)}, u32[]{:S(2)}, u32[]{:S(2)}) collective-permute-start(bf16[256,1536]{1,0:T(8,128)(2,1)} %collective-permute-done.5), channel_id=1, source_target_pairs={{0,3},{1,0},{2,1},{3,2},{4,7},{5,4},{6,5},{7,6},{8,11},{9,8},{10,9... | collective-permute-start | bytes 2359304 | tf_op jit(solution)/shard_map/ppermute | solution.py:42
  41.1 2.7 %bitcast_dynamic-update-slice_fusion = bf16[2048,1536]{1,0:T(8,128)(2,1)} fusion(bf16[1,512,1536]{2,1,0:T(8,128)(2,1)} %param.5), kind=kLoop, calls=%fused_computation.18 | loop fusion | bytes 3145728
  43.8 10.7 %collective-permute-done.8 = bf16[256,1536]{1,0:T(8,128)(2,1)S(1)} collective-permute-done((bf16[256,1536]{1,0:T(8,128)(2,1)}, bf16[256,1536]{1,0:T(8,128)(2,1)S(1)}, u32[]{:S(2)}, u32[]{:S(2)}) %collective-permute-start.8) | collective-permute-done | bytes 786464 | tf_op jit(solution)/shard_map/ppermute | solution.py:39
  54.6 2.3 %constant_dynamic-update-slice_fusion.5 = bf16[2048,1536]{1,0:T(8,128)(2,1)} fusion(bf16[2048,1536]{1,0:T(8,128)(2,1)} %bitcast_dynamic-update-slice_fusion, bf16[256,1536]{1,0:T(8,128)(2,1)} %collective-permute-done.5), kind=kLoop, calls=%fused_computation.61 | loop fusion | bytes 1572864
  56.9 2.1 %constant_dynamic-update-slice_fusion.4 = bf16[2048,1536]{1,0:T(8,128)(2,1)} fusion(bf16[2048,1536]{1,0:T(8,128)(2,1)} %constant_dynamic-update-slice_fusion.5, bf16[256,1536]{1,0:T(8,128)(2,1)} %collective-permute-done.6), kind=kLoop, calls=%fused_computation.60 | loop fusion | bytes 1572864
  59.0 10.7 %collective-permute-done.7 = bf16[256,1536]{1,0:T(8,128)(2,1)} collective-permute-done((bf16[256,1536]{1,0:T(8,128)(2,1)}, bf16[256,1536]{1,0:T(8,128)(2,1)}, u32[]{:S(2)}, u32[]{:S(2)}) %collective-permute-start.7) | collective-permute-done | bytes 786464 | tf_op jit(solution)/shard_map/ppermute | solution.py:42
  69.7 2.1 %constant_dynamic-update-slice_fusion.3 = bf16[2048,1536]{1,0:T(8,128)(2,1)} fusion(bf16[2048,1536]{1,0:T(8,128)(2,1)} %constant_dynamic-update-slice_fusion.4, bf16[256,1536]{1,0:T(8,128)(2,1)} %collective-permute-done.7), kind=kLoop, calls=%fused_computation.59 | loop fusion | bytes 1572864
  71.8 13.9 %collective-permute-done.9 = bf16[256,1536]{1,0:T(8,128)(2,1)} collective-permute-done((bf16[256,1536]{1,0:T(8,128)(2,1)S(1)}, bf16[256,1536]{1,0:T(8,128)(2,1)}, u32[]{:S(2)}, u32[]{:S(2)}) %collective-permute-start.9) | collective-permute-done | bytes 786464 | tf_op jit(solution)/shard_map/ppermute | solution.py:43
  85.7 2.1 %constant_dynamic-update-slice_fusion.2 = bf16[2048,1536]{1,0:T(8,128)(2,1)} fusion(bf16[2048,1536]{1,0:T(8,128)(2,1)} %constant_dynamic-update-slice_fusion.3, bf16[256,1536]{1,0:T(8,128)(2,1)} %collective-permute-done.9), kind=kLoop, calls=%fused_computation.58 | loop fusion | bytes 1572864
  87.8 2.1 %constant_dynamic-update-slice_fusion.1 = bf16[2048,1536]{1,0:T(8,128)(2,1)} fusion(bf16[2048,1536]{1,0:T(8,128)(2,1)} %constant_dynamic-update-slice_fusion.2, bf16[256,1536]{1,0:T(8,128)(2,1)} %collective-permute-done.10), kind=kLoop, calls=%fused_computation.57 | loop fusion | bytes 1572864
  92.1 9.2 %convolution_convert_fusion.1 = bf16[768,2048]{1,0:T(8,128)(2,1)} fusion(bf16[768,1536]{1,0:T(8,128)(2,1)S(1)} %bitcast.57, bf16[2048,1536]{1,0:T(8,128)(2,1)} %constant_dynamic-update-slice_fusion), kind=kOutput, calls=%fused_computation.1 | convolution fusion | flops 4833411072 | bytes 11796480 | tf_op jit(solution)/shard_map/dot_general | solution.py:20
  101.3 6.9 %all-to-all-start.1 = ((bf16[16,48,2048]{2,1,0:T(8,128)(2,1)}), bf16[16,48,2048]{2,1,0:T(8,128)(2,1)}, u32[]{:S(2)}, u32[]{:S(2)}) async-start(bf16[16,48,2048]{2,1,0:T(8,128)(2,1)} %bitcast.67), calls=%async_computation.1 | async-start | bytes 6291456 | tf_op jit(solution)/shard_map/all_to_all | solution.py:84
  108.2 9.8 %collective-permute-done.2 = bf16[384,1536]{1,0:T(8,128)(2,1)} collective-permute-done((bf16[384,1536]{1,0:T(8,128)(2,1)}, bf16[384,1536]{1,0:T(8,128)(2,1)}, u32[]{:S(2)}, u32[]{:S(2)}) %collective-permute-start.2) | collective-permute-done | bytes 1179680 | tf_op jit(solution)/shard_map/ppermute | solution.py:110
  118.0 1.8 %pad_maximum_fusion.1 = bf16[8,96,1536]{2,1,0:T(8,128)(2,1)S(1)} fusion(bf16[8,48,1536]{2,1,0:T(8,128)(2,1)} %bitcast.17, bf16[8,48,1536]{2,1,0:T(8,128)(2,1)} %get-tuple-element.9), kind=kLoop, calls=%fused_computation.13 | loop fusion | flops 4718592 | bytes 4718592 | tf_op jit(solution)/shard_map/concatenate | solution.py:109
  119.9 2.9 %pad_maximum_fusion = bf16[8,96,1536]{2,1,0:T(8,128)(2,1)} fusion(bf16[8,48,1536]{2,1,0:T(8,128)(2,1)} %bitcast.13, bf16[8,48,1536]{2,1,0:T(8,128)(2,1)S(1)} %get-tuple-element.8), kind=kLoop, calls=%fused_computation.12 | loop fusion | flops 4718592 | bytes 4718592 | tf_op jit(solution)/shard_map/concatenate | solution.py:109
  123.9 3.9 %convolution_convert_fusion.4 = bf16[16,96,1024]{2,1,0:T(8,128)(2,1)S(1)} fusion(bf16[16,136,1024]{2,1,0:T(8,128)(2,1)} %bitcast.64, s32[16,136]{1,0:T(8,128)S(1)} %pad.14), kind=kOutput, calls=%fused_computation.16 | convolution fusion | flops 429600768 | bytes 7610880 | tf_op jit(solution)/shard_map/dot_general | solution.py:102
  128.2 1.9 %copy-done = bf16[8,96,1536]{2,1,0:T(8,128)(2,1)S(1)} copy-done((bf16[8,96,1536]{2,1,0:T(8,128)(2,1)S(1)}, bf16[8,96,1536]{2,1,0:T(8,128)(2,1)}, u32[]{:S(2)}) %copy-start) | copy-done | bytes 2359320
  130.1 2.6 %convolution_convert_fusion.3 = bf16[512,1536]{1,0:T(8,128)(2,1)} fusion(bf16[768,1536]{1,0:T(8,128)(2,1)S(1)} %bitcast.58, bf16[768,1024]{1,0:T(8,128)(2,1)S(1)} %bitcast.65), kind=kOutput, calls=%fused_computation.10 | convolution fusion | flops 1208745984 | bytes 4718592 | tf_op jit(solution)/shard_map/dot_general | solution.py:20
  133.3 2.6 %convolution_convert_fusion.2 = bf16[512,1536]{1,0:T(8,128)(2,1)} fusion(bf16[768,1536]{1,0:T(8,128)(2,1)S(1)} %bitcast.55, bf16[768,1024]{1,0:T(8,128)(2,1)S(1)} %bitcast.60), kind=kOutput, calls=%fused_computation.9 | convolution fusion | flops 1208745984 | bytes 4718592 | tf_op jit(solution)/shard_map/dot_general | solution.py:20
  135.9 12.9 %all-to-all-done.1 = bf16[16,48,2048]{2,1,0:T(8,128)(2,1)} async-done(((bf16[16,48,2048]{2,1,0:T(8,128)(2,1)}), bf16[16,48,2048]{2,1,0:T(8,128)(2,1)}, u32[]{:S(2)}, u32[]{:S(2)}) %all-to-all-start.1) | async-done | bytes 3145760 | tf_op jit(solution)/shard_map/all_to_all | solution.py:84
  148.8 2.6 %fusion.6 = bf16[64,2048]{1,0:T(8,128)(2,1)S(1)} fusion(bf16[16,48,2048]{2,1,0:T(8,128)(2,1)} %all-to-all-done.1, s32[16,64]{1,0:T(8,128)S(1)} %get-tuple-element.16), kind=kOutput, calls=%fused_computation.15 | convolution fusion | flops 201506816 | bytes 3411968 | tf_op jit(solution)/shard_map/dot_general | solution.py:20
  152.7 2.1 %collective-permute-done.11 = bf16[64,2048]{1,0:T(8,128)(2,1)S(1)} collective-permute-done((bf16[64,2048]{1,0:T(8,128)(2,1)S(1)}, bf16[64,2048]{1,0:T(8,128)(2,1)S(1)}, u32[]{:S(2)}, u32[]{:S(2)}) %collective-permute-start.11) | collective-permute-done | bytes 262176 | tf_op jit(solution)/shard_map/ppermute | solution.py:91
  155.7 2.7 %fusion.12 = f32[512,1536]{1,0:T(8,128)S(1)} fusion(bf16[768,1536]{1,0:T(8,128)(2,1)S(1)} %bitcast.56, bf16[768,1024]{1,0:T(8,128)(2,1)} %bitcast.61), kind=kOutput, calls=%fused_computation.26 | convolution fusion | flops 1207959552 | bytes 6291456 | tf_op jit(solution)/shard_map/dot_general | solution.py:20
  158.4 8.7 %collective-permute-done.3 = bf16[512,1536]{1,0:T(8,128)(2,1)} collective-permute-done((bf16[512,1536]{1,0:T(8,128)(2,1)}, bf16[512,1536]{1,0:T(8,128)(2,1)}, u32[]{:S(2)}, u32[]{:S(2)}) %collective-permute-start.3) | collective-permute-done | bytes 1572896 | tf_op jit(solution)/shard_map/ppermute | solution.py:114
  167.1 1.7 collective-permute-done.4
  168.8 5.0 %fusion.5 = bf16[1,512,1536]{2,1,0:T(8,128)(2,1)} fusion(bf16[512,1536]{1,0:T(8,128)(2,1)} %collective-permute-done.4, bf16[512,1536]{1,0:T(8,128)(2,1)} %collective-permute-done.3, f32[512,1536]{1,0:T(8,128)S(1)} %fusion.12, bf16[768,1536]{1,0:T(8,128)(2,1)S(1)} %bitcast.59, bf16[768,1024]{1,0:T(8,128)(2,1)S(1)} %bitcast.66), kind=kOutput, calls=%fused_computation.11 | convolution fusion | flops 1213464576 | bytes 11010048 | tf_op jit(solution)/shard_map/dot_general | solution.py:20
  (64 shorter events, 12.5 us)
Async XLA Ops:
  7.2 8.3 %copy-start.2 = (bf16[1,512,1536]{2,1,0:T(8,128)(2,1)S(1)}, bf16[1,512,1536]{2,1,0:T(8,128)(2,1)}, u32[]{:S(2)}) copy-start(bf16[1,512,1536]{2,1,0:T(8,128)(2,1)} %param.5) | copy-start | bytes 4718596
  7.2 115.6 %all-gather.3.cloned.1.call-start = ((), (), s32[]{:S(2)}) async-start(), calls=%async_computation.2 | async-start | bytes 4734976 | tf_op jit(solution)/shard_map/all_gather | solution.py:60
  9.0 10.7 %copy-start.8 = (s32[1,64,8]{1,2,0:T(8,128)S(1)}, s32[1,64,8]{1,2,0:T(8,128)}, u32[]{:S(2)}) copy-start(s32[1,64,8]{1,2,0:T(8,128)} %param.8) | copy-start | bytes 6148
  9.0 11.1 %copy-start.9 = (f32[1,64,8]{1,2,0:T(8,128)S(1)}, f32[1,64,8]{1,2,0:T(8,128)}, u32[]{:S(2)}) copy-start(f32[1,64,8]{1,2,0:T(8,128)} %param.9) | copy-start | bytes 6148
  9.0 11.2 %copy-start.10 = (bf16[1,64,8,1536]{3,2,1,0:T(8,128)(2,1)S(1)}, bf16[1,64,8,1536]{3,2,1,0:T(8,128)(2,1)}, u32[]{:S(2)}) copy-start(bf16[1,64,8,1536]{3,2,1,0:T(8,128)(2,1)} %param.7) | copy-start | bytes 4718596
  9.1 5.5 %collective-permute-start = (bf16[72,1024]{1,0:T(8,128)(2,1)S(1)}, bf16[72,1024]{1,0:T(8,128)(2,1)S(1)}, u32[]{:S(2)}, u32[]{:S(2)}) collective-permute-start(bf16[72,1024]{1,0:T(8,128)(2,1)S(1)} %fusion.21), channel_id=1, source_target_pairs={{0,1},{1,0},{2,3},{3,2},{16,17},{17,16},{18,19},{19,18},{32,35},{3... | collective-permute-start | bytes 442376 | tf_op jit(solution)/shard_map/ppermute | solution.py:57
  16.7 20.7 %collective-permute-start.5 = (bf16[256,1536]{1,0:T(8,128)(2,1)}, bf16[256,1536]{1,0:T(8,128)(2,1)}, u32[]{:S(2)}, u32[]{:S(2)}) collective-permute-start(bf16[256,1536]{1,0:T(8,128)(2,1)} %get-tuple-element.11), channel_id=1, source_target_pairs={{0,3},{1,0},{2,1},{3,2},{4,7},{5,4},{6,5},{7,6},{8,11},{9,8},{10,9... | collective-permute-start | bytes 2359304 | tf_op jit(solution)/shard_map/ppermute | solution.py:38
  23.3 66.6 %all-to-all-start = ((bf16[16,48,1536]{2,1,0:T(8,128)(2,1)}), bf16[16,48,1536]{2,1,0:T(8,128)(2,1)S(1)}, u32[]{:S(2)}, u32[]{:S(2)}) async-start(bf16[16,48,1536]{2,1,0:T(8,128)(2,1)} %bitcast.68), calls=%async_computation | async-start | bytes 4718592 | tf_op jit(solution)/shard_map/all_to_all | solution.py:79
  32.6 22.0 %collective-permute-start.8 = (bf16[256,1536]{1,0:T(8,128)(2,1)}, bf16[256,1536]{1,0:T(8,128)(2,1)S(1)}, u32[]{:S(2)}, u32[]{:S(2)}) collective-permute-start(bf16[256,1536]{1,0:T(8,128)(2,1)} %get-tuple-element.10), channel_id=1, source_target_pairs={{0,1},{1,2},{2,3},{3,0},{4,5},{5,6},{6,7},{7,4},{8,9},{9,10},{10,1... | collective-permute-start | bytes 2359304 | tf_op jit(solution)/shard_map/ppermute | solution.py:39
  32.7 24.3 %collective-permute-start.6 = (bf16[256,1536]{1,0:T(8,128)(2,1)}, bf16[256,1536]{1,0:T(8,128)(2,1)}, u32[]{:S(2)}, u32[]{:S(2)}) collective-permute-start(bf16[256,1536]{1,0:T(8,128)(2,1)} %get-tuple-element.10), channel_id=1, source_target_pairs={{0,3},{1,0},{2,1},{3,2},{4,7},{5,4},{6,5},{7,6},{8,11},{9,8},{10,9... | collective-permute-start | bytes 2359304 | tf_op jit(solution)/shard_map/ppermute | solution.py:40
  35.9 52.0 %collective-permute-start.10 = (bf16[256,1536]{1,0:T(8,128)(2,1)}, bf16[256,1536]{1,0:T(8,128)(2,1)}, u32[]{:S(2)}, u32[]{:S(2)}) collective-permute-start(bf16[256,1536]{1,0:T(8,128)(2,1)} %get-tuple-element.11), channel_id=1, source_target_pairs={{0,1},{1,2},{2,3},{3,0},{4,5},{5,6},{6,7},{7,4},{8,9},{9,10},{10,1... | collective-permute-start | bytes 2359304 | tf_op jit(solution)/shard_map/ppermute | solution.py:41
  37.4 32.3 %collective-permute-start.7 = (bf16[256,1536]{1,0:T(8,128)(2,1)}, bf16[256,1536]{1,0:T(8,128)(2,1)}, u32[]{:S(2)}, u32[]{:S(2)}) collective-permute-start(bf16[256,1536]{1,0:T(8,128)(2,1)} %collective-permute-done.5), channel_id=1, source_target_pairs={{0,3},{1,0},{2,1},{3,2},{4,7},{5,4},{6,5},{7,6},{8,11},{9,8},{10,9... | collective-permute-start | bytes 2359304 | tf_op jit(solution)/shard_map/ppermute | solution.py:42
  54.5 17.2 %copy-start.6 = (bf16[256,1536]{1,0:T(8,128)(2,1)}, bf16[256,1536]{1,0:T(8,128)(2,1)S(1)}, u32[]{:S(2)}) copy-start(bf16[256,1536]{1,0:T(8,128)(2,1)S(1)} %collective-permute-done.8) | copy-start | bytes 2359300
  54.5 31.2 %collective-permute-start.9 = (bf16[256,1536]{1,0:T(8,128)(2,1)S(1)}, bf16[256,1536]{1,0:T(8,128)(2,1)}, u32[]{:S(2)}, u32[]{:S(2)}) collective-permute-start(bf16[256,1536]{1,0:T(8,128)(2,1)S(1)} %collective-permute-done.8), channel_id=1, source_target_pairs={{0,1},{1,2},{2,3},{3,0},{4,5},{5,6},{6,7},{7,4},{8,9},{9,10},{10,1... | collective-permute-start | bytes 2359304 | tf_op jit(solution)/shard_map/ppermute | solution.py:43
  89.9 1.2 copy-start.7
  91.1 26.9 %collective-permute-start.2 = (bf16[384,1536]{1,0:T(8,128)(2,1)}, bf16[384,1536]{1,0:T(8,128)(2,1)}, u32[]{:S(2)}, u32[]{:S(2)}) collective-permute-start(bf16[384,1536]{1,0:T(8,128)(2,1)} %bitcast.16), channel_id=1, source_target_pairs={{0,3},{1,2},{2,1},{3,0},{4,7},{5,6},{6,5},{7,4},{8,11},{9,10},{10,... | collective-permute-start | bytes 3538952 | tf_op jit(solution)/shard_map/ppermute | solution.py:110
  92.1 27.8 %collective-permute-start.1 = (bf16[384,1536]{1,0:T(8,128)(2,1)S(1)}, bf16[384,1536]{1,0:T(8,128)(2,1)}, u32[]{:S(2)}, u32[]{:S(2)}) collective-permute-start(bf16[384,1536]{1,0:T(8,128)(2,1)S(1)} %bitcast.62), channel_id=1, source_target_pairs={{0,1},{1,0},{2,3},{3,2},{4,5},{5,4},{6,7},{7,6},{8,9},{9,8},{10,11... | collective-permute-start | bytes 3538952 | tf_op jit(solution)/shard_map/ppermute | solution.py:110
  101.3 47.5 %all-to-all-start.1 = ((bf16[16,48,2048]{2,1,0:T(8,128)(2,1)}), bf16[16,48,2048]{2,1,0:T(8,128)(2,1)}, u32[]{:S(2)}, u32[]{:S(2)}) async-start(bf16[16,48,2048]{2,1,0:T(8,128)(2,1)} %bitcast.67), calls=%async_computation.1 | async-start | bytes 6291456 | tf_op jit(solution)/shard_map/all_to_all | solution.py:84
  127.8 2.3 %copy-start = (bf16[8,96,1536]{2,1,0:T(8,128)(2,1)S(1)}, bf16[8,96,1536]{2,1,0:T(8,128)(2,1)}, u32[]{:S(2)}) copy-start(bf16[8,96,1536]{2,1,0:T(8,128)(2,1)} %pad_maximum_fusion) | copy-start | bytes 7077892
  128.2 4.5 %copy-start.4 = (bf16[8,96,1024]{2,1,0:T(8,128)(2,1)}, bf16[8,96,1024]{2,1,0:T(8,128)(2,1)S(1)}, u32[]{:S(2)}) copy-start(bf16[8,96,1024]{2,1,0:T(8,128)(2,1)S(1)} %get-tuple-element.6) | copy-start | bytes 4718596
  128.2 5.1 %copy-start.3 = (bf16[8,96,1024]{2,1,0:T(8,128)(2,1)}, bf16[8,96,1024]{2,1,0:T(8,128)(2,1)S(1)}, u32[]{:S(2)}) copy-start(bf16[8,96,1024]{2,1,0:T(8,128)(2,1)S(1)} %get-tuple-element.7) | copy-start | bytes 4718596
  132.7 34.4 %collective-permute-start.3 = (bf16[512,1536]{1,0:T(8,128)(2,1)}, bf16[512,1536]{1,0:T(8,128)(2,1)}, u32[]{:S(2)}, u32[]{:S(2)}) collective-permute-start(bf16[512,1536]{1,0:T(8,128)(2,1)} %convolution_convert_fusion.3), channel_id=1, source_target_pairs={{0,3},{1,2},{2,1},{3,0},{4,7},{5,6},{6,5},{7,4},{8,11},{9,10},{10,... | collective-permute-start | bytes 4718600 | tf_op jit(solution)/shard_map/ppermute | solution.py:114
  135.9 32.8 %collective-permute-start.4 = (bf16[512,1536]{1,0:T(8,128)(2,1)}, bf16[512,1536]{1,0:T(8,128)(2,1)}, u32[]{:S(2)}, u32[]{:S(2)}) collective-permute-start(bf16[512,1536]{1,0:T(8,128)(2,1)} %convolution_convert_fusion.2), channel_id=1, source_target_pairs={{0,1},{1,0},{2,3},{3,2},{4,5},{5,4},{6,7},{7,6},{8,9},{9,8},{10,11... | collective-permute-start | bytes 4718600 | tf_op jit(solution)/shard_map/ppermute | solution.py:114
  151.4 3.4 %collective-permute-start.11 = (bf16[64,2048]{1,0:T(8,128)(2,1)S(1)}, bf16[64,2048]{1,0:T(8,128)(2,1)S(1)}, u32[]{:S(2)}, u32[]{:S(2)}) collective-permute-start(bf16[64,2048]{1,0:T(8,128)(2,1)S(1)} %fusion.6), channel_id=1, source_target_pairs={{64,0},{65,1},{66,2},{67,3},{68,4},{69,5},{70,6},{71,7},{72,8},{73... | collective-permute-start | bytes 786440 | tf_op jit(solution)/shard_map/ppermute | solution.py:91
  155.7 13.0 %copy-start.1 = (bf16[8,96,1536]{2,1,0:T(8,128)(2,1)S(1)}, bf16[8,96,1536]{2,1,0:T(8,128)(2,1)}, u32[]{:S(2)}) copy-start(bf16[8,96,1536]{2,1,0:T(8,128)(2,1)} %pad_maximum_fusion) | copy-start | bytes 7077892
  155.7 13.1 %copy-start.5 = (bf16[8,96,1024]{2,1,0:T(8,128)(2,1)S(1)}, bf16[8,96,1024]{2,1,0:T(8,128)(2,1)}, u32[]{:S(2)}) copy-start(bf16[8,96,1024]{2,1,0:T(8,128)(2,1)} %copy-done.4) | copy-start | bytes 4718596
Sparse Core Ops, SparseCore 0:
  15.5 77.9 all-gather.2

commit v4 on v3

v4 whole, which is shorter than its diff:
```python
import functools

import jax
import jax.numpy as jnp
from jax import lax
from jax.experimental import pallas as pl
from jax.experimental.pallas import tpu as pltpu
from jax.sharding import Mesh, PartitionSpec as P

loss_scale_inverse = 0.0625
bf16 = jnp.bfloat16
f32 = jnp.float32
ZY = ("z", "y")
TO_RIGHT = [(i, (i + 1) % 4) for i in range(4)]
TO_LEFT = [(i, (i + 3) % 4) for i in range(4)]


FLIP_1 = [(i, i ^ 1) for i in range(4)]
FLIP_3 = [(i, i ^ 3) for i in range(4)]
MATES = [(4 * z + i, 4 * z + (i ^ (1 if z < 2 else 3))) for z in range(4) for i in range(4)]


def dot(a, b, dims):
    return lax.dot_general(a, b, (dims, ((), ())), preferred_element_type=f32)


def pack_kernel(capacity, experts, ids_ref, weight_ref, grad_ref, out_ref, target_ref, route_ref):
    tokens, top = ids_ref.shape
    routes = tokens * top

    @pl.when(pl.program_id(0) == 0)
    def _():
        ids = ids_ref[...]
        names = lax.broadcasted_iota(jnp.int32, (tokens, experts), 1)
        hits = [ids[:, k : k + 1] == names for k in range(top)]
        chosen = jnp.zeros((tokens, experts), f32)
        for hit in hits:
            chosen = chosen + jnp.where(hit, 1.0, 0.0)
        row = lax.broadcasted_iota(jnp.int32, (tokens, tokens), 0)
        col = lax.broadcasted_iota(jnp.int32, (tokens, tokens), 1)
        earlier = jnp.where(col < row, 1.0, 0.0).astype(bf16)
        slot = jnp.dot(earlier, chosen.astype(bf16), preferred_element_type=f32)
        mine = jnp.zeros((tokens, top), f32)
        order = lax.broadcasted_iota(jnp.int32, (tokens, top), 1)
        for k, hit in enumerate(hits):
            one = jnp.sum(jnp.where(hit, slot, 0.0), axis=1, keepdims=True)
            mine = jnp.where(order == k, one, mine)
        spread = jnp.where(
            lax.broadcasted_iota(jnp.int32, (top, routes), 0)
            == lax.broadcasted_iota(jnp.int32, (top, routes), 1) % top,
            1.0,
            0.0,
        ).astype(bf16)
        here = (
            lax.broadcasted_iota(jnp.int32, (tokens, routes), 0)
            == lax.broadcasted_iota(jnp.int32, (tokens, routes), 1) // top
        )

        def as_row(a):
            wide = jnp.dot(a.astype(bf16), spread, preferred_element_type=f32)
            return jnp.sum(jnp.where(here, wide, 0.0), axis=0, keepdims=True)

        target = as_row(mine) + capacity * as_row(ids.astype(f32))
        target_ref[...] = jnp.broadcast_to(target.astype(jnp.int32), target_ref.shape)
        owner = jnp.where(
            lax.broadcasted_iota(jnp.int32, (routes, tokens), 0) // top
            == lax.broadcasted_iota(jnp.int32, (routes, tokens), 1),
            1.0,
            0.0,
        )
        wide = lax.dot_general(
            owner, weight_ref[...], (((1,), (0,)), ((), ())),
            precision=lax.Precision.HIGHEST, preferred_element_type=f32,
        )
        rank = lax.broadcasted_iota(jnp.int32, (routes, top), 0) % top
        wide = jnp.where(lax.broadcasted_iota(jnp.int32, (routes, top), 1) == rank, wide, 0.0)
        route_ref[...] = jnp.broadcast_to(jnp.sum(wide, axis=1, keepdims=True), route_ref.shape)

    slots = experts * capacity
    scaled = (route_ref[:, :1] * grad_ref[...].astype(f32)).astype(bf16)
    place = jnp.where(
        lax.broadcasted_iota(jnp.int32, (slots, routes), 0) == target_ref[:1, :], 1.0, 0.0
    ).astype(bf16)
    out_ref[...] = jnp.dot(place, scaled, preferred_element_type=f32).astype(bf16)


def pack(ids, weights, grads, capacity, experts):
    routes, hidden = grads.shape
    part = hidden // 3
    slots = experts * capacity
    return pl.pallas_call(
        functools.partial(pack_kernel, capacity, experts),
        grid=(3,),
        in_specs=[
            pl.BlockSpec(ids.shape, lambda i: (0, 0)),
            pl.BlockSpec(weights.shape, lambda i: (0, 0)),
            pl.BlockSpec((routes, part), lambda i: (0, i)),
        ],
        out_specs=pl.BlockSpec((slots, part), lambda i: (0, i)),
        out_shape=jax.ShapeDtypeStruct((slots, hidden), bf16),
        scratch_shapes=[pltpu.VMEM((8, routes), jnp.int32), pltpu.VMEM((routes, 128), f32)],
        compiler_params=pltpu.CompilerParams(vmem_limit_bytes=16 << 20),
        cost_estimate=pl.CostEstimate(flops=2 * slots * routes * hidden, bytes_accessed=4 << 20, transcendentals=0),
    )(ids, weights, grads)


def route_kernel(grads, weights, out_hbm, out, sems):
    part = weights.shape[0] // 4
    copies = []
    for i in range(4):
        cols = pl.ds(i * part, part)
        out[:, cols] = lax.dot_general(
            grads[...], weights[cols, :], (((1,), (1,)), ((), ())), preferred_element_type=f32
        ).astype(bf16)
        copies.append(pltpu.make_async_copy(out.at[:, cols], out_hbm.at[:, cols], sems.at[i]))
        copies[-1].start()
    for copy in copies:
        copy.wait()


def route_product(grads, weights):
    slots, hidden = grads.shape
    width = weights.shape[0]
    vmem = pl.BlockSpec(memory_space=pltpu.VMEM)
    return pl.pallas_call(
        route_kernel,
        in_specs=[vmem, vmem],
        out_specs=pl.BlockSpec(memory_space=pltpu.HBM),
        out_shape=jax.ShapeDtypeStruct((slots, width), bf16),
        scratch_shapes=[pltpu.VMEM((slots, width), bf16), pltpu.SemaphoreType.DMA((4,))],
        compiler_params=pltpu.CompilerParams(vmem_limit_bytes=24 << 20),
        cost_estimate=pl.CostEstimate(flops=1, bytes_accessed=1, transcendentals=0),
    )(grads, weights)


def sum_kernel(own_ref, far_a, far_b, out_ref):
    total = own_ref[...] + far_a[...].astype(f32) + far_b[...].astype(f32)
    out_ref[...] = (total * loss_scale_inverse).astype(bf16)


def scaled_sum(own, far_a, far_b):
    rows, hidden = own.shape
    block = pl.BlockSpec((rows // 4, hidden), lambda i: (i, 0))
    return pl.pallas_call(
        sum_kernel,
        grid=(4,),
        in_specs=[block] * 3,
        out_specs=block,
        out_shape=jax.ShapeDtypeStruct((rows, hidden), bf16),
        compiler_params=pltpu.CompilerParams(vmem_limit_bytes=16 << 20),
    )(own, far_a, far_b)


def rows_kernel(capacity, me_ref, rows_hbm, grads_hbm, lent_0, lent_1, far_a, far_b, own_hbm,
                rows, grads, lent, packed, far, own, sems, out_sems):
    experts, span, half = rows.shape
    slots, hidden = grads.shape
    tokens = (span - 16) // 2
    quarter = half // 2
    hs = slots // 2
    in_copies = [
        pltpu.make_async_copy(rows_hbm, rows, sems.at[0]),
        pltpu.make_async_copy(grads_hbm, grads, sems.at[1]),
    ]
    at = 0
    for i, part in enumerate((lent_0, lent_1)):
        n = part.shape[0]
        in_copies.append(pltpu.make_async_copy(part, lent.at[pl.ds(at, n)], sems.at[2 + i]))
        at += n
    for copy in in_copies:
        copy.start()
    row = lax.broadcasted_iota(jnp.int32, (2 * tokens, 2 * tokens), 0)
    col = lax.broadcasted_iota(jnp.int32, (2 * tokens, 2 * tokens), 1)
    same = (row < tokens) == (col < tokens)
    earlier = jnp.where(jnp.logical_and(row < col, same), 1.0, 0.0).astype(bf16)
    me = me_ref[0].astype(f32)
    place = lax.broadcasted_iota(jnp.int32, (1, 2 * tokens), 1)
    base = jnp.where(place < tokens, 0, capacity)
    in_copies[0].wait()
    named = []
    for s in range(experts):
        ids = rows[s, 2 * tokens :, : 2 * tokens].astype(f32)
        named.append(jnp.max(jnp.where(ids == me, 1.0, 0.0), axis=0, keepdims=True))
    named = jnp.concatenate(named, axis=0)
    where = jnp.dot(named.astype(bf16), earlier, preferred_element_type=f32).astype(jnp.int32)
    where = jnp.where(named > 0.5, where + base, -1)
    line = lax.broadcasted_iota(jnp.int32, (2 * capacity, 2 * tokens), 0)
    for s in range(experts):
        pick = jnp.where(line == where[s : s + 1, :], 1.0, 0.0).astype(bf16)
        got = jnp.dot(pick, rows[s, : 2 * tokens, :], preferred_element_type=f32).astype(bf16)
        packed[0, s * capacity : (s + 1) * capacity, :] = got[:capacity]
        packed[1, s * capacity : (s + 1) * capacity, :] = got[capacity:]
    for copy in in_copies[1:]:
        copy.wait()
    tn = (((0,), (0,)), ((), ()))
    part = hidden // 3
    out_copies = []
    for g, out in enumerate((far_a, far_b)):
        span_g = slice(g * hs, (g + 1) * hs)
        for c in range(3):
            cols = slice(c * part, (c + 1) * part)
            sums = lax.dot_general(
                packed[0, span_g, quarter:], grads[span_g, cols], tn, preferred_element_type=f32
            ) + lax.dot_general(
                packed[1, span_g, quarter:], lent[span_g, cols], tn, preferred_element_type=f32
            )
            far[g, :, cols] = sums.astype(bf16)
        out_copies.append(pltpu.make_async_copy(far.at[g], out, out_sems.at[g]))
        out_copies[-1].start()
    own[...] = packed[:, :, :quarter]
    out_copies.append(pltpu.make_async_copy(own, own_hbm, out_sems.at[2]))
    out_copies[-1].start()
    for copy in out_copies:
        copy.wait()


def rows_product(me, rows, grads, lent, capacity):
    experts, span, half = rows.shape
    slots, hidden = grads.shape
    quarter = half // 2
    any_space = pl.BlockSpec(memory_space=pl.ANY)
    return pl.pallas_call(
        functools.partial(rows_kernel, capacity),
        in_specs=[pl.BlockSpec(memory_space=pltpu.SMEM)] + [any_space] * 4,
        out_specs=[pl.BlockSpec(memory_space=pltpu.HBM)] * 2 + [any_space],
        out_shape=[
            jax.ShapeDtypeStruct((quarter, hidden), bf16),
            jax.ShapeDtypeStruct((quarter, hidden), bf16),
            jax.ShapeDtypeStruct((2, slots, quarter), bf16),
        ],
        scratch_shapes=[
            pltpu.VMEM(rows.shape, bf16),
            pltpu.VMEM((slots, hidden), bf16),
            pltpu.VMEM((slots, hidden), bf16),
            pltpu.VMEM((2, slots, half), bf16),
            pltpu.VMEM((2, quarter, hidden), bf16),
            pltpu.VMEM((2, slots, quarter), bf16),
            pltpu.SemaphoreType.DMA((4,)),
            pltpu.SemaphoreType.DMA((3,)),
        ],
        compiler_params=pltpu.CompilerParams(vmem_limit_bytes=24 << 20),
        cost_estimate=pl.CostEstimate(
            flops=60 * slots * quarter * hidden, bytes_accessed=16 << 20, transcendentals=0
        ),
    )(me, rows, grads, *lent)


def body(w_up, saved_rows, hidden_grad, expert_ids, route_weight):
    experts = lax.axis_size("z") * lax.axis_size("y")
    x = lax.axis_index("x")
    me = lax.axis_index("z") * lax.axis_size("y") + lax.axis_index("y")
    tokens = saved_rows.shape[1]
    width = saved_rows.shape[2]
    top = hidden_grad.shape[2]
    hidden = hidden_grad.shape[3]
    quarter = width // 4
    half = width // 2
    capacity = 3 * tokens * top // (2 * experts)
    slots = experts * capacity

    w = w_up[0]
    mid = quarter // 2
    right_a = lax.ppermute(w[:mid], "x", TO_LEFT)
    left_b = lax.ppermute(w[mid:], "x", TO_RIGHT)
    right_b = lax.ppermute(w[mid:], "x", TO_LEFT)
    left_a = lax.ppermute(w[:mid], "x", TO_RIGHT)

    low = lax.axis_index("z") < 2
    other = jnp.where(low, x ^ 3, x ^ 1)
    mate = jnp.where(low, x ^ 1, x ^ 3)

    def features(q, r):
        parts = [lax.dynamic_slice_in_dim(saved_rows[0], i * quarter, quarter, 1) for i in (q, r)]
        return jnp.concatenate(parts, axis=1)

    ids = expert_ids[0]
    ids_t = ids.T
    ids_16 = ids_t.astype(bf16)
    lent = jnp.concatenate([features(mate, x ^ 2), jnp.pad(ids_16, ((0, 0), (0, half - tokens)))], axis=0)
    lent = lax.ppermute(lent, ("z", "x"), MATES)
    ids_pair = jnp.concatenate([ids_16, lent[tokens:, :tokens]], axis=1)
    ids_pair = jnp.pad(ids_pair, ((0, 16 - top), (0, half - 2 * tokens)), constant_values=-1)
    gathered = lax.all_gather(
        jnp.concatenate([features(x, other), lent[:tokens], ids_pair], axis=0), ZY
    )

    names = jnp.arange(experts, dtype=jnp.int32)
    row = lax.broadcasted_iota(jnp.int32, (tokens, tokens), 0)
    col = lax.broadcasted_iota(jnp.int32, (tokens, tokens), 1)
    earlier = (row < col).astype(bf16)
    chosen = jnp.any(ids_t[:, None, :] == names[None, :, None], axis=0)
    slot = dot(chosen.astype(bf16), earlier, ((1,), (0,))).astype(jnp.int32)
    target_t = jnp.where(chosen, slot, -1)
    scaled = hidden_grad[0].reshape(tokens * top, hidden)
    packed = pack(ids, route_weight[0], scaled, capacity, experts).reshape(experts, capacity, hidden)
    packed, right_a, left_b = lax.optimization_barrier((packed, right_a, left_b))
    far_a = lax.ppermute(right_a, "x", TO_LEFT)
    far_b = lax.ppermute(left_b, "x", TO_RIGHT)
    arrived = lax.all_to_all(packed, ZY, 0, 0, tiled=True).reshape(slots, hidden)

    weights = jnp.concatenate([w, right_a, right_b, far_a, far_b, left_a, left_b], axis=0)
    held, weights = lax.optimization_barrier((arrived, weights))
    hs = slots // 2
    lent = [lax.ppermute(held[:hs], "x", FLIP_1), lax.ppermute(held[hs:], "x", FLIP_3)]
    routed = route_product(held, weights)
    routed = routed.reshape(experts, capacity, width)
    back = lax.all_to_all(routed, ZY, 0, 0, tiled=True).reshape(slots, width)
    far_3, far_1, mine = rows_product(me[None], gathered, held, lent, capacity)
    target_t, far_3, far_1 = lax.optimization_barrier((target_t, far_3, far_1))
    place_tok = (
        (lax.broadcasted_iota(jnp.int32, (1, capacity, 1), 1) == target_t[:, None, :])
        .astype(bf16)
        .reshape(slots, tokens)
    )
    turned = dot(place_tok, back, ((0,), (0,))).astype(bf16)
    turned = lax.ppermute(turned, "section", [(1, 0)])
    upstream = lax.dynamic_slice_in_dim(
        jnp.concatenate([turned, turned], axis=1), (4 - x) * quarter, width, 1
    )

    far_3 = lax.ppermute(far_3, "x", FLIP_3)
    far_1 = lax.ppermute(far_1, "x", FLIP_1)
    own = dot(mine[0], held, ((0,), (0,)))
    lo = 0
    for part in lent:
        hi = lo + part.shape[0]
        own = own + dot(mine[1, lo:hi], part, ((0,), (0,)))
        lo = hi
    return scaled_sum(own, far_3, far_1)[None], upstream[None]


def solution(mesh):
    grid = Mesh(mesh.devices.reshape(2, 4, 4, 4), ("section", "z", "y", "x"))
    expert = ("z", "y", "x")
    return jax.shard_map(
        body,
        mesh=grid,
        in_specs=(
            P("section", expert, None),
            P("section", expert, None),
            P("section", expert, None, None),
            P("section", expert, None),
            P("section", expert, None),
        ),
        out_specs=(P("section", expert, None), P("section", expert, None)),
        check_vma=False,
    )
```

time: 181 us -> 173 us (0.956); the launches traced: 181 us -> 170 us
  matrix products: 31.9 us -> 7.62 us
  Pallas kernels: 0 us -> 20.5 us
  other arithmetic: 8.06 us -> 1.7 us
  waiting for transfers between devices: 75.9 us -> 79.4 us
  starting transfers between devices: 29.8 us -> 26.7 us
    pallas_call x0 -> x4, Pallas kernels: none -> 20.5 us  [the longest x1 6.78 us: rows_product(): pl.pallas_call(functools.partial(rows_kernel, capacity), in_specs=[pl.Blo...]
    dot_general x9 -> x5, matrix products: 28 us -> 7.62 us  [dot(): return lax.dot_general(a, b, (dims, ((), ())), preferred_element_type=f32)]
    ppermute x4, waiting for transfers between devices: 20.1 us -> 3.23 us  [the longest x1 1.91 us: body(): lax.ppermute(held[:hs], 'x', FLIP_1)]
    ppermute x1, waiting for transfers between devices: 0.01 us -> 13.9 us  [body(): right_b = lax.ppermute(w[mid:], 'x', TO_LEFT)]
    ppermute x1, waiting for transfers between devices: 13.9 us -> 1.54 us  [body(): far_b = lax.ppermute(left_b, 'x', TO_RIGHT)]
    ppermute x1, waiting for transfers between devices: 1.52 us -> 11.4 us  [body(): right_a = lax.ppermute(w[:mid], 'x', TO_LEFT)]
    all_to_all x1, waiting for transfers between devices: 12.9 us -> 22.2 us  [body(): back = lax.all_to_all(routed, ZY, 0, 0, tiled=True).reshape(slots, width)]
    ppermute x1, waiting for transfers between devices: 10.7 us -> 3.31 us  [body(): left_b = lax.ppermute(w[mid:], 'x', TO_RIGHT)]
  transfers between devices with their start and end apart: 15 -> 15, of which waited for: 10 -> 10; matrix products, arithmetic and copies ran while one was open for 28% -> 8% of each run, Pallas kernels for 0% -> 10%
where the time goes in v4:
time: 173 us; the launch traced here: 170 us
  waiting for transfers between devices  79.4 us (46%)
  starting transfers between devices  26.7 us (15%)
  Pallas kernels  20.5 us (12%)
  local copies, waits for them, and re-layouts  20 us (12%)
  between operations  14.3 us (8%)
  matrix products  7.62 us (4%)
    all_to_all x1, waiting for transfers between devices, body(): back = lax.all_to_all(routed, ZY, 0, 0, tiled=True).reshape(slots, width)  22.2 us
    unnamed x31, local copies, waits for them, and re-layouts  16.1 us
    ppermute x1, waiting for transfers between devices, body(): right_b = lax.ppermute(w[mid:], 'x', TO_LEFT)  13.9 us
    ppermute x1, waiting for transfers between devices, body(): far_a = lax.ppermute(right_a, 'x', TO_LEFT)  13.2 us
    ppermute x1, waiting for transfers between devices, body(): right_a = lax.ppermute(w[:mid], 'x', TO_LEFT)  11.4 us
    all_to_all x1, starting transfers between devices, body(): lax.all_to_all(packed, ZY, 0, 0, tiled=True).reshape(slots, hidden)  9.26 us
    dot_general x5, matrix products, dot(): return lax.dot_general(a, b, (dims, ((), ())), preferred_element_type=f32)  7.62 us
    pallas_call x1, Pallas kernels, rows_product(): pl.pallas_call(functools.partial(rows_kernel, capacity), in_specs=[pl.Blo...  6.78 us
  transfers between devices with their start and end apart: 15, of which 10 were waited for; matrix products, arithmetic and copies ran while one was open for 8% of the time, Pallas kernels for 10%

profile of v4, /device:TPU:0, one launch (start us, length us, event | category | flops | bytes accessed | tf_op | source)
XLA Modules:
  0.0 170.2 jit_solution(3214854612717714268)
XLA Ops:
  9.3 1.7 collective-permute-start
  10.9 3.8 %collective-permute-done = bf16[72,1024]{1,0:T(8,128)(2,1)S(1)} collective-permute-done((bf16[72,1024]{1,0:T(8,128)(2,1)S(1)}, bf16[72,1024]{1,0:T(8,128)(2,1)S(1)}, u32[]{:S(2)}, u32[]{:S(2)}) %collective-permute-start) | collective-permute-done | bytes 147488 | tf_op jit(solution)/shard_map/ppermute | solution.py:280
  15.6 1.3 slice_bitcast_fusion
  16.9 3.0 %collective-permute-start.1 = (bf16[256,1536]{1,0:T(8,128)(2,1)}, bf16[256,1536]{1,0:T(8,128)(2,1)}, u32[]{:S(2)}, u32[]{:S(2)}) collective-permute-start(bf16[256,1536]{1,0:T(8,128)(2,1)} %get-tuple-element.27), channel_id=1, source_target_pairs={{0,3},{1,0},{2,1},{3,2},{4,7},{5,4},{6,5},{7,6},{8,11},{9,8},{10,9... | collective-permute-start | bytes 2359304 | tf_op jit(solution)/shard_map/ppermute | solution.py:263
  20.0 3.2 %shard_map.68 = bf16[768,1536]{1,0:T(8,128)(2,1)S(1)} custom-call(s32[64,8]{1,0:T(8,128)S(1)} %bitcast.53, f32[64,8]{1,0:T(8,128)S(1)} %bitcast.54, bf16[512,1536]{1,0:T(8,128)(2,1)S(1)} %bitcast.56), custom_call_target="tpu_custom_call" | custom-call | flops 1207959552 | bytes 4194304 | tf_op jit(solution)/shard_map/pallas_call | solution.py:91
  23.2 1.5 copy-done.3
  24.7 11.4 %collective-permute-done.1 = bf16[256,1536]{1,0:T(8,128)(2,1)} collective-permute-done((bf16[256,1536]{1,0:T(8,128)(2,1)}, bf16[256,1536]{1,0:T(8,128)(2,1)}, u32[]{:S(2)}, u32[]{:S(2)}) %collective-permute-start.1) | collective-permute-done | bytes 786464 | tf_op jit(solution)/shard_map/ppermute | solution.py:263
  36.1 3.3 %collective-permute-done.2 = bf16[256,1536]{1,0:T(8,128)(2,1)S(1)} collective-permute-done((bf16[256,1536]{1,0:T(8,128)(2,1)}, bf16[256,1536]{1,0:T(8,128)(2,1)S(1)}, u32[]{:S(2)}, u32[]{:S(2)}) %collective-permute-start.2) | collective-permute-done | bytes 786464 | tf_op jit(solution)/shard_map/ppermute | solution.py:264
  39.4 9.3 %all-to-all-start = ((bf16[16,48,1536]{2,1,0:T(8,128)(2,1)}), bf16[16,48,1536]{2,1,0:T(8,128)(2,1)S(1)}, u32[]{:S(2)}, u32[]{:S(2)}) async-start(bf16[16,48,1536]{2,1,0:T(8,128)(2,1)} %bitcast.52), calls=%async_computation | async-start | bytes 4718592 | tf_op jit(solution)/shard_map/all_to_all | solution.py:299
  49.2 1.6 collective-permute-start.6
  50.8 1.6 collective-permute-start.4
  52.8 1.5 bitcast_dynamic-update-slice_fusion
  55.5 13.9 %collective-permute-done.3 = bf16[256,1536]{1,0:T(8,128)(2,1)S(1)} collective-permute-done((bf16[256,1536]{1,0:T(8,128)(2,1)}, bf16[256,1536]{1,0:T(8,128)(2,1)S(1)}, u32[]{:S(2)}, u32[]{:S(2)}) %collective-permute-start.3) | collective-permute-done | bytes 786464 | tf_op jit(solution)/shard_map/ppermute | solution.py:265
  69.5 13.2 %collective-permute-done.4 = bf16[256,1536]{1,0:T(8,128)(2,1)S(1)} collective-permute-done((bf16[256,1536]{1,0:T(8,128)(2,1)}, bf16[256,1536]{1,0:T(8,128)(2,1)S(1)}, u32[]{:S(2)}, u32[]{:S(2)}) %collective-permute-start.4) | collective-permute-done | bytes 786464 | tf_op jit(solution)/shard_map/ppermute | solution.py:297
  82.8 1.5 collective-permute-done.5
  84.6 2.6 %copy-done.1 = bf16[2048,1536]{1,0:T(8,128)(2,1)} copy-done((bf16[2048,1536]{1,0:T(8,128)(2,1)}, bf16[2048,1536]{1,0:T(8,128)(2,1)S(1)}, u32[]{:S(2)}) %copy-start.1) | copy-done | bytes 6291480
  87.2 6.6 %all-to-all-done = bf16[16,48,1536]{2,1,0:T(8,128)(2,1)S(1)} async-done(((bf16[16,48,1536]{2,1,0:T(8,128)(2,1)}), bf16[16,48,1536]{2,1,0:T(8,128)(2,1)S(1)}, u32[]{:S(2)}, u32[]{:S(2)}) %all-to-all-start) | async-done | bytes 2359328 | tf_op jit(solution)/shard_map/all_to_all | solution.py:299
  93.8 1.6 fusion.21
  95.9 2.8 %copy-done.2 = bf16[2048,1536]{1,0:T(8,128)(2,1)S(1)} copy-done((bf16[2048,1536]{1,0:T(8,128)(2,1)S(1)}, bf16[2048,1536]{1,0:T(8,128)(2,1)}, u32[]{:S(2)}) %copy-start.2) | copy-done | bytes 6291480
  98.7 6.5 %shard_map.71 = bf16[768,2048]{1,0:T(8,128)(2,1)S(1)} custom-call(bf16[768,1536]{1,0:T(8,128)(2,1)S(1)} %bitcast.48, bf16[2048,1536]{1,0:T(8,128)(2,1)S(1)} %copy-done.2), custom_call_target="tpu_custom_call" | custom-call | flops 1 | bytes 1 | tf_op jit(solution)/shard_map/pallas_call | solution.py:125
  105.2 1.7 copy-done
  106.8 6.2 %all-to-all-start.1 = ((bf16[16,48,2048]{2,1,0:T(8,128)(2,1)}), bf16[16,48,2048]{2,1,0:T(8,128)(2,1)}, u32[]{:S(2)}, u32[]{:S(2)}) async-start(bf16[16,48,2048]{2,1,0:T(8,128)(2,1)} %bitcast.51), calls=%async_computation.1 | async-start | bytes 6291456 | tf_op jit(solution)/shard_map/all_to_all | solution.py:307
  113.0 1.9 %collective-permute-done.7.lent_0 = bf16[384,1536]{1,0:T(8,128)(2,1)S(1)} collective-permute-done((bf16[384,1536]{1,0:T(8,128)(2,1)}, bf16[384,1536]{1,0:T(8,128)(2,1)S(1)}, u32[]{:S(2)}, u32[]{:S(2)}) %collective-permute-start.7) | collective-permute-done | bytes 1179680 | tf_op jit(solution)/shard_map/ppermute | solution.py:304
  115.0 1.3 collective-permute-done.8.lent_1
  116.3 2.3 %copy-done.6 = bf16[2304,1024]{1,0:T(8,128)(2,1)S(1)} copy-done((bf16[2304,1024]{1,0:T(8,128)(2,1)S(1)}, bf16[2304,1024]{1,0:T(8,128)(2,1)}, u32[]{:S(2)}) %copy-start.6) | copy-done | bytes 4718616
  118.6 6.8 %shard_map.69 = (bf16[512,1536]{1,0:T(8,128)(2,1)}, bf16[512,1536]{1,0:T(8,128)(2,1)}, bf16[2,768,512]{2,1,0:T(8,128)(2,1)S(1)}) custom-call(s32[1]{0:T(128)} %bitcast.me_ref, bf16[16,144,1024]{2,1,0:T(8,128)(2,1)S(1)} %bitcast.55, bf16[768,1536]{1,0:T(8,128)(2,1)S(1)} %bitcast.49, bf16[384,1536]{1,0:T(8,128)(2,1)S(1)} %collective-permute-done.7.lent_0, ...), custom_call_target="tpu_custom_call" | custom-call | flops 36238786560 | bytes 16777216 | tf_op jit(solution)/shard_map/pallas_call | solution.py:222
  127.4 22.2 %all-to-all-done.1 = bf16[16,48,2048]{2,1,0:T(8,128)(2,1)} async-done(((bf16[16,48,2048]{2,1,0:T(8,128)(2,1)}), bf16[16,48,2048]{2,1,0:T(8,128)(2,1)}, u32[]{:S(2)}, u32[]{:S(2)}) %all-to-all-start.1) | async-done | bytes 3145760 | tf_op jit(solution)/shard_map/all_to_all | solution.py:307
  149.6 2.7 %fusion = bf16[64,2048]{1,0:T(8,128)(2,1)S(1)} fusion(bf16[16,48,2048]{2,1,0:T(8,128)(2,1)} %all-to-all-done.1, s32[16,64]{1,0:T(8,128)S(1)} %fusion.1), kind=kOutput, calls=%fused_computation.3 | convolution fusion | flops 201506816 | bytes 3411968 | tf_op jit(solution)/shard_map/dot_general | solution.py:24
  152.3 1.3 collective-permute-start.11
  154.7 1.5 convolution_add_fusion.1
  156.1 2.3 %convolution_add_fusion.own_ref = f32[512,1536]{1,0:T(8,128)S(1)} fusion(f32[512,1536]{1,0:T(8,128)S(1)} %convolution_add_fusion.1, bf16[384,1536]{1,0:T(8,128)(2,1)} %collective-permute-done.8.lent_1, bf16[2,768,512]{2,1,0:T(8,128)(2,1)S(1)} %copy-done.5), kind=kOutput, calls=%fused_computation | convolution fusion | flops 604766208 | bytes 7864320 | tf_op jit(solution)/shard_map/dot_general | solution.py:24
  159.3 4.1 %shard_map.70 = bf16[512,1536]{1,0:T(8,128)(2,1)} custom-call(f32[512,1536]{1,0:T(8,128)S(1)} %convolution_add_fusion.own_ref, bf16[512,1536]{1,0:T(8,128)(2,1)} %collective-permute-done.9.far_a, bf16[512,1536]{1,0:T(8,128)(2,1)} %collective-permute-done.10.far_b), custom_call_target="tpu_custom_call" | custom-call | tf_op jit(solution)/shard_map/pallas_call | solution.py:144
  (51 shorter events, 9.7 us)
Async XLA Ops:
  7.2 8.4 %copy-start.8 = (bf16[1,512,1536]{2,1,0:T(8,128)(2,1)S(1)}, bf16[1,512,1536]{2,1,0:T(8,128)(2,1)}, u32[]{:S(2)}) copy-start(bf16[1,512,1536]{2,1,0:T(8,128)(2,1)} %param.5) | copy-start | bytes 4718596
  7.2 12.7 %copy-start.10 = (f32[1,64,8]{1,2,0:T(8,128)S(1)}, f32[1,64,8]{1,2,0:T(8,128)}, u32[]{:S(2)}) copy-start(f32[1,64,8]{1,2,0:T(8,128)} %param.9) | copy-start | bytes 6148
  7.2 12.8 %copy-start.7 = (bf16[1,64,8,1536]{3,2,1,0:T(8,128)(2,1)S(1)}, bf16[1,64,8,1536]{3,2,1,0:T(8,128)(2,1)}, u32[]{:S(2)}) copy-start(bf16[1,64,8,1536]{3,2,1,0:T(8,128)(2,1)} %param.7) | copy-start | bytes 4718596
  7.2 109.1 %all-gather.3.cloned.1.call-start = ((), (), s32[]{:S(2)}) async-start(), calls=%async_computation.2 | async-start | bytes 5013504 | tf_op jit(solution)/shard_map/all_gather | solution.py:283
  9.3 5.5 %collective-permute-start = (bf16[72,1024]{1,0:T(8,128)(2,1)S(1)}, bf16[72,1024]{1,0:T(8,128)(2,1)S(1)}, u32[]{:S(2)}, u32[]{:S(2)}) collective-permute-start(bf16[72,1024]{1,0:T(8,128)(2,1)S(1)} %fusion.13), channel_id=1, source_target_pairs={{0,1},{1,0},{2,3},{3,2},{16,17},{17,16},{18,19},{19,18},{32,35},{3... | collective-permute-start | bytes 442376 | tf_op jit(solution)/shard_map/ppermute | solution.py:280
  16.9 19.3 %collective-permute-start.1 = (bf16[256,1536]{1,0:T(8,128)(2,1)}, bf16[256,1536]{1,0:T(8,128)(2,1)}, u32[]{:S(2)}, u32[]{:S(2)}) collective-permute-start(bf16[256,1536]{1,0:T(8,128)(2,1)} %get-tuple-element.27), channel_id=1, source_target_pairs={{0,3},{1,0},{2,1},{3,2},{4,7},{5,4},{6,5},{7,6},{8,11},{9,8},{10,9... | collective-permute-start | bytes 2359304 | tf_op jit(solution)/shard_map/ppermute | solution.py:263
  19.9 19.6 %collective-permute-start.2 = (bf16[256,1536]{1,0:T(8,128)(2,1)}, bf16[256,1536]{1,0:T(8,128)(2,1)S(1)}, u32[]{:S(2)}, u32[]{:S(2)}) collective-permute-start(bf16[256,1536]{1,0:T(8,128)(2,1)} %get-tuple-element.26), channel_id=1, source_target_pairs={{0,1},{1,2},{2,3},{3,0},{4,5},{5,6},{6,7},{7,4},{8,9},{9,10},{10,1... | collective-permute-start | bytes 2359304 | tf_op jit(solution)/shard_map/ppermute | solution.py:264
  23.2 1.5 copy-start.3
  39.4 54.4 %all-to-all-start = ((bf16[16,48,1536]{2,1,0:T(8,128)(2,1)}), bf16[16,48,1536]{2,1,0:T(8,128)(2,1)S(1)}, u32[]{:S(2)}, u32[]{:S(2)}) async-start(bf16[16,48,1536]{2,1,0:T(8,128)(2,1)} %bitcast.52), calls=%async_computation | async-start | bytes 4718592 | tf_op jit(solution)/shard_map/all_to_all | solution.py:299
  48.7 20.8 %collective-permute-start.3 = (bf16[256,1536]{1,0:T(8,128)(2,1)}, bf16[256,1536]{1,0:T(8,128)(2,1)S(1)}, u32[]{:S(2)}, u32[]{:S(2)}) collective-permute-start(bf16[256,1536]{1,0:T(8,128)(2,1)} %get-tuple-element.26), channel_id=1, source_target_pairs={{0,3},{1,0},{2,1},{3,2},{4,7},{5,4},{6,5},{7,6},{8,11},{9,8},{10,9... | collective-permute-start | bytes 2359304 | tf_op jit(solution)/shard_map/ppermute | solution.py:265
  49.2 35.3 %collective-permute-start.6 = (bf16[256,1536]{1,0:T(8,128)(2,1)}, bf16[256,1536]{1,0:T(8,128)(2,1)S(1)}, u32[]{:S(2)}, u32[]{:S(2)}) collective-permute-start(bf16[256,1536]{1,0:T(8,128)(2,1)} %get-tuple-element.27), channel_id=1, source_target_pairs={{0,1},{1,2},{2,3},{3,0},{4,5},{5,6},{6,7},{7,4},{8,9},{9,10},{10,1... | collective-permute-start | bytes 2359304 | tf_op jit(solution)/shard_map/ppermute | solution.py:266
  50.8 32.0 %collective-permute-start.4 = (bf16[256,1536]{1,0:T(8,128)(2,1)}, bf16[256,1536]{1,0:T(8,128)(2,1)S(1)}, u32[]{:S(2)}, u32[]{:S(2)}) collective-permute-start(bf16[256,1536]{1,0:T(8,128)(2,1)} %collective-permute-done.1), channel_id=1, source_target_pairs={{0,3},{1,0},{2,1},{3,2},{4,7},{5,4},{6,5},{7,6},{8,11},{9,8},{10,9... | collective-permute-start | bytes 2359304 | tf_op jit(solution)/shard_map/ppermute | solution.py:297
  52.4 32.0 %collective-permute-start.5 = (bf16[256,1536]{1,0:T(8,128)(2,1)S(1)}, bf16[256,1536]{1,0:T(8,128)(2,1)S(1)}, u32[]{:S(2)}, u32[]{:S(2)}) collective-permute-start(bf16[256,1536]{1,0:T(8,128)(2,1)S(1)} %collective-permute-done.2), channel_id=1, source_target_pairs={{0,1},{1,2},{2,3},{3,0},{4,5},{5,6},{6,7},{7,4},{8,9},{9,10},{10,1... | collective-permute-start | bytes 2359304 | tf_op jit(solution)/shard_map/ppermute | solution.py:298
  84.5 11.2 %copy-start.9 = (s32[1,64,8]{1,2,0:T(8,128)S(1)}, s32[1,64,8]{1,2,0:T(8,128)}, u32[]{:S(2)}) copy-start(s32[1,64,8]{1,2,0:T(8,128)} %param.8) | copy-start | bytes 6148
  84.6 2.6 %copy-start.1 = (bf16[2048,1536]{1,0:T(8,128)(2,1)}, bf16[2048,1536]{1,0:T(8,128)(2,1)S(1)}, u32[]{:S(2)}) copy-start(bf16[2048,1536]{1,0:T(8,128)(2,1)S(1)} %constant_dynamic-update-slice_fusion.weights) | copy-start | bytes 18874372
  95.4 19.6 %collective-permute-start.7 = (bf16[384,1536]{1,0:T(8,128)(2,1)}, bf16[384,1536]{1,0:T(8,128)(2,1)S(1)}, u32[]{:S(2)}, u32[]{:S(2)}) collective-permute-start(bf16[384,1536]{1,0:T(8,128)(2,1)} %get-tuple-element.25), channel_id=1, source_target_pairs={{0,1},{1,0},{2,3},{3,2},{4,5},{5,4},{6,7},{7,6},{8,9},{9,8},{10,11... | collective-permute-start | bytes 3538952 | tf_op jit(solution)/shard_map/ppermute | solution.py:304
  95.4 20.9 %collective-permute-start.8 = (bf16[384,1536]{1,0:T(8,128)(2,1)}, bf16[384,1536]{1,0:T(8,128)(2,1)}, u32[]{:S(2)}, u32[]{:S(2)}) collective-permute-start(bf16[384,1536]{1,0:T(8,128)(2,1)} %get-tuple-element.24), channel_id=1, source_target_pairs={{0,3},{1,2},{2,1},{3,0},{4,7},{5,6},{6,5},{7,4},{8,11},{9,10},{10,... | collective-permute-start | bytes 3538952 | tf_op jit(solution)/shard_map/ppermute | solution.py:304
  95.9 2.8 %copy-start.2 = (bf16[2048,1536]{1,0:T(8,128)(2,1)S(1)}, bf16[2048,1536]{1,0:T(8,128)(2,1)}, u32[]{:S(2)}) copy-start(bf16[2048,1536]{1,0:T(8,128)(2,1)} %copy-done.1) | copy-start | bytes 18874372
  105.1 1.7 copy-start
  106.8 42.8 %all-to-all-start.1 = ((bf16[16,48,2048]{2,1,0:T(8,128)(2,1)}), bf16[16,48,2048]{2,1,0:T(8,128)(2,1)}, u32[]{:S(2)}, u32[]{:S(2)}) async-start(bf16[16,48,2048]{2,1,0:T(8,128)(2,1)} %bitcast.51), calls=%async_computation.1 | async-start | bytes 6291456 | tf_op jit(solution)/shard_map/all_to_all | solution.py:307
  116.3 2.3 %copy-start.6 = (bf16[2304,1024]{1,0:T(8,128)(2,1)S(1)}, bf16[2304,1024]{1,0:T(8,128)(2,1)}, u32[]{:S(2)}) copy-start(bf16[2304,1024]{1,0:T(8,128)(2,1)} %all-gather.3.cloned.1.call-done) | copy-start | bytes 14155780
  125.4 1.2 copy-start.4
  126.6 32.7 %collective-permute-start.9 = (bf16[512,1536]{1,0:T(8,128)(2,1)}, bf16[512,1536]{1,0:T(8,128)(2,1)}, u32[]{:S(2)}, u32[]{:S(2)}) collective-permute-start(bf16[512,1536]{1,0:T(8,128)(2,1)} %get-tuple-element.20), channel_id=1, source_target_pairs={{0,3},{1,2},{2,1},{3,0},{4,7},{5,6},{6,5},{7,4},{8,11},{9,10},{10,... | collective-permute-start | bytes 4718600 | tf_op jit(solution)/shard_map/ppermute | solution.py:321
  126.9 32.4 %collective-permute-start.10 = (bf16[512,1536]{1,0:T(8,128)(2,1)}, bf16[512,1536]{1,0:T(8,128)(2,1)}, u32[]{:S(2)}, u32[]{:S(2)}) collective-permute-start(bf16[512,1536]{1,0:T(8,128)(2,1)} %get-tuple-element.21), channel_id=1, source_target_pairs={{0,1},{1,0},{2,3},{3,2},{4,5},{5,4},{6,7},{7,6},{8,9},{9,8},{10,11... | collective-permute-start | bytes 4718600 | tf_op jit(solution)/shard_map/ppermute | solution.py:322
  149.6 4.0 %copy-start.5 = (bf16[2,768,512]{2,1,0:T(8,128)(2,1)S(1)}, bf16[2,768,512]{2,1,0:T(8,128)(2,1)}, u32[]{:S(2)}) copy-start(bf16[2,768,512]{2,1,0:T(8,128)(2,1)} %copy-done.4) | copy-start | bytes 4718596
  152.3 6.1 %collective-permute-start.11 = (bf16[64,2048]{1,0:T(8,128)(2,1)S(1)}, bf16[64,2048]{1,0:T(8,128)(2,1)S(1)}, u32[]{:S(2)}, u32[]{:S(2)}) collective-permute-start(bf16[64,2048]{1,0:T(8,128)(2,1)S(1)} %fusion), channel_id=1, source_target_pairs={{64,0},{65,1},{66,2},{67,3},{68,4},{69,5},{70,6},{71,7},{72,8},{73... | collective-permute-start | bytes 786440 | tf_op jit(solution)/shard_map/ppermute | solution.py:316
Sparse Core Ops, SparseCore 0:
  15.7 79.3 all-gather.2

commit v5 on v4

--- a/solution.py
+++ b/solution.py
@@ -100,37 +100,27 @@
         out_shape=jax.ShapeDtypeStruct((slots, hidden), bf16),
         scratch_shapes=[pltpu.VMEM((8, routes), jnp.int32), pltpu.VMEM((routes, 128), f32)],
         compiler_params=pltpu.CompilerParams(vmem_limit_bytes=16 << 20),
-        cost_estimate=pl.CostEstimate(flops=2 * slots * routes * hidden, bytes_accessed=4 << 20, transcendentals=0),
+        cost_estimate=pl.CostEstimate(flops=1, bytes_accessed=1, transcendentals=0),
     )(ids, weights, grads)
 
 
-def route_kernel(grads, weights, out_hbm, out, sems):
-    part = weights.shape[0] // 4
-    copies = []
-    for i in range(4):
-        cols = pl.ds(i * part, part)
-        out[:, cols] = lax.dot_general(
-            grads[...], weights[cols, :], (((1,), (1,)), ((), ())), preferred_element_type=f32
-        ).astype(bf16)
-        copies.append(pltpu.make_async_copy(out.at[:, cols], out_hbm.at[:, cols], sems.at[i]))
-        copies[-1].start()
-    for copy in copies:
-        copy.wait()
-
-
-def route_product(grads, weights):
+def halves_kernel(grads_ref, low_ref, high_ref):
+    n = low_ref.shape[0]
+    low_ref[...] = grads_ref[:n, :]
+    high_ref[...] = grads_ref[n:, :]
+
+
+def halves(grads):
     slots, hidden = grads.shape
-    width = weights.shape[0]
     vmem = pl.BlockSpec(memory_space=pltpu.VMEM)
     return pl.pallas_call(
-        route_kernel,
-        in_specs=[vmem, vmem],
-        out_specs=pl.BlockSpec(memory_space=pltpu.HBM),
-        out_shape=jax.ShapeDtypeStruct((slots, width), bf16),
-        scratch_shapes=[pltpu.VMEM((slots, width), bf16), pltpu.SemaphoreType.DMA((4,))],
-        compiler_params=pltpu.CompilerParams(vmem_limit_bytes=24 << 20),
-        cost_estimate=pl.CostEstimate(flops=1, bytes_accessed=1, transcendentals=0),
-    )(grads, weights)
+        halves_kernel,
+        in_specs=[vmem],
+        out_specs=[vmem, vmem],
+        out_shape=[jax.ShapeDtypeStruct((slots // 2, hidden), bf16)] * 2,
+        compiler_params=pltpu.CompilerParams(vmem_limit_bytes=12 << 20),
+        cost_estimate=pl.CostEstimate(flops=45 << 30, bytes_accessed=4 << 20, transcendentals=0),
+    )(grads)
 
 
 def sum_kernel(own_ref, far_a, far_b, out_ref):
@@ -278,12 +268,6 @@
     ids_16 = ids_t.astype(bf16)
     lent = jnp.concatenate([features(mate, x ^ 2), jnp.pad(ids_16, ((0, 0), (0, half - tokens)))], axis=0)
     lent = lax.ppermute(lent, ("z", "x"), MATES)
-    ids_pair = jnp.concatenate([ids_16, lent[tokens:, :tokens]], axis=1)
-    ids_pair = jnp.pad(ids_pair, ((0, 16 - top), (0, half - 2 * tokens)), constant_values=-1)
-    gathered = lax.all_gather(
-        jnp.concatenate([features(x, other), lent[:tokens], ids_pair], axis=0), ZY
-    )
-
     names = jnp.arange(experts, dtype=jnp.int32)
     row = lax.broadcasted_iota(jnp.int32, (tokens, tokens), 0)
     col = lax.broadcasted_iota(jnp.int32, (tokens, tokens), 1)
@@ -293,7 +277,13 @@
     target_t = jnp.where(chosen, slot, -1)
     scaled = hidden_grad[0].reshape(tokens * top, hidden)
     packed = pack(ids, route_weight[0], scaled, capacity, experts).reshape(experts, capacity, hidden)
-    packed, right_a, left_b = lax.optimization_barrier((packed, right_a, left_b))
+    packed, lent = lax.optimization_barrier((packed, lent))
+    ids_pair = jnp.concatenate([ids_16, lent[tokens:, :tokens]], axis=1)
+    ids_pair = jnp.pad(ids_pair, ((0, 16 - top), (0, half - 2 * tokens)), constant_values=-1)
+    block = jnp.concatenate([features(x, other), lent[:tokens], ids_pair], axis=0)
+
+    packed, block = lax.optimization_barrier((packed, block))
+    gathered = lax.all_gather(block, ZY)
     far_a = lax.ppermute(right_a, "x", TO_LEFT)
     far_b = lax.ppermute(left_b, "x", TO_RIGHT)
     arrived = lax.all_to_all(packed, ZY, 0, 0, tiled=True).reshape(slots, hidden)
@@ -301,12 +291,21 @@
     weights = jnp.concatenate([w, right_a, right_b, far_a, far_b, left_a, left_b], axis=0)
     held, weights = lax.optimization_barrier((arrived, weights))
     hs = slots // 2
-    lent = [lax.ppermute(held[:hs], "x", FLIP_1), lax.ppermute(held[hs:], "x", FLIP_3)]
-    routed = route_product(held, weights)
+    low_half, high_half = halves(held)
+    lent = [lax.ppermute(low_half, "x", FLIP_1), lax.ppermute(high_half, "x", FLIP_3)]
+    routed = dot(held, weights, ((1,), (1,))).astype(bf16)
     routed = routed.reshape(experts, capacity, width)
     back = lax.all_to_all(routed, ZY, 0, 0, tiled=True).reshape(slots, width)
     far_3, far_1, mine = rows_product(me[None], gathered, held, lent, capacity)
-    target_t, far_3, far_1 = lax.optimization_barrier((target_t, far_3, far_1))
+    far_3 = lax.ppermute(far_3, "x", FLIP_3)
+    far_1 = lax.ppermute(far_1, "x", FLIP_1)
+    own = dot(mine[0], held, ((0,), (0,)))
+    lo = 0
+    for part in lent:
+        hi = lo + part.shape[0]
+        own = own + dot(mine[1, lo:hi], part, ((0,), (0,)))
+        lo = hi
+    target_t, own = lax.optimization_barrier((target_t, own))
     place_tok = (
         (lax.broadcasted_iota(jnp.int32, (1, capacity, 1), 1) == target_t[:, None, :])
         .astype(bf16)
@@ -318,14 +317,6 @@
         jnp.concatenate([turned, turned], axis=1), (4 - x) * quarter, width, 1
     )
 
-    far_3 = lax.ppermute(far_3, "x", FLIP_3)
-    far_1 = lax.ppermute(far_1, "x", FLIP_1)
-    own = dot(mine[0], held, ((0,), (0,)))
-    lo = 0
-    for part in lent:
-        hi = lo + part.shape[0]
-        own = own + dot(mine[1, lo:hi], part, ((0,), (0,)))
-        lo = hi
     return scaled_sum(own, far_3, far_1)[None], upstream[None]
 
 

time: 173 us -> 164 us (0.948); the launches traced: 170 us -> 164 us
  waiting for transfers between devices: 79.4 us -> 66.5 us
  matrix products: 7.62 us -> 17.5 us
  starting transfers between devices: 26.7 us -> 30.6 us
  Pallas kernels: 20.5 us -> 16.6 us
  local copies, waits for them, and re-layouts: 20 us -> 16.5 us
    dot_general x5 -> x6, matrix products: 7.62 us -> 17.5 us  [dot(): return lax.dot_general(a, b, (dims, ((), ())), preferred_element_type=f32)]
    ppermute x1, waiting for transfers between devices: 11.4 us -> 1.58 us  [body(): right_a = lax.ppermute(w[:mid], 'x', TO_LEFT)]
    ppermute x1, waiting for transfers between devices: 13.9 us -> 7.04 us  [body(): right_b = lax.ppermute(w[mid:], 'x', TO_LEFT)]
    all_to_all x1, waiting for transfers between devices: 6.61 us -> 0.01 us  [body(): lax.all_to_all(packed, ZY, 0, 0, tiled=True).reshape(slots, hidden)]
    ppermute x2, waiting for transfers between devices: 3.23 us -> 9.27 us  [the longest x1 7.95 us: body(): lax.ppermute(low_half, 'x', FLIP_1)]
    ppermute x1, waiting for transfers between devices: 1.54 us -> 7.35 us  [body(): far_b = lax.ppermute(left_b, 'x', TO_RIGHT)]
    unnamed x31 -> x17, local copies, waits for them, and re-layouts: 16.1 us -> 10.8 us
    all_to_all x1, waiting for transfers between devices: 22.2 us -> 16.9 us  [body(): back = lax.all_to_all(routed, ZY, 0, 0, tiled=True).reshape(slots, width)]
  transfers between devices with their start and end apart: 15 -> 15, of which waited for: 10 -> 11; matrix products, arithmetic and copies ran while one was open for 8% -> 19% of each run, Pallas kernels for 10% -> 8%
where the time goes in v5:
time: 164 us
  waiting for transfers between devices  66.5 us (41%)
  starting transfers between devices  30.6 us (19%)
  matrix products  17.5 us (11%)
  Pallas kernels  16.6 us (10%)
  local copies, waits for them, and re-layouts  16.5 us (10%)
  between operations  14.2 us (9%)
  other arithmetic  1.71 us (1%)
    dot_general x6, matrix products, dot(): return lax.dot_general(a, b, (dims, ((), ())), preferred_element_type=f32)  17.5 us
    all_to_all x1, waiting for transfers between devices, body(): back = lax.all_to_all(routed, ZY, 0, 0, tiled=True).reshape(slots, width)  16.9 us
    ppermute x1, waiting for transfers between devices, body(): far_a = lax.ppermute(right_a, 'x', TO_LEFT)  14.6 us
    unnamed x17, local copies, waits for them, and re-layouts  10.8 us
    all_to_all x1, starting transfers between devices, body(): lax.all_to_all(packed, ZY, 0, 0, tiled=True).reshape(slots, hidden)  9.23 us
    all_to_all x1, starting transfers between devices, body(): back = lax.all_to_all(routed, ZY, 0, 0, tiled=True).reshape(slots, width)  8.76 us
    ppermute x1, waiting for transfers between devices, body(): lax.ppermute(low_half, 'x', FLIP_1)  7.95 us
    ppermute x1, waiting for transfers between devices, body(): far_b = lax.ppermute(left_b, 'x', TO_RIGHT)  7.35 us
  transfers between devices with their start and end apart: 15, of which 11 were waited for; matrix products, arithmetic and copies ran while one was open for 19% of the time, Pallas kernels for 8%

profile of v5, /device:TPU:0, one launch (start us, length us, event | category | flops | bytes accessed | tf_op | source)
XLA Modules:
  0.0 163.6 jit_solution(1692587230950928517)
XLA Ops:
  8.2 1.0 dynamic-slice_bitcast_fusion.1
  9.2 1.7 %collective-permute-start = (bf16[72,1024]{1,0:T(8,128)(2,1)S(1)}, bf16[72,1024]{1,0:T(8,128)(2,1)S(1)}, u32[]{:S(2)}, u32[]{:S(2)}) collective-permute-start(bf16[72,1024]{1,0:T(8,128)(2,1)S(1)} %fusion.13), channel_id=1, source_target_pairs={{0,1},{1,0},{2,3},{3,2},{16,17},{17,16},{18,19},{19,18},{32,35},{3... | collective-permute-start | bytes 442376 | tf_op jit(solution)/shard_map/ppermute | solution.py:270
  10.9 2.6 %slice_bitcast_fusion = (bf16[256,1536]{1,0:T(8,128)(2,1)}, bf16[256,1536]{1,0:T(8,128)(2,1)}) fusion(bf16[1,512,1536]{2,1,0:T(8,128)(2,1)} %param.5), kind=kLoop, calls=%fused_computation.10 | loop fusion | bytes 3145728 | tf_op jit(solution)/shard_map/slice | solution.py:255
  13.5 2.1 %collective-permute-start.1 = (bf16[256,1536]{1,0:T(8,128)(2,1)}, bf16[256,1536]{1,0:T(8,128)(2,1)S(1)}, u32[]{:S(2)}, u32[]{:S(2)}) collective-permute-start(bf16[256,1536]{1,0:T(8,128)(2,1)} %get-tuple-element.29), channel_id=1, source_target_pairs={{0,3},{1,0},{2,1},{3,2},{4,7},{5,4},{6,5},{7,6},{8,11},{9,8},{10,9... | collective-permute-start | bytes 2359304 | tf_op jit(solution)/shard_map/ppermute | solution.py:253
  15.7 4.2 %shard_map.68 = bf16[768,1536]{1,0:T(8,128)(2,1)} custom-call(s32[64,8]{1,0:T(8,128)S(1)} %bitcast.54, f32[64,8]{1,0:T(8,128)S(1)} %bitcast.55, bf16[512,1536]{1,0:T(8,128)(2,1)S(1)} %bitcast.53), custom_call_target="tpu_custom_call" | custom-call | flops 1 | bytes 1 | tf_op jit(solution)/shard_map/pallas_call | solution.py:91
  20.8 9.2 %all-to-all-start = ((bf16[16,48,1536]{2,1,0:T(8,128)(2,1)}), bf16[16,48,1536]{2,1,0:T(8,128)(2,1)S(1)}, u32[]{:S(2)}, u32[]{:S(2)}) async-start(bf16[16,48,1536]{2,1,0:T(8,128)(2,1)} %bitcast.6), calls=%async_computation | async-start | bytes 4718592 | tf_op jit(solution)/shard_map/all_to_all | solution.py:289
  30.1 1.8 %collective-permute-start.2 = (bf16[256,1536]{1,0:T(8,128)(2,1)}, bf16[256,1536]{1,0:T(8,128)(2,1)S(1)}, u32[]{:S(2)}, u32[]{:S(2)}) collective-permute-start(bf16[256,1536]{1,0:T(8,128)(2,1)} %get-tuple-element.28), channel_id=1, source_target_pairs={{0,3},{1,0},{2,1},{3,2},{4,7},{5,4},{6,5},{7,6},{8,11},{9,8},{10,9... | collective-permute-start | bytes 2359304 | tf_op jit(solution)/shard_map/ppermute | solution.py:255
  32.2 1.6 collective-permute-done.1
  33.8 3.6 %collective-permute-start.3 = (bf16[256,1536]{1,0:T(8,128)(2,1)S(1)}, bf16[256,1536]{1,0:T(8,128)(2,1)S(1)}, u32[]{:S(2)}, u32[]{:S(2)}) collective-permute-start(bf16[256,1536]{1,0:T(8,128)(2,1)S(1)} %collective-permute-done.1), channel_id=1, source_target_pairs={{0,3},{1,0},{2,1},{3,2},{4,7},{5,4},{6,5},{7,6},{8,11},{9,8},{10,9... | collective-permute-start | bytes 2359304 | tf_op jit(solution)/shard_map/ppermute | solution.py:287
  37.4 2.7 %bitcast_dynamic-update-slice_fusion = bf16[2048,1536]{1,0:T(8,128)(2,1)} fusion(bf16[1,512,1536]{2,1,0:T(8,128)(2,1)} %param.5), kind=kLoop, calls=%fused_computation.5 | loop fusion | bytes 3145728
  40.0 2.8 %collective-permute-done.4 = bf16[256,1536]{1,0:T(8,128)(2,1)} collective-permute-done((bf16[256,1536]{1,0:T(8,128)(2,1)}, bf16[256,1536]{1,0:T(8,128)(2,1)}, u32[]{:S(2)}, u32[]{:S(2)}) %collective-permute-start.4) | collective-permute-done | bytes 786464 | tf_op jit(solution)/shard_map/ppermute | solution.py:254
  43.8 7.0 %collective-permute-done.2 = bf16[256,1536]{1,0:T(8,128)(2,1)S(1)} collective-permute-done((bf16[256,1536]{1,0:T(8,128)(2,1)}, bf16[256,1536]{1,0:T(8,128)(2,1)S(1)}, u32[]{:S(2)}, u32[]{:S(2)}) %collective-permute-start.2) | collective-permute-done | bytes 786464 | tf_op jit(solution)/shard_map/ppermute | solution.py:255
  51.8 14.6 %collective-permute-done.3 = bf16[256,1536]{1,0:T(8,128)(2,1)S(1)} collective-permute-done((bf16[256,1536]{1,0:T(8,128)(2,1)S(1)}, bf16[256,1536]{1,0:T(8,128)(2,1)S(1)}, u32[]{:S(2)}, u32[]{:S(2)}) %collective-permute-start.3) | collective-permute-done | bytes 786464 | tf_op jit(solution)/shard_map/ppermute | solution.py:287
  67.3 7.4 %collective-permute-done.5 = bf16[256,1536]{1,0:T(8,128)(2,1)S(1)} collective-permute-done((bf16[256,1536]{1,0:T(8,128)(2,1)}, bf16[256,1536]{1,0:T(8,128)(2,1)S(1)}, u32[]{:S(2)}, u32[]{:S(2)}) %collective-permute-start.5) | collective-permute-done | bytes 786464 | tf_op jit(solution)/shard_map/ppermute | solution.py:288
  76.6 2.1 %constant_dynamic-update-slice_fusion = bf16[2048,1536]{1,0:T(8,128)(2,1)} fusion(bf16[2048,1536]{1,0:T(8,128)(2,1)} %constant_dynamic-update-slice_fusion.1, bf16[256,1536]{1,0:T(8,128)(2,1)} %collective-permute-done.4), kind=kLoop, calls=%fused_computation.43 | loop fusion | bytes 1572864 | tf_op jit(solution)/shard_map/concatenate | solution.py:291
  78.7 1.6 shard_map.69
  80.6 9.3 %convolution_convert_fusion = bf16[768,2048]{1,0:T(8,128)(2,1)} fusion(bf16[768,1536]{1,0:T(8,128)(2,1)S(1)} %bitcast.50, bf16[2048,1536]{1,0:T(8,128)(2,1)} %constant_dynamic-update-slice_fusion), kind=kOutput, calls=%fused_computation | convolution fusion | flops 4833411072 | bytes 11796480 | tf_op jit(solution)/shard_map/dot_general | solution.py:24
  89.9 8.8 %all-to-all-start.1 = ((bf16[16,48,2048]{2,1,0:T(8,128)(2,1)}), bf16[16,48,2048]{2,1,0:T(8,128)(2,1)}, u32[]{:S(2)}, u32[]{:S(2)}) async-start(bf16[16,48,2048]{2,1,0:T(8,128)(2,1)} %bitcast.57), calls=%async_computation.1 | async-start | bytes 6291456 | tf_op jit(solution)/shard_map/all_to_all | solution.py:298
  98.7 8.0 %collective-permute-done.7.lent_0 = bf16[384,1536]{1,0:T(8,128)(2,1)S(1)} collective-permute-done((bf16[384,1536]{1,0:T(8,128)(2,1)}, bf16[384,1536]{1,0:T(8,128)(2,1)S(1)}, u32[]{:S(2)}, u32[]{:S(2)}) %collective-permute-start.7) | collective-permute-done | bytes 1179680 | tf_op jit(solution)/shard_map/ppermute | solution.py:295
  106.7 1.3 collective-permute-done.8.lent_1
  108.0 2.3 %copy-done.1 = bf16[2304,1024]{1,0:T(8,128)(2,1)S(1)} copy-done((bf16[2304,1024]{1,0:T(8,128)(2,1)S(1)}, bf16[2304,1024]{1,0:T(8,128)(2,1)}, u32[]{:S(2)}) %copy-start.1) | copy-done | bytes 4718616
  110.3 6.8 %shard_map.70 = (bf16[512,1536]{1,0:T(8,128)(2,1)}, bf16[512,1536]{1,0:T(8,128)(2,1)}, bf16[2,768,512]{2,1,0:T(8,128)(2,1)S(1)}) custom-call(s32[1]{0:T(128)} %bitcast.3.me_ref, bf16[16,144,1024]{2,1,0:T(8,128)(2,1)S(1)} %bitcast.56, bf16[768,1536]{1,0:T(8,128)(2,1)S(1)} %bitcast.51, bf16[384,1536]{1,0:T(8,128)(2,1)S(1)} %collective-permute-done.7.lent_0, ...), custom_call_target="tpu_custom_call" | custom-call | flops 36238786560 | bytes 16777216 | tf_op jit(solution)/shard_map/pallas_call | solution.py:212
  118.6 1.0 fusion.5
  119.6 1.5 convolution_add_fusion.1
  121.1 2.3 %convolution_add_fusion.own_ref = f32[512,1536]{1,0:T(8,128)S(1)} fusion(f32[512,1536]{1,0:T(8,128)S(1)} %convolution_add_fusion.1, bf16[384,1536]{1,0:T(8,128)(2,1)} %collective-permute-done.8.lent_1, bf16[2,768,512]{2,1,0:T(8,128)(2,1)S(1)} %get-tuple-element.22), kind=kOutput, calls=%fused_computation.1 | convolution fusion | flops 604766208 | bytes 7864320 | tf_op jit(solution)/shard_map/dot_general | solution.py:24
  123.4 16.9 %all-to-all-done.1 = bf16[16,48,2048]{2,1,0:T(8,128)(2,1)} async-done(((bf16[16,48,2048]{2,1,0:T(8,128)(2,1)}), bf16[16,48,2048]{2,1,0:T(8,128)(2,1)}, u32[]{:S(2)}, u32[]{:S(2)}) %all-to-all-start.1) | async-done | bytes 3145760 | tf_op jit(solution)/shard_map/all_to_all | solution.py:298
  140.3 3.3 %fusion = bf16[64,2048]{1,0:T(8,128)(2,1)} fusion(bf16[16,48,2048]{2,1,0:T(8,128)(2,1)} %all-to-all-done.1, s32[16,64]{1,0:T(8,128)S(1)} %fusion.1), kind=kOutput, calls=%fused_computation.4 | convolution fusion | flops 201506816 | bytes 3411968 | tf_op jit(solution)/shard_map/dot_general | solution.py:24
  143.6 1.3 collective-permute-start.11
  144.9 2.3 %collective-permute-done.11 = bf16[64,2048]{1,0:T(8,128)(2,1)S(1)} collective-permute-done((bf16[64,2048]{1,0:T(8,128)(2,1)}, bf16[64,2048]{1,0:T(8,128)(2,1)S(1)}, u32[]{:S(2)}, u32[]{:S(2)}) %collective-permute-start.11) | collective-permute-done | bytes 262176 | tf_op jit(solution)/shard_map/ppermute | solution.py:315
  148.0 3.2 %collective-permute-done.10.far_b = bf16[512,1536]{1,0:T(8,128)(2,1)} collective-permute-done((bf16[512,1536]{1,0:T(8,128)(2,1)}, bf16[512,1536]{1,0:T(8,128)(2,1)}, u32[]{:S(2)}, u32[]{:S(2)}) %collective-permute-start.10) | collective-permute-done | bytes 1572896 | tf_op jit(solution)/shard_map/ppermute | solution.py:301
  151.2 1.5 collective-permute-done.9.far_a
  152.7 4.1 %shard_map.71 = bf16[512,1536]{1,0:T(8,128)(2,1)} custom-call(f32[512,1536]{1,0:T(8,128)S(1)} %convolution_add_fusion.own_ref, bf16[512,1536]{1,0:T(8,128)(2,1)} %collective-permute-done.9.far_a, bf16[512,1536]{1,0:T(8,128)(2,1)} %collective-permute-done.10.far_b), custom_call_target="tpu_custom_call" | custom-call | tf_op jit(solution)/shard_map/pallas_call | solution.py:134
  (37 shorter events, 9.8 us)
Async XLA Ops:
  7.2 8.4 %copy-start.3 = (f32[1,64,8]{1,2,0:T(8,128)S(1)}, f32[1,64,8]{1,2,0:T(8,128)}, u32[]{:S(2)}) copy-start(f32[1,64,8]{1,2,0:T(8,128)} %param.9) | copy-start | bytes 6148
  7.2 8.5 %copy-start = (bf16[1,64,8,1536]{3,2,1,0:T(8,128)(2,1)S(1)}, bf16[1,64,8,1536]{3,2,1,0:T(8,128)(2,1)}, u32[]{:S(2)}) copy-start(bf16[1,64,8,1536]{3,2,1,0:T(8,128)(2,1)} %param.7) | copy-start | bytes 4718596
  7.2 100.8 %all-gather.3.cloned.1.call-start = ((), (), s32[]{:S(2)}) async-start(), calls=%async_computation.2 | async-start | bytes 5013504 | tf_op jit(solution)/shard_map/all_gather | solution.py:286
  9.2 10.7 %collective-permute-start = (bf16[72,1024]{1,0:T(8,128)(2,1)S(1)}, bf16[72,1024]{1,0:T(8,128)(2,1)S(1)}, u32[]{:S(2)}, u32[]{:S(2)}) collective-permute-start(bf16[72,1024]{1,0:T(8,128)(2,1)S(1)} %fusion.13), channel_id=1, source_target_pairs={{0,1},{1,0},{2,3},{3,2},{16,17},{17,16},{18,19},{19,18},{32,35},{3... | collective-permute-start | bytes 442376 | tf_op jit(solution)/shard_map/ppermute | solution.py:270
  13.5 20.3 %collective-permute-start.1 = (bf16[256,1536]{1,0:T(8,128)(2,1)}, bf16[256,1536]{1,0:T(8,128)(2,1)S(1)}, u32[]{:S(2)}, u32[]{:S(2)}) collective-permute-start(bf16[256,1536]{1,0:T(8,128)(2,1)} %get-tuple-element.29), channel_id=1, source_target_pairs={{0,3},{1,0},{2,1},{3,2},{4,7},{5,4},{6,5},{7,6},{8,11},{9,8},{10,9... | collective-permute-start | bytes 2359304 | tf_op jit(solution)/shard_map/ppermute | solution.py:253
  20.8 22.1 %copy-start.2 = (s32[1,64,8]{1,2,0:T(8,128)S(1)}, s32[1,64,8]{1,2,0:T(8,128)}, u32[]{:S(2)}) copy-start(s32[1,64,8]{1,2,0:T(8,128)} %param.8) | copy-start | bytes 6148
  20.8 22.1 %collective-permute-start.4 = (bf16[256,1536]{1,0:T(8,128)(2,1)}, bf16[256,1536]{1,0:T(8,128)(2,1)}, u32[]{:S(2)}, u32[]{:S(2)}) collective-permute-start(bf16[256,1536]{1,0:T(8,128)(2,1)} %get-tuple-element.28), channel_id=1, source_target_pairs={{0,1},{1,2},{2,3},{3,0},{4,5},{5,6},{6,7},{7,4},{8,9},{9,10},{10,1... | collective-permute-start | bytes 2359304 | tf_op jit(solution)/shard_map/ppermute | solution.py:254
  20.8 57.8 %all-to-all-start = ((bf16[16,48,1536]{2,1,0:T(8,128)(2,1)}), bf16[16,48,1536]{2,1,0:T(8,128)(2,1)S(1)}, u32[]{:S(2)}, u32[]{:S(2)}) async-start(bf16[16,48,1536]{2,1,0:T(8,128)(2,1)} %bitcast.6), calls=%async_computation | async-start | bytes 4718592 | tf_op jit(solution)/shard_map/all_to_all | solution.py:289
  30.1 20.8 %collective-permute-start.2 = (bf16[256,1536]{1,0:T(8,128)(2,1)}, bf16[256,1536]{1,0:T(8,128)(2,1)S(1)}, u32[]{:S(2)}, u32[]{:S(2)}) collective-permute-start(bf16[256,1536]{1,0:T(8,128)(2,1)} %get-tuple-element.28), channel_id=1, source_target_pairs={{0,3},{1,0},{2,1},{3,2},{4,7},{5,4},{6,5},{7,6},{8,11},{9,8},{10,9... | collective-permute-start | bytes 2359304 | tf_op jit(solution)/shard_map/ppermute | solution.py:255
  31.8 43.8 %collective-permute-start.6 = (bf16[256,1536]{1,0:T(8,128)(2,1)}, bf16[256,1536]{1,0:T(8,128)(2,1)S(1)}, u32[]{:S(2)}, u32[]{:S(2)}) collective-permute-start(bf16[256,1536]{1,0:T(8,128)(2,1)} %get-tuple-element.29), channel_id=1, source_target_pairs={{0,1},{1,2},{2,3},{3,0},{4,5},{5,6},{6,7},{7,4},{8,9},{9,10},{10,1... | collective-permute-start | bytes 2359304 | tf_op jit(solution)/shard_map/ppermute | solution.py:256
  33.8 32.6 %collective-permute-start.3 = (bf16[256,1536]{1,0:T(8,128)(2,1)S(1)}, bf16[256,1536]{1,0:T(8,128)(2,1)S(1)}, u32[]{:S(2)}, u32[]{:S(2)}) collective-permute-start(bf16[256,1536]{1,0:T(8,128)(2,1)S(1)} %collective-permute-done.1), channel_id=1, source_target_pairs={{0,3},{1,0},{2,1},{3,2},{4,7},{5,4},{6,5},{7,6},{8,11},{9,8},{10,9... | collective-permute-start | bytes 2359304 | tf_op jit(solution)/shard_map/ppermute | solution.py:287
  42.8 31.8 %collective-permute-start.5 = (bf16[256,1536]{1,0:T(8,128)(2,1)}, bf16[256,1536]{1,0:T(8,128)(2,1)S(1)}, u32[]{:S(2)}, u32[]{:S(2)}) collective-permute-start(bf16[256,1536]{1,0:T(8,128)(2,1)} %collective-permute-done.4), channel_id=1, source_target_pairs={{0,1},{1,2},{2,3},{3,0},{4,5},{5,6},{6,7},{7,4},{8,9},{9,10},{10,1... | collective-permute-start | bytes 2359304 | tf_op jit(solution)/shard_map/ppermute | solution.py:288
  80.3 26.4 %collective-permute-start.7 = (bf16[384,1536]{1,0:T(8,128)(2,1)}, bf16[384,1536]{1,0:T(8,128)(2,1)S(1)}, u32[]{:S(2)}, u32[]{:S(2)}) collective-permute-start(bf16[384,1536]{1,0:T(8,128)(2,1)} %get-tuple-element.20), channel_id=1, source_target_pairs={{0,1},{1,0},{2,3},{3,2},{4,5},{5,4},{6,7},{7,6},{8,9},{9,8},{10,11... | collective-permute-start | bytes 3538952 | tf_op jit(solution)/shard_map/ppermute | solution.py:295
  80.3 27.7 %collective-permute-start.8 = (bf16[384,1536]{1,0:T(8,128)(2,1)}, bf16[384,1536]{1,0:T(8,128)(2,1)}, u32[]{:S(2)}, u32[]{:S(2)}) collective-permute-start(bf16[384,1536]{1,0:T(8,128)(2,1)} %get-tuple-element.21), channel_id=1, source_target_pairs={{0,3},{1,2},{2,1},{3,0},{4,7},{5,6},{6,5},{7,4},{8,11},{9,10},{10,... | collective-permute-start | bytes 3538952 | tf_op jit(solution)/shard_map/ppermute | solution.py:295
  89.9 50.3 %all-to-all-start.1 = ((bf16[16,48,2048]{2,1,0:T(8,128)(2,1)}), bf16[16,48,2048]{2,1,0:T(8,128)(2,1)}, u32[]{:S(2)}, u32[]{:S(2)}) async-start(bf16[16,48,2048]{2,1,0:T(8,128)(2,1)} %bitcast.57), calls=%async_computation.1 | async-start | bytes 6291456 | tf_op jit(solution)/shard_map/all_to_all | solution.py:298
  108.0 2.3 %copy-start.1 = (bf16[2304,1024]{1,0:T(8,128)(2,1)S(1)}, bf16[2304,1024]{1,0:T(8,128)(2,1)}, u32[]{:S(2)}) copy-start(bf16[2304,1024]{1,0:T(8,128)(2,1)} %all-gather.3.cloned.1.call-done) | copy-start | bytes 14155780
  117.1 34.1 %collective-permute-start.10 = (bf16[512,1536]{1,0:T(8,128)(2,1)}, bf16[512,1536]{1,0:T(8,128)(2,1)}, u32[]{:S(2)}, u32[]{:S(2)}) collective-permute-start(bf16[512,1536]{1,0:T(8,128)(2,1)} %get-tuple-element.25), channel_id=1, source_target_pairs={{0,1},{1,0},{2,3},{3,2},{4,5},{5,4},{6,7},{7,6},{8,9},{9,8},{10,11... | collective-permute-start | bytes 4718600 | tf_op jit(solution)/shard_map/ppermute | solution.py:301
  117.7 35.0 %collective-permute-start.9 = (bf16[512,1536]{1,0:T(8,128)(2,1)}, bf16[512,1536]{1,0:T(8,128)(2,1)}, u32[]{:S(2)}, u32[]{:S(2)}) collective-permute-start(bf16[512,1536]{1,0:T(8,128)(2,1)} %get-tuple-element.24), channel_id=1, source_target_pairs={{0,3},{1,2},{2,1},{3,0},{4,7},{5,6},{6,5},{7,4},{8,11},{9,10},{10,... | collective-permute-start | bytes 4718600 | tf_op jit(solution)/shard_map/ppermute | solution.py:300
  143.6 3.6 %collective-permute-start.11 = (bf16[64,2048]{1,0:T(8,128)(2,1)}, bf16[64,2048]{1,0:T(8,128)(2,1)S(1)}, u32[]{:S(2)}, u32[]{:S(2)}) collective-permute-start(bf16[64,2048]{1,0:T(8,128)(2,1)} %fusion), channel_id=1, source_target_pairs={{64,0},{65,1},{66,2},{67,3},{68,4},{69,5},{70,6},{71,7},{72,8},{73... | collective-permute-start | bytes 786440 | tf_op jit(solution)/shard_map/ppermute | solution.py:315
Sparse Core Ops, SparseCore 0:
  20.9 72.6 all-gather.2

commit v6 on v5

--- a/solution.py
+++ b/solution.py
@@ -141,24 +141,10 @@
     )(own, far_a, far_b)
 
 
-def rows_kernel(capacity, me_ref, rows_hbm, grads_hbm, lent_0, lent_1, far_a, far_b, own_hbm,
-                rows, grads, lent, packed, far, own, sems, out_sems):
+def pick_kernel(capacity, me_ref, rows, near, other):
     experts, span, half = rows.shape
-    slots, hidden = grads.shape
     tokens = (span - 16) // 2
     quarter = half // 2
-    hs = slots // 2
-    in_copies = [
-        pltpu.make_async_copy(rows_hbm, rows, sems.at[0]),
-        pltpu.make_async_copy(grads_hbm, grads, sems.at[1]),
-    ]
-    at = 0
-    for i, part in enumerate((lent_0, lent_1)):
-        n = part.shape[0]
-        in_copies.append(pltpu.make_async_copy(part, lent.at[pl.ds(at, n)], sems.at[2 + i]))
-        at += n
-    for copy in in_copies:
-        copy.start()
     row = lax.broadcasted_iota(jnp.int32, (2 * tokens, 2 * tokens), 0)
     col = lax.broadcasted_iota(jnp.int32, (2 * tokens, 2 * tokens), 1)
     same = (row < tokens) == (col < tokens)
@@ -166,7 +152,6 @@
     me = me_ref[0].astype(f32)
     place = lax.broadcasted_iota(jnp.int32, (1, 2 * tokens), 1)
     base = jnp.where(place < tokens, 0, capacity)
-    in_copies[0].wait()
     named = []
     for s in range(experts):
         ids = rows[s, 2 * tokens :, : 2 * tokens].astype(f32)
@@ -178,61 +163,56 @@
     for s in range(experts):
         pick = jnp.where(line == where[s : s + 1, :], 1.0, 0.0).astype(bf16)
         got = jnp.dot(pick, rows[s, : 2 * tokens, :], preferred_element_type=f32).astype(bf16)
-        packed[0, s * capacity : (s + 1) * capacity, :] = got[:capacity]
-        packed[1, s * capacity : (s + 1) * capacity, :] = got[capacity:]
-    for copy in in_copies[1:]:
-        copy.wait()
+        here = pl.ds(s * capacity, capacity)
+        for p in range(2):
+            part = got[p * capacity : (p + 1) * capacity]
+            near[p, here, :] = part[:, :quarter]
+            other[p, here, :] = part[:, quarter:]
+
+
+def pick_rows(me, rows, capacity):
+    experts, span, half = rows.shape
+    vmem = pl.BlockSpec(memory_space=pltpu.VMEM)
+    out = jax.ShapeDtypeStruct((2, experts * capacity, half // 2), bf16)
+    return pl.pallas_call(
+        functools.partial(pick_kernel, capacity),
+        in_specs=[pl.BlockSpec(memory_space=pltpu.SMEM), vmem],
+        out_specs=[vmem, vmem],
+        out_shape=[out, out],
+        compiler_params=pltpu.CompilerParams(vmem_limit_bytes=20 << 20),
+        cost_estimate=pl.CostEstimate(flops=1, bytes_accessed=1, transcendentals=0),
+    )(me, rows)
+
+
+def far_kernel(rows, grads, lent_a, lent_b, far_a, far_b):
     tn = (((0,), (0,)), ((), ()))
+    hs, hidden = lent_a.shape
     part = hidden // 3
-    out_copies = []
-    for g, out in enumerate((far_a, far_b)):
-        span_g = slice(g * hs, (g + 1) * hs)
+    for g, (lent, far) in enumerate(((lent_a, far_a), (lent_b, far_b))):
+        span = pl.ds(g * hs, hs)
         for c in range(3):
-            cols = slice(c * part, (c + 1) * part)
+            cols = pl.ds(c * part, part)
             sums = lax.dot_general(
-                packed[0, span_g, quarter:], grads[span_g, cols], tn, preferred_element_type=f32
-            ) + lax.dot_general(
-                packed[1, span_g, quarter:], lent[span_g, cols], tn, preferred_element_type=f32
-            )
-            far[g, :, cols] = sums.astype(bf16)
-        out_copies.append(pltpu.make_async_copy(far.at[g], out, out_sems.at[g]))
-        out_copies[-1].start()
-    own[...] = packed[:, :, :quarter]
-    out_copies.append(pltpu.make_async_copy(own, own_hbm, out_sems.at[2]))
-    out_copies[-1].start()
-    for copy in out_copies:
-        copy.wait()
-
-
-def rows_product(me, rows, grads, lent, capacity):
-    experts, span, half = rows.shape
+                rows[0, span, :], grads[span, cols], tn, preferred_element_type=f32
+            ) + lax.dot_general(rows[1, span, :], lent[:, cols], tn, preferred_element_type=f32)
+            far[:, cols] = sums.astype(bf16)
+
+
+def far_products(rows, grads, lent):
     slots, hidden = grads.shape
-    quarter = half // 2
-    any_space = pl.BlockSpec(memory_space=pl.ANY)
-    return pl.pallas_call(
-        functools.partial(rows_kernel, capacity),
-        in_specs=[pl.BlockSpec(memory_space=pltpu.SMEM)] + [any_space] * 4,
-        out_specs=[pl.BlockSpec(memory_space=pltpu.HBM)] * 2 + [any_space],
-        out_shape=[
-            jax.ShapeDtypeStruct((quarter, hidden), bf16),
-            jax.ShapeDtypeStruct((quarter, hidden), bf16),
-            jax.ShapeDtypeStruct((2, slots, quarter), bf16),
-        ],
-        scratch_shapes=[
-            pltpu.VMEM(rows.shape, bf16),
-            pltpu.VMEM((slots, hidden), bf16),
-            pltpu.VMEM((slots, hidden), bf16),
-            pltpu.VMEM((2, slots, half), bf16),
-            pltpu.VMEM((2, quarter, hidden), bf16),
-            pltpu.VMEM((2, slots, quarter), bf16),
-            pltpu.SemaphoreType.DMA((4,)),
-            pltpu.SemaphoreType.DMA((3,)),
-        ],
+    quarter = rows.shape[2]
+    vmem = pl.BlockSpec(memory_space=pltpu.VMEM)
+    out = jax.ShapeDtypeStruct((quarter, hidden), bf16)
+    return pl.pallas_call(
+        far_kernel,
+        in_specs=[vmem] * 4,
+        out_specs=[vmem, vmem],
+        out_shape=[out, out],
         compiler_params=pltpu.CompilerParams(vmem_limit_bytes=24 << 20),
         cost_estimate=pl.CostEstimate(
             flops=60 * slots * quarter * hidden, bytes_accessed=16 << 20, transcendentals=0
         ),
-    )(me, rows, grads, *lent)
+    )(rows, grads, *lent)
 
 
 def body(w_up, saved_rows, hidden_grad, expert_ids, route_weight):
@@ -296,7 +276,8 @@
     routed = dot(held, weights, ((1,), (1,))).astype(bf16)
     routed = routed.reshape(experts, capacity, width)
     back = lax.all_to_all(routed, ZY, 0, 0, tiled=True).reshape(slots, width)
-    far_3, far_1, mine = rows_product(me[None], gathered, held, lent, capacity)
+    mine, other_rows = pick_rows(me[None], gathered, capacity)
+    far_3, far_1 = far_products(other_rows, held, lent)
     far_3 = lax.ppermute(far_3, "x", FLIP_3)
     far_1 = lax.ppermute(far_1, "x", FLIP_1)
     own = dot(mine[0], held, ((0,), (0,)))

time: 164 us -> 161 us (0.982)
  waiting for transfers between devices: 66.5 us -> 62.8 us
    ppermute x1, waiting for transfers between devices: 7.95 us -> 4.45 us  [body(): lax.ppermute(low_half, 'x', FLIP_1)]
    all_to_all x1, waiting for transfers between devices: 16.9 us -> 20.1 us  [body(): back = lax.all_to_all(routed, ZY, 0, 0, tiled=True).reshape(slots, width)]
    ppermute x1, waiting for transfers between devices: 3.17 us -> 0.01 us  [body(): far_1 = lax.ppermute(far_1, 'x', FLIP_1)]
    pallas_call x1 -> x2, Pallas kernels: 6.8 us -> 7.18 us  [the longest x1 6.06 us: far_products(): pl.pallas_call(far_kernel, in_specs=[vmem] * 4, out_specs=[vmem, vmem], o...]
  transfers between devices with their start and end apart: 15 -> 15, of which waited for: 11 -> 10; matrix products, arithmetic and copies ran while one was open for 19% -> 20% of each run, Pallas kernels for 8% -> 8%
where the time goes in v6:
time: 161 us; the launch traced here: 160 us
  waiting for transfers between devices  62.8 us (39%)
  starting transfers between devices  30.5 us (19%)
  matrix products  17.5 us (11%)
  Pallas kernels  17 us (11%)
  local copies, waits for them, and re-layouts  16.5 us (10%)
  between operations  14.2 us (9%)
  other arithmetic  1.7 us (1%)
    all_to_all x1, waiting for transfers between devices, body(): back = lax.all_to_all(routed, ZY, 0, 0, tiled=True).reshape(slots, width)  20.1 us
    dot_general x6, matrix products, dot(): return lax.dot_general(a, b, (dims, ((), ())), preferred_element_type=f32)  17.5 us
    ppermute x1, waiting for transfers between devices, body(): far_a = lax.ppermute(right_a, 'x', TO_LEFT)  14.6 us
    unnamed x17, local copies, waits for them, and re-layouts  10.8 us
    all_to_all x1, starting transfers between devices, body(): lax.all_to_all(packed, ZY, 0, 0, tiled=True).reshape(slots, hidden)  9.23 us
    all_to_all x1, starting transfers between devices, body(): back = lax.all_to_all(routed, ZY, 0, 0, tiled=True).reshape(slots, width)  8.75 us
    ppermute x1, waiting for transfers between devices, body(): far_b = lax.ppermute(left_b, 'x', TO_RIGHT)  7.35 us
    ppermute x1, waiting for transfers between devices, body(): right_b = lax.ppermute(w[mid:], 'x', TO_LEFT)  7.04 us
  transfers between devices with their start and end apart: 15, of which 10 were waited for; matrix products, arithmetic and copies ran while one was open for 20% of the time, Pallas kernels for 8%

profile of v6, /device:TPU:0, one launch (start us, length us, event | category | flops | bytes accessed | tf_op | source)
XLA Modules:
  0.0 160.2 jit_solution(10055304283469680610)
XLA Ops:
  8.2 1.0 dynamic-slice_bitcast_fusion.1
  9.2 1.7 %collective-permute-start = (bf16[72,1024]{1,0:T(8,128)(2,1)S(1)}, bf16[72,1024]{1,0:T(8,128)(2,1)S(1)}, u32[]{:S(2)}, u32[]{:S(2)}) collective-permute-start(bf16[72,1024]{1,0:T(8,128)(2,1)S(1)} %fusion.13), channel_id=1, source_target_pairs={{0,1},{1,0},{2,3},{3,2},{16,17},{17,16},{18,19},{19,18},{32,35},{3... | collective-permute-start | bytes 442376 | tf_op jit(solution)/shard_map/ppermute | solution.py:250
  10.9 2.6 %slice_bitcast_fusion = (bf16[256,1536]{1,0:T(8,128)(2,1)}, bf16[256,1536]{1,0:T(8,128)(2,1)}) fusion(bf16[1,512,1536]{2,1,0:T(8,128)(2,1)} %param.5), kind=kLoop, calls=%fused_computation.9 | loop fusion | bytes 3145728 | tf_op jit(solution)/shard_map/slice | solution.py:235
  13.5 2.1 %collective-permute-start.1 = (bf16[256,1536]{1,0:T(8,128)(2,1)}, bf16[256,1536]{1,0:T(8,128)(2,1)S(1)}, u32[]{:S(2)}, u32[]{:S(2)}) collective-permute-start(bf16[256,1536]{1,0:T(8,128)(2,1)} %get-tuple-element.31), channel_id=1, source_target_pairs={{0,3},{1,0},{2,1},{3,2},{4,7},{5,4},{6,5},{7,6},{8,11},{9,8},{10,9... | collective-permute-start | bytes 2359304 | tf_op jit(solution)/shard_map/ppermute | solution.py:233
  15.7 4.2 %shard_map.68 = bf16[768,1536]{1,0:T(8,128)(2,1)} custom-call(s32[64,8]{1,0:T(8,128)S(1)} %bitcast.55, f32[64,8]{1,0:T(8,128)S(1)} %bitcast.56, bf16[512,1536]{1,0:T(8,128)(2,1)S(1)} %bitcast.54), custom_call_target="tpu_custom_call" | custom-call | flops 1 | bytes 1 | tf_op jit(solution)/shard_map/pallas_call | solution.py:91
  20.9 9.2 %all-to-all-start = ((bf16[16,48,1536]{2,1,0:T(8,128)(2,1)}), bf16[16,48,1536]{2,1,0:T(8,128)(2,1)S(1)}, u32[]{:S(2)}, u32[]{:S(2)}) async-start(bf16[16,48,1536]{2,1,0:T(8,128)(2,1)} %bitcast.6), calls=%async_computation | async-start | bytes 4718592 | tf_op jit(solution)/shard_map/all_to_all | solution.py:269
  30.1 1.8 %collective-permute-start.2 = (bf16[256,1536]{1,0:T(8,128)(2,1)}, bf16[256,1536]{1,0:T(8,128)(2,1)S(1)}, u32[]{:S(2)}, u32[]{:S(2)}) collective-permute-start(bf16[256,1536]{1,0:T(8,128)(2,1)} %get-tuple-element.30), channel_id=1, source_target_pairs={{0,3},{1,0},{2,1},{3,2},{4,7},{5,4},{6,5},{7,6},{8,11},{9,8},{10,9... | collective-permute-start | bytes 2359304 | tf_op jit(solution)/shard_map/ppermute | solution.py:235
  32.2 1.6 collective-permute-done.1
  33.8 3.6 %collective-permute-start.3 = (bf16[256,1536]{1,0:T(8,128)(2,1)S(1)}, bf16[256,1536]{1,0:T(8,128)(2,1)S(1)}, u32[]{:S(2)}, u32[]{:S(2)}) collective-permute-start(bf16[256,1536]{1,0:T(8,128)(2,1)S(1)} %collective-permute-done.1), channel_id=1, source_target_pairs={{0,3},{1,0},{2,1},{3,2},{4,7},{5,4},{6,5},{7,6},{8,11},{9,8},{10,9... | collective-permute-start | bytes 2359304 | tf_op jit(solution)/shard_map/ppermute | solution.py:267
  37.3 2.7 %bitcast_dynamic-update-slice_fusion = bf16[2048,1536]{1,0:T(8,128)(2,1)} fusion(bf16[1,512,1536]{2,1,0:T(8,128)(2,1)} %param.5), kind=kLoop, calls=%fused_computation.5 | loop fusion | bytes 3145728
  40.0 2.8 %collective-permute-done.4 = bf16[256,1536]{1,0:T(8,128)(2,1)} collective-permute-done((bf16[256,1536]{1,0:T(8,128)(2,1)}, bf16[256,1536]{1,0:T(8,128)(2,1)}, u32[]{:S(2)}, u32[]{:S(2)}) %collective-permute-start.4) | collective-permute-done | bytes 786464 | tf_op jit(solution)/shard_map/ppermute | solution.py:234
  43.8 7.0 %collective-permute-done.2 = bf16[256,1536]{1,0:T(8,128)(2,1)S(1)} collective-permute-done((bf16[256,1536]{1,0:T(8,128)(2,1)}, bf16[256,1536]{1,0:T(8,128)(2,1)S(1)}, u32[]{:S(2)}, u32[]{:S(2)}) %collective-permute-start.2) | collective-permute-done | bytes 786464 | tf_op jit(solution)/shard_map/ppermute | solution.py:235
  51.8 14.6 %collective-permute-done.3 = bf16[256,1536]{1,0:T(8,128)(2,1)S(1)} collective-permute-done((bf16[256,1536]{1,0:T(8,128)(2,1)S(1)}, bf16[256,1536]{1,0:T(8,128)(2,1)S(1)}, u32[]{:S(2)}, u32[]{:S(2)}) %collective-permute-start.3) | collective-permute-done | bytes 786464 | tf_op jit(solution)/shard_map/ppermute | solution.py:267
  67.3 7.3 %collective-permute-done.5 = bf16[256,1536]{1,0:T(8,128)(2,1)S(1)} collective-permute-done((bf16[256,1536]{1,0:T(8,128)(2,1)}, bf16[256,1536]{1,0:T(8,128)(2,1)S(1)}, u32[]{:S(2)}, u32[]{:S(2)}) %collective-permute-start.5) | collective-permute-done | bytes 786464 | tf_op jit(solution)/shard_map/ppermute | solution.py:268
  76.6 2.1 %constant_dynamic-update-slice_fusion = bf16[2048,1536]{1,0:T(8,128)(2,1)} fusion(bf16[2048,1536]{1,0:T(8,128)(2,1)} %constant_dynamic-update-slice_fusion.1, bf16[256,1536]{1,0:T(8,128)(2,1)} %collective-permute-done.4), kind=kLoop, calls=%fused_computation.43 | loop fusion | bytes 1572864 | tf_op jit(solution)/shard_map/concatenate | solution.py:271
  78.7 1.6 shard_map.70
  80.6 9.3 %convolution_convert_fusion = bf16[768,2048]{1,0:T(8,128)(2,1)} fusion(bf16[768,1536]{1,0:T(8,128)(2,1)S(1)} %bitcast.50, bf16[2048,1536]{1,0:T(8,128)(2,1)} %constant_dynamic-update-slice_fusion), kind=kOutput, calls=%fused_computation | convolution fusion | flops 4833411072 | bytes 11796480 | tf_op jit(solution)/shard_map/dot_general | solution.py:24
  89.9 8.8 %all-to-all-start.1 = ((bf16[16,48,2048]{2,1,0:T(8,128)(2,1)}), bf16[16,48,2048]{2,1,0:T(8,128)(2,1)}, u32[]{:S(2)}, u32[]{:S(2)}) async-start(bf16[16,48,2048]{2,1,0:T(8,128)(2,1)} %bitcast.57), calls=%async_computation.1 | async-start | bytes 6291456 | tf_op jit(solution)/shard_map/all_to_all | solution.py:278
  98.7 2.3 %copy-done = bf16[2304,1024]{1,0:T(8,128)(2,1)S(1)} copy-done((bf16[2304,1024]{1,0:T(8,128)(2,1)S(1)}, bf16[2304,1024]{1,0:T(8,128)(2,1)}, u32[]{:S(2)}) %copy-start) | copy-done | bytes 4718616
  101.1 1.1 shard_map.69
  102.2 4.4 %collective-permute-done.7.lent_a = bf16[384,1536]{1,0:T(8,128)(2,1)S(1)} collective-permute-done((bf16[384,1536]{1,0:T(8,128)(2,1)}, bf16[384,1536]{1,0:T(8,128)(2,1)S(1)}, u32[]{:S(2)}, u32[]{:S(2)}) %collective-permute-start.7) | collective-permute-done | bytes 1179680 | tf_op jit(solution)/shard_map/ppermute | solution.py:275
  106.6 1.3 collective-permute-done.8.lent_b
  108.0 6.1 %shard_map.71 = (bf16[512,1536]{1,0:T(8,128)(2,1)}, bf16[512,1536]{1,0:T(8,128)(2,1)}) custom-call(bf16[2,768,512]{2,1,0:T(8,128)(2,1)S(1)} %get-tuple-element.25.rows, bf16[768,1536]{1,0:T(8,128)(2,1)S(1)} %bitcast.51, bf16[384,1536]{1,0:T(8,128)(2,1)S(1)} %collective-permute-done.7.lent_a, bf16[384,1536]{1,0:T(8,128)(2,1)} %collective-permute-done.8.lent_b), custom_call_target="tpu_custom_call" | custom-call | flops 36238786560 | bytes 16777216 | tf_op jit(solution)/shard_map/pallas_call | solution.py:206
  115.4 1.0 fusion.5
  116.4 1.5 convolution_add_fusion.1
  117.9 2.3 %convolution_add_fusion.own_ref = f32[512,1536]{1,0:T(8,128)S(1)} fusion(f32[512,1536]{1,0:T(8,128)S(1)} %convolution_add_fusion.1, bf16[384,1536]{1,0:T(8,128)(2,1)} %collective-permute-done.8.lent_b, bf16[2,768,512]{2,1,0:T(8,128)(2,1)S(1)} %get-tuple-element.19), kind=kOutput, calls=%fused_computation.1 | convolution fusion | flops 604766208 | bytes 7864320 | tf_op jit(solution)/shard_map/dot_general | solution.py:24
  120.2 20.1 %all-to-all-done.1 = bf16[16,48,2048]{2,1,0:T(8,128)(2,1)} async-done(((bf16[16,48,2048]{2,1,0:T(8,128)(2,1)}), bf16[16,48,2048]{2,1,0:T(8,128)(2,1)}, u32[]{:S(2)}, u32[]{:S(2)}) %all-to-all-start.1) | async-done | bytes 3145760 | tf_op jit(solution)/shard_map/all_to_all | solution.py:278
  140.3 3.3 %fusion = bf16[64,2048]{1,0:T(8,128)(2,1)} fusion(bf16[16,48,2048]{2,1,0:T(8,128)(2,1)} %all-to-all-done.1, s32[16,64]{1,0:T(8,128)S(1)} %fusion.1), kind=kOutput, calls=%fused_computation.4 | convolution fusion | flops 201506816 | bytes 3411968 | tf_op jit(solution)/shard_map/dot_general | solution.py:24
  143.6 1.3 collective-permute-start.11
  144.9 2.3 %collective-permute-done.11 = bf16[64,2048]{1,0:T(8,128)(2,1)S(1)} collective-permute-done((bf16[64,2048]{1,0:T(8,128)(2,1)}, bf16[64,2048]{1,0:T(8,128)(2,1)S(1)}, u32[]{:S(2)}, u32[]{:S(2)}) %collective-permute-start.11) | collective-permute-done | bytes 262176 | tf_op jit(solution)/shard_map/ppermute | solution.py:296
  148.0 1.2 collective-permute-done.9.far_a
  149.2 4.1 %shard_map.72 = bf16[512,1536]{1,0:T(8,128)(2,1)} custom-call(f32[512,1536]{1,0:T(8,128)S(1)} %convolution_add_fusion.own_ref, bf16[512,1536]{1,0:T(8,128)(2,1)} %collective-permute-done.9.far_a, bf16[512,1536]{1,0:T(8,128)(2,1)} %collective-permute-done.10.far_b), custom_call_target="tpu_custom_call" | custom-call | tf_op jit(solution)/shard_map/pallas_call | solution.py:134
  (38 shorter events, 9.8 us)
Async XLA Ops:
  7.2 8.4 %copy-start.3 = (f32[1,64,8]{1,2,0:T(8,128)S(1)}, f32[1,64,8]{1,2,0:T(8,128)}, u32[]{:S(2)}) copy-start(f32[1,64,8]{1,2,0:T(8,128)} %param.9) | copy-start | bytes 6148
  7.2 8.5 %copy-start.1 = (bf16[1,64,8,1536]{3,2,1,0:T(8,128)(2,1)S(1)}, bf16[1,64,8,1536]{3,2,1,0:T(8,128)(2,1)}, u32[]{:S(2)}) copy-start(bf16[1,64,8,1536]{3,2,1,0:T(8,128)(2,1)} %param.7) | copy-start | bytes 4718596
  7.2 91.5 %all-gather.3.cloned.1.call-start = ((), (), s32[]{:S(2)}) async-start(), calls=%async_computation.2 | async-start | bytes 5013504 | tf_op jit(solution)/shard_map/all_gather | solution.py:266
  9.2 10.7 %collective-permute-start = (bf16[72,1024]{1,0:T(8,128)(2,1)S(1)}, bf16[72,1024]{1,0:T(8,128)(2,1)S(1)}, u32[]{:S(2)}, u32[]{:S(2)}) collective-permute-start(bf16[72,1024]{1,0:T(8,128)(2,1)S(1)} %fusion.13), channel_id=1, source_target_pairs={{0,1},{1,0},{2,3},{3,2},{16,17},{17,16},{18,19},{19,18},{32,35},{3... | collective-permute-start | bytes 442376 | tf_op jit(solution)/shard_map/ppermute | solution.py:250
  13.5 20.3 %collective-permute-start.1 = (bf16[256,1536]{1,0:T(8,128)(2,1)}, bf16[256,1536]{1,0:T(8,128)(2,1)S(1)}, u32[]{:S(2)}, u32[]{:S(2)}) collective-permute-start(bf16[256,1536]{1,0:T(8,128)(2,1)} %get-tuple-element.31), channel_id=1, source_target_pairs={{0,3},{1,0},{2,1},{3,2},{4,7},{5,4},{6,5},{7,6},{8,11},{9,8},{10,9... | collective-permute-start | bytes 2359304 | tf_op jit(solution)/shard_map/ppermute | solution.py:233
  20.8 22.1 %copy-start.2 = (s32[1,64,8]{1,2,0:T(8,128)S(1)}, s32[1,64,8]{1,2,0:T(8,128)}, u32[]{:S(2)}) copy-start(s32[1,64,8]{1,2,0:T(8,128)} %param.8) | copy-start | bytes 6148
  20.8 22.1 %collective-permute-start.4 = (bf16[256,1536]{1,0:T(8,128)(2,1)}, bf16[256,1536]{1,0:T(8,128)(2,1)}, u32[]{:S(2)}, u32[]{:S(2)}) collective-permute-start(bf16[256,1536]{1,0:T(8,128)(2,1)} %get-tuple-element.30), channel_id=1, source_target_pairs={{0,1},{1,2},{2,3},{3,0},{4,5},{5,6},{6,7},{7,4},{8,9},{9,10},{10,1... | collective-permute-start | bytes 2359304 | tf_op jit(solution)/shard_map/ppermute | solution.py:234
  20.9 57.8 %all-to-all-start = ((bf16[16,48,1536]{2,1,0:T(8,128)(2,1)}), bf16[16,48,1536]{2,1,0:T(8,128)(2,1)S(1)}, u32[]{:S(2)}, u32[]{:S(2)}) async-start(bf16[16,48,1536]{2,1,0:T(8,128)(2,1)} %bitcast.6), calls=%async_computation | async-start | bytes 4718592 | tf_op jit(solution)/shard_map/all_to_all | solution.py:269
  30.1 20.8 %collective-permute-start.2 = (bf16[256,1536]{1,0:T(8,128)(2,1)}, bf16[256,1536]{1,0:T(8,128)(2,1)S(1)}, u32[]{:S(2)}, u32[]{:S(2)}) collective-permute-start(bf16[256,1536]{1,0:T(8,128)(2,1)} %get-tuple-element.30), channel_id=1, source_target_pairs={{0,3},{1,0},{2,1},{3,2},{4,7},{5,4},{6,5},{7,6},{8,11},{9,8},{10,9... | collective-permute-start | bytes 2359304 | tf_op jit(solution)/shard_map/ppermute | solution.py:235
  31.9 43.8 %collective-permute-start.6 = (bf16[256,1536]{1,0:T(8,128)(2,1)}, bf16[256,1536]{1,0:T(8,128)(2,1)S(1)}, u32[]{:S(2)}, u32[]{:S(2)}) collective-permute-start(bf16[256,1536]{1,0:T(8,128)(2,1)} %get-tuple-element.31), channel_id=1, source_target_pairs={{0,1},{1,2},{2,3},{3,0},{4,5},{5,6},{6,7},{7,4},{8,9},{9,10},{10,1... | collective-permute-start | bytes 2359304 | tf_op jit(solution)/shard_map/ppermute | solution.py:236
  33.8 32.6 %collective-permute-start.3 = (bf16[256,1536]{1,0:T(8,128)(2,1)S(1)}, bf16[256,1536]{1,0:T(8,128)(2,1)S(1)}, u32[]{:S(2)}, u32[]{:S(2)}) collective-permute-start(bf16[256,1536]{1,0:T(8,128)(2,1)S(1)} %collective-permute-done.1), channel_id=1, source_target_pairs={{0,3},{1,0},{2,1},{3,2},{4,7},{5,4},{6,5},{7,6},{8,11},{9,8},{10,9... | collective-permute-start | bytes 2359304 | tf_op jit(solution)/shard_map/ppermute | solution.py:267
  42.8 31.8 %collective-permute-start.5 = (bf16[256,1536]{1,0:T(8,128)(2,1)}, bf16[256,1536]{1,0:T(8,128)(2,1)S(1)}, u32[]{:S(2)}, u32[]{:S(2)}) collective-permute-start(bf16[256,1536]{1,0:T(8,128)(2,1)} %collective-permute-done.4), channel_id=1, source_target_pairs={{0,1},{1,2},{2,3},{3,0},{4,5},{5,6},{6,7},{7,4},{8,9},{9,10},{10,1... | collective-permute-start | bytes 2359304 | tf_op jit(solution)/shard_map/ppermute | solution.py:268
  80.2 26.4 %collective-permute-start.7 = (bf16[384,1536]{1,0:T(8,128)(2,1)}, bf16[384,1536]{1,0:T(8,128)(2,1)S(1)}, u32[]{:S(2)}, u32[]{:S(2)}) collective-permute-start(bf16[384,1536]{1,0:T(8,128)(2,1)} %get-tuple-element.22), channel_id=1, source_target_pairs={{0,1},{1,0},{2,3},{3,2},{4,5},{5,4},{6,7},{7,6},{8,9},{9,8},{10,11... | collective-permute-start | bytes 3538952 | tf_op jit(solution)/shard_map/ppermute | solution.py:275
  80.2 27.7 %collective-permute-start.8 = (bf16[384,1536]{1,0:T(8,128)(2,1)}, bf16[384,1536]{1,0:T(8,128)(2,1)}, u32[]{:S(2)}, u32[]{:S(2)}) collective-permute-start(bf16[384,1536]{1,0:T(8,128)(2,1)} %get-tuple-element.23), channel_id=1, source_target_pairs={{0,3},{1,2},{2,1},{3,0},{4,7},{5,6},{6,5},{7,4},{8,11},{9,10},{10,... | collective-permute-start | bytes 3538952 | tf_op jit(solution)/shard_map/ppermute | solution.py:275
  89.9 50.3 %all-to-all-start.1 = ((bf16[16,48,2048]{2,1,0:T(8,128)(2,1)}), bf16[16,48,2048]{2,1,0:T(8,128)(2,1)}, u32[]{:S(2)}, u32[]{:S(2)}) async-start(bf16[16,48,2048]{2,1,0:T(8,128)(2,1)} %bitcast.57), calls=%async_computation.1 | async-start | bytes 6291456 | tf_op jit(solution)/shard_map/all_to_all | solution.py:278
  98.7 2.3 %copy-start = (bf16[2304,1024]{1,0:T(8,128)(2,1)S(1)}, bf16[2304,1024]{1,0:T(8,128)(2,1)}, u32[]{:S(2)}) copy-start(bf16[2304,1024]{1,0:T(8,128)(2,1)} %all-gather.3.cloned.1.call-done) | copy-start | bytes 14155780
  114.0 34.0 %collective-permute-start.10 = (bf16[512,1536]{1,0:T(8,128)(2,1)}, bf16[512,1536]{1,0:T(8,128)(2,1)}, u32[]{:S(2)}, u32[]{:S(2)}) collective-permute-start(bf16[512,1536]{1,0:T(8,128)(2,1)} %get-tuple-element.27), channel_id=1, source_target_pairs={{0,1},{1,0},{2,3},{3,2},{4,5},{5,4},{6,7},{7,6},{8,9},{9,8},{10,11... | collective-permute-start | bytes 4718600 | tf_op jit(solution)/shard_map/ppermute | solution.py:282
  114.6 34.7 %collective-permute-start.9 = (bf16[512,1536]{1,0:T(8,128)(2,1)}, bf16[512,1536]{1,0:T(8,128)(2,1)}, u32[]{:S(2)}, u32[]{:S(2)}) collective-permute-start(bf16[512,1536]{1,0:T(8,128)(2,1)} %get-tuple-element.26), channel_id=1, source_target_pairs={{0,3},{1,2},{2,1},{3,0},{4,7},{5,6},{6,5},{7,4},{8,11},{9,10},{10,... | collective-permute-start | bytes 4718600 | tf_op jit(solution)/shard_map/ppermute | solution.py:281
  143.6 3.6 %collective-permute-start.11 = (bf16[64,2048]{1,0:T(8,128)(2,1)}, bf16[64,2048]{1,0:T(8,128)(2,1)S(1)}, u32[]{:S(2)}, u32[]{:S(2)}) collective-permute-start(bf16[64,2048]{1,0:T(8,128)(2,1)} %fusion), channel_id=1, source_target_pairs={{64,0},{65,1},{66,2},{67,3},{68,4},{69,5},{70,6},{71,7},{72,8},{73... | collective-permute-start | bytes 786440 | tf_op jit(solution)/shard_map/ppermute | solution.py:296
Sparse Core Ops, SparseCore 0:
  20.9 72.6 all-gather.2

commit v7 on v6

--- a/solution.py
+++ b/solution.py
@@ -129,14 +129,12 @@
 
 
 def scaled_sum(own, far_a, far_b):
-    rows, hidden = own.shape
-    block = pl.BlockSpec((rows // 4, hidden), lambda i: (i, 0))
+    vmem = pl.BlockSpec(memory_space=pltpu.VMEM)
     return pl.pallas_call(
         sum_kernel,
-        grid=(4,),
-        in_specs=[block] * 3,
-        out_specs=block,
-        out_shape=jax.ShapeDtypeStruct((rows, hidden), bf16),
+        in_specs=[vmem] * 3,
+        out_specs=vmem,
+        out_shape=jax.ShapeDtypeStruct(own.shape, bf16),
         compiler_params=pltpu.CompilerParams(vmem_limit_bytes=16 << 20),
     )(own, far_a, far_b)
 

time: 161 us -> 160 us (level)
  no operation moved by 1% of the time
where the time goes in v7:
time: 160 us
  waiting for transfers between devices  62.8 us (39%)
  starting transfers between devices  30.5 us (19%)
  matrix products  17.5 us (11%)
  local copies, waits for them, and re-layouts  16.5 us (10%)
  Pallas kernels  16.5 us (10%)
  between operations  14.2 us (9%)
  other arithmetic  1.7 us (1%)
    all_to_all x1, waiting for transfers between devices, body(): back = lax.all_to_all(routed, ZY, 0, 0, tiled=True).reshape(slots, width)  20.1 us
    dot_general x6, matrix products, dot(): return lax.dot_general(a, b, (dims, ((), ())), preferred_element_type=f32)  17.5 us
    ppermute x1, waiting for transfers between devices, body(): far_a = lax.ppermute(right_a, 'x', TO_LEFT)  14.6 us
    unnamed x17, local copies, waits for them, and re-layouts  10.8 us
    all_to_all x1, starting transfers between devices, body(): lax.all_to_all(packed, ZY, 0, 0, tiled=True).reshape(slots, hidden)  9.23 us
    all_to_all x1, starting transfers between devices, body(): back = lax.all_to_all(routed, ZY, 0, 0, tiled=True).reshape(slots, width)  8.75 us
    ppermute x1, waiting for transfers between devices, body(): far_b = lax.ppermute(left_b, 'x', TO_RIGHT)  7.35 us
    ppermute x1, waiting for transfers between devices, body(): right_b = lax.ppermute(w[mid:], 'x', TO_LEFT)  7.04 us
  transfers between devices with their start and end apart: 15, of which 10 were waited for; matrix products, arithmetic and copies ran while one was open for 20% of the time, Pallas kernels for 8%

profile of v7, /device:TPU:0, one launch (start us, length us, event | category | flops | bytes accessed | tf_op | source)
XLA Modules:
  0.0 159.7 jit_solution(444306139605809451)
XLA Ops:
  8.2 1.0 dynamic-slice_bitcast_fusion.1
  9.2 1.7 %collective-permute-start = (bf16[72,1024]{1,0:T(8,128)(2,1)S(1)}, bf16[72,1024]{1,0:T(8,128)(2,1)S(1)}, u32[]{:S(2)}, u32[]{:S(2)}) collective-permute-start(bf16[72,1024]{1,0:T(8,128)(2,1)S(1)} %fusion.13), channel_id=1, source_target_pairs={{0,1},{1,0},{2,3},{3,2},{16,17},{17,16},{18,19},{19,18},{32,35},{3... | collective-permute-start | bytes 442376 | tf_op jit(solution)/shard_map/ppermute | solution.py:248
  10.9 2.6 %slice_bitcast_fusion = (bf16[256,1536]{1,0:T(8,128)(2,1)}, bf16[256,1536]{1,0:T(8,128)(2,1)}) fusion(bf16[1,512,1536]{2,1,0:T(8,128)(2,1)} %param.5), kind=kLoop, calls=%fused_computation.9 | loop fusion | bytes 3145728 | tf_op jit(solution)/shard_map/slice | solution.py:233
  13.5 2.1 %collective-permute-start.1 = (bf16[256,1536]{1,0:T(8,128)(2,1)}, bf16[256,1536]{1,0:T(8,128)(2,1)S(1)}, u32[]{:S(2)}, u32[]{:S(2)}) collective-permute-start(bf16[256,1536]{1,0:T(8,128)(2,1)} %get-tuple-element.31), channel_id=1, source_target_pairs={{0,3},{1,0},{2,1},{3,2},{4,7},{5,4},{6,5},{7,6},{8,11},{9,8},{10,9... | collective-permute-start | bytes 2359304 | tf_op jit(solution)/shard_map/ppermute | solution.py:231
  15.7 4.2 %shard_map.68 = bf16[768,1536]{1,0:T(8,128)(2,1)} custom-call(s32[64,8]{1,0:T(8,128)S(1)} %bitcast.55, f32[64,8]{1,0:T(8,128)S(1)} %bitcast.56, bf16[512,1536]{1,0:T(8,128)(2,1)S(1)} %bitcast.54), custom_call_target="tpu_custom_call" | custom-call | flops 1 | bytes 1 | tf_op jit(solution)/shard_map/pallas_call | solution.py:91
  20.9 9.2 %all-to-all-start = ((bf16[16,48,1536]{2,1,0:T(8,128)(2,1)}), bf16[16,48,1536]{2,1,0:T(8,128)(2,1)S(1)}, u32[]{:S(2)}, u32[]{:S(2)}) async-start(bf16[16,48,1536]{2,1,0:T(8,128)(2,1)} %bitcast.6), calls=%async_computation | async-start | bytes 4718592 | tf_op jit(solution)/shard_map/all_to_all | solution.py:267
  30.1 1.8 %collective-permute-start.2 = (bf16[256,1536]{1,0:T(8,128)(2,1)}, bf16[256,1536]{1,0:T(8,128)(2,1)S(1)}, u32[]{:S(2)}, u32[]{:S(2)}) collective-permute-start(bf16[256,1536]{1,0:T(8,128)(2,1)} %get-tuple-element.30), channel_id=1, source_target_pairs={{0,3},{1,0},{2,1},{3,2},{4,7},{5,4},{6,5},{7,6},{8,11},{9,8},{10,9... | collective-permute-start | bytes 2359304 | tf_op jit(solution)/shard_map/ppermute | solution.py:233
  32.2 1.6 collective-permute-done.1
  33.8 3.6 %collective-permute-start.3 = (bf16[256,1536]{1,0:T(8,128)(2,1)S(1)}, bf16[256,1536]{1,0:T(8,128)(2,1)S(1)}, u32[]{:S(2)}, u32[]{:S(2)}) collective-permute-start(bf16[256,1536]{1,0:T(8,128)(2,1)S(1)} %collective-permute-done.1), channel_id=1, source_target_pairs={{0,3},{1,0},{2,1},{3,2},{4,7},{5,4},{6,5},{7,6},{8,11},{9,8},{10,9... | collective-permute-start | bytes 2359304 | tf_op jit(solution)/shard_map/ppermute | solution.py:265
  37.3 2.7 %bitcast_dynamic-update-slice_fusion = bf16[2048,1536]{1,0:T(8,128)(2,1)} fusion(bf16[1,512,1536]{2,1,0:T(8,128)(2,1)} %param.5), kind=kLoop, calls=%fused_computation.5 | loop fusion | bytes 3145728
  40.0 2.8 %collective-permute-done.4 = bf16[256,1536]{1,0:T(8,128)(2,1)} collective-permute-done((bf16[256,1536]{1,0:T(8,128)(2,1)}, bf16[256,1536]{1,0:T(8,128)(2,1)}, u32[]{:S(2)}, u32[]{:S(2)}) %collective-permute-start.4) | collective-permute-done | bytes 786464 | tf_op jit(solution)/shard_map/ppermute | solution.py:232
  43.8 7.0 %collective-permute-done.2 = bf16[256,1536]{1,0:T(8,128)(2,1)S(1)} collective-permute-done((bf16[256,1536]{1,0:T(8,128)(2,1)}, bf16[256,1536]{1,0:T(8,128)(2,1)S(1)}, u32[]{:S(2)}, u32[]{:S(2)}) %collective-permute-start.2) | collective-permute-done | bytes 786464 | tf_op jit(solution)/shard_map/ppermute | solution.py:233
  51.8 14.6 %collective-permute-done.3 = bf16[256,1536]{1,0:T(8,128)(2,1)S(1)} collective-permute-done((bf16[256,1536]{1,0:T(8,128)(2,1)S(1)}, bf16[256,1536]{1,0:T(8,128)(2,1)S(1)}, u32[]{:S(2)}, u32[]{:S(2)}) %collective-permute-start.3) | collective-permute-done | bytes 786464 | tf_op jit(solution)/shard_map/ppermute | solution.py:265
  67.3 7.3 %collective-permute-done.5 = bf16[256,1536]{1,0:T(8,128)(2,1)S(1)} collective-permute-done((bf16[256,1536]{1,0:T(8,128)(2,1)}, bf16[256,1536]{1,0:T(8,128)(2,1)S(1)}, u32[]{:S(2)}, u32[]{:S(2)}) %collective-permute-start.5) | collective-permute-done | bytes 786464 | tf_op jit(solution)/shard_map/ppermute | solution.py:266
  76.6 2.1 %constant_dynamic-update-slice_fusion = bf16[2048,1536]{1,0:T(8,128)(2,1)} fusion(bf16[2048,1536]{1,0:T(8,128)(2,1)} %constant_dynamic-update-slice_fusion.1, bf16[256,1536]{1,0:T(8,128)(2,1)} %collective-permute-done.4), kind=kLoop, calls=%fused_computation.43 | loop fusion | bytes 1572864 | tf_op jit(solution)/shard_map/concatenate | solution.py:269
  78.7 1.6 shard_map.70
  80.6 9.3 %convolution_convert_fusion = bf16[768,2048]{1,0:T(8,128)(2,1)} fusion(bf16[768,1536]{1,0:T(8,128)(2,1)S(1)} %bitcast.50, bf16[2048,1536]{1,0:T(8,128)(2,1)} %constant_dynamic-update-slice_fusion), kind=kOutput, calls=%fused_computation | convolution fusion | flops 4833411072 | bytes 11796480 | tf_op jit(solution)/shard_map/dot_general | solution.py:24
  89.9 8.8 %all-to-all-start.1 = ((bf16[16,48,2048]{2,1,0:T(8,128)(2,1)}), bf16[16,48,2048]{2,1,0:T(8,128)(2,1)}, u32[]{:S(2)}, u32[]{:S(2)}) async-start(bf16[16,48,2048]{2,1,0:T(8,128)(2,1)} %bitcast.57), calls=%async_computation.1 | async-start | bytes 6291456 | tf_op jit(solution)/shard_map/all_to_all | solution.py:276
  98.7 2.3 %copy-done = bf16[2304,1024]{1,0:T(8,128)(2,1)S(1)} copy-done((bf16[2304,1024]{1,0:T(8,128)(2,1)S(1)}, bf16[2304,1024]{1,0:T(8,128)(2,1)}, u32[]{:S(2)}) %copy-start) | copy-done | bytes 4718616
  101.1 1.1 shard_map.69
  102.2 4.4 %collective-permute-done.7.lent_a = bf16[384,1536]{1,0:T(8,128)(2,1)S(1)} collective-permute-done((bf16[384,1536]{1,0:T(8,128)(2,1)}, bf16[384,1536]{1,0:T(8,128)(2,1)S(1)}, u32[]{:S(2)}, u32[]{:S(2)}) %collective-permute-start.7) | collective-permute-done | bytes 1179680 | tf_op jit(solution)/shard_map/ppermute | solution.py:273
  106.6 1.3 collective-permute-done.8.lent_b
  108.0 6.1 %shard_map.71 = (bf16[512,1536]{1,0:T(8,128)(2,1)}, bf16[512,1536]{1,0:T(8,128)(2,1)}) custom-call(bf16[2,768,512]{2,1,0:T(8,128)(2,1)S(1)} %get-tuple-element.25.rows, bf16[768,1536]{1,0:T(8,128)(2,1)S(1)} %bitcast.51, bf16[384,1536]{1,0:T(8,128)(2,1)S(1)} %collective-permute-done.7.lent_a, bf16[384,1536]{1,0:T(8,128)(2,1)} %collective-permute-done.8.lent_b), custom_call_target="tpu_custom_call" | custom-call | flops 36238786560 | bytes 16777216 | tf_op jit(solution)/shard_map/pallas_call | solution.py:204
  115.4 1.0 fusion.5
  116.4 1.5 convolution_add_fusion.1
  117.9 2.3 %convolution_add_fusion.own_ref = f32[512,1536]{1,0:T(8,128)S(1)} fusion(f32[512,1536]{1,0:T(8,128)S(1)} %convolution_add_fusion.1, bf16[384,1536]{1,0:T(8,128)(2,1)} %collective-permute-done.8.lent_b, bf16[2,768,512]{2,1,0:T(8,128)(2,1)S(1)} %get-tuple-element.19), kind=kOutput, calls=%fused_computation.1 | convolution fusion | flops 604766208 | bytes 7864320 | tf_op jit(solution)/shard_map/dot_general | solution.py:24
  120.2 20.1 %all-to-all-done.1 = bf16[16,48,2048]{2,1,0:T(8,128)(2,1)} async-done(((bf16[16,48,2048]{2,1,0:T(8,128)(2,1)}), bf16[16,48,2048]{2,1,0:T(8,128)(2,1)}, u32[]{:S(2)}, u32[]{:S(2)}) %all-to-all-start.1) | async-done | bytes 3145760 | tf_op jit(solution)/shard_map/all_to_all | solution.py:276
  140.3 3.3 %fusion = bf16[64,2048]{1,0:T(8,128)(2,1)} fusion(bf16[16,48,2048]{2,1,0:T(8,128)(2,1)} %all-to-all-done.1, s32[16,64]{1,0:T(8,128)S(1)} %fusion.1), kind=kOutput, calls=%fused_computation.4 | convolution fusion | flops 201506816 | bytes 3411968 | tf_op jit(solution)/shard_map/dot_general | solution.py:24
  143.6 1.3 collective-permute-start.11
  144.9 2.3 %collective-permute-done.11 = bf16[64,2048]{1,0:T(8,128)(2,1)S(1)} collective-permute-done((bf16[64,2048]{1,0:T(8,128)(2,1)}, bf16[64,2048]{1,0:T(8,128)(2,1)S(1)}, u32[]{:S(2)}, u32[]{:S(2)}) %collective-permute-start.11) | collective-permute-done | bytes 262176 | tf_op jit(solution)/shard_map/ppermute | solution.py:294
  148.0 1.2 collective-permute-done.9.far_a
  149.2 3.6 %shard_map.72 = bf16[512,1536]{1,0:T(8,128)(2,1)} custom-call(f32[512,1536]{1,0:T(8,128)S(1)} %convolution_add_fusion.own_ref, bf16[512,1536]{1,0:T(8,128)(2,1)} %collective-permute-done.9.far_a, bf16[512,1536]{1,0:T(8,128)(2,1)} %collective-permute-done.10.far_b), custom_call_target="tpu_custom_call" | custom-call | tf_op jit(solution)/shard_map/pallas_call | solution.py:133
  (38 shorter events, 9.8 us)
Async XLA Ops:
  7.2 8.4 %copy-start.3 = (f32[1,64,8]{1,2,0:T(8,128)S(1)}, f32[1,64,8]{1,2,0:T(8,128)}, u32[]{:S(2)}) copy-start(f32[1,64,8]{1,2,0:T(8,128)} %param.9) | copy-start | bytes 6148
  7.2 8.5 %copy-start.1 = (bf16[1,64,8,1536]{3,2,1,0:T(8,128)(2,1)S(1)}, bf16[1,64,8,1536]{3,2,1,0:T(8,128)(2,1)}, u32[]{:S(2)}) copy-start(bf16[1,64,8,1536]{3,2,1,0:T(8,128)(2,1)} %param.7) | copy-start | bytes 4718596
  7.2 91.5 %all-gather.3.cloned.1.call-start = ((), (), s32[]{:S(2)}) async-start(), calls=%async_computation.2 | async-start | bytes 5013504 | tf_op jit(solution)/shard_map/all_gather | solution.py:264
  9.2 10.7 %collective-permute-start = (bf16[72,1024]{1,0:T(8,128)(2,1)S(1)}, bf16[72,1024]{1,0:T(8,128)(2,1)S(1)}, u32[]{:S(2)}, u32[]{:S(2)}) collective-permute-start(bf16[72,1024]{1,0:T(8,128)(2,1)S(1)} %fusion.13), channel_id=1, source_target_pairs={{0,1},{1,0},{2,3},{3,2},{16,17},{17,16},{18,19},{19,18},{32,35},{3... | collective-permute-start | bytes 442376 | tf_op jit(solution)/shard_map/ppermute | solution.py:248
  13.5 20.3 %collective-permute-start.1 = (bf16[256,1536]{1,0:T(8,128)(2,1)}, bf16[256,1536]{1,0:T(8,128)(2,1)S(1)}, u32[]{:S(2)}, u32[]{:S(2)}) collective-permute-start(bf16[256,1536]{1,0:T(8,128)(2,1)} %get-tuple-element.31), channel_id=1, source_target_pairs={{0,3},{1,0},{2,1},{3,2},{4,7},{5,4},{6,5},{7,6},{8,11},{9,8},{10,9... | collective-permute-start | bytes 2359304 | tf_op jit(solution)/shard_map/ppermute | solution.py:231
  20.8 22.1 %copy-start.2 = (s32[1,64,8]{1,2,0:T(8,128)S(1)}, s32[1,64,8]{1,2,0:T(8,128)}, u32[]{:S(2)}) copy-start(s32[1,64,8]{1,2,0:T(8,128)} %param.8) | copy-start | bytes 6148
  20.8 22.1 %collective-permute-start.4 = (bf16[256,1536]{1,0:T(8,128)(2,1)}, bf16[256,1536]{1,0:T(8,128)(2,1)}, u32[]{:S(2)}, u32[]{:S(2)}) collective-permute-start(bf16[256,1536]{1,0:T(8,128)(2,1)} %get-tuple-element.30), channel_id=1, source_target_pairs={{0,1},{1,2},{2,3},{3,0},{4,5},{5,6},{6,7},{7,4},{8,9},{9,10},{10,1... | collective-permute-start | bytes 2359304 | tf_op jit(solution)/shard_map/ppermute | solution.py:232
  20.9 57.8 %all-to-all-start = ((bf16[16,48,1536]{2,1,0:T(8,128)(2,1)}), bf16[16,48,1536]{2,1,0:T(8,128)(2,1)S(1)}, u32[]{:S(2)}, u32[]{:S(2)}) async-start(bf16[16,48,1536]{2,1,0:T(8,128)(2,1)} %bitcast.6), calls=%async_computation | async-start | bytes 4718592 | tf_op jit(solution)/shard_map/all_to_all | solution.py:267
  30.1 20.8 %collective-permute-start.2 = (bf16[256,1536]{1,0:T(8,128)(2,1)}, bf16[256,1536]{1,0:T(8,128)(2,1)S(1)}, u32[]{:S(2)}, u32[]{:S(2)}) collective-permute-start(bf16[256,1536]{1,0:T(8,128)(2,1)} %get-tuple-element.30), channel_id=1, source_target_pairs={{0,3},{1,0},{2,1},{3,2},{4,7},{5,4},{6,5},{7,6},{8,11},{9,8},{10,9... | collective-permute-start | bytes 2359304 | tf_op jit(solution)/shard_map/ppermute | solution.py:233
  31.9 43.8 %collective-permute-start.6 = (bf16[256,1536]{1,0:T(8,128)(2,1)}, bf16[256,1536]{1,0:T(8,128)(2,1)S(1)}, u32[]{:S(2)}, u32[]{:S(2)}) collective-permute-start(bf16[256,1536]{1,0:T(8,128)(2,1)} %get-tuple-element.31), channel_id=1, source_target_pairs={{0,1},{1,2},{2,3},{3,0},{4,5},{5,6},{6,7},{7,4},{8,9},{9,10},{10,1... | collective-permute-start | bytes 2359304 | tf_op jit(solution)/shard_map/ppermute | solution.py:234
  33.8 32.6 %collective-permute-start.3 = (bf16[256,1536]{1,0:T(8,128)(2,1)S(1)}, bf16[256,1536]{1,0:T(8,128)(2,1)S(1)}, u32[]{:S(2)}, u32[]{:S(2)}) collective-permute-start(bf16[256,1536]{1,0:T(8,128)(2,1)S(1)} %collective-permute-done.1), channel_id=1, source_target_pairs={{0,3},{1,0},{2,1},{3,2},{4,7},{5,4},{6,5},{7,6},{8,11},{9,8},{10,9... | collective-permute-start | bytes 2359304 | tf_op jit(solution)/shard_map/ppermute | solution.py:265
  42.8 31.8 %collective-permute-start.5 = (bf16[256,1536]{1,0:T(8,128)(2,1)}, bf16[256,1536]{1,0:T(8,128)(2,1)S(1)}, u32[]{:S(2)}, u32[]{:S(2)}) collective-permute-start(bf16[256,1536]{1,0:T(8,128)(2,1)} %collective-permute-done.4), channel_id=1, source_target_pairs={{0,1},{1,2},{2,3},{3,0},{4,5},{5,6},{6,7},{7,4},{8,9},{9,10},{10,1... | collective-permute-start | bytes 2359304 | tf_op jit(solution)/shard_map/ppermute | solution.py:266
  80.2 26.4 %collective-permute-start.7 = (bf16[384,1536]{1,0:T(8,128)(2,1)}, bf16[384,1536]{1,0:T(8,128)(2,1)S(1)}, u32[]{:S(2)}, u32[]{:S(2)}) collective-permute-start(bf16[384,1536]{1,0:T(8,128)(2,1)} %get-tuple-element.22), channel_id=1, source_target_pairs={{0,1},{1,0},{2,3},{3,2},{4,5},{5,4},{6,7},{7,6},{8,9},{9,8},{10,11... | collective-permute-start | bytes 3538952 | tf_op jit(solution)/shard_map/ppermute | solution.py:273
  80.2 27.7 %collective-permute-start.8 = (bf16[384,1536]{1,0:T(8,128)(2,1)}, bf16[384,1536]{1,0:T(8,128)(2,1)}, u32[]{:S(2)}, u32[]{:S(2)}) collective-permute-start(bf16[384,1536]{1,0:T(8,128)(2,1)} %get-tuple-element.23), channel_id=1, source_target_pairs={{0,3},{1,2},{2,1},{3,0},{4,7},{5,6},{6,5},{7,4},{8,11},{9,10},{10,... | collective-permute-start | bytes 3538952 | tf_op jit(solution)/shard_map/ppermute | solution.py:273
  89.9 50.3 %all-to-all-start.1 = ((bf16[16,48,2048]{2,1,0:T(8,128)(2,1)}), bf16[16,48,2048]{2,1,0:T(8,128)(2,1)}, u32[]{:S(2)}, u32[]{:S(2)}) async-start(bf16[16,48,2048]{2,1,0:T(8,128)(2,1)} %bitcast.57), calls=%async_computation.1 | async-start | bytes 6291456 | tf_op jit(solution)/shard_map/all_to_all | solution.py:276
  98.7 2.3 %copy-start = (bf16[2304,1024]{1,0:T(8,128)(2,1)S(1)}, bf16[2304,1024]{1,0:T(8,128)(2,1)}, u32[]{:S(2)}) copy-start(bf16[2304,1024]{1,0:T(8,128)(2,1)} %all-gather.3.cloned.1.call-done) | copy-start | bytes 14155780
  114.0 34.0 %collective-permute-start.10 = (bf16[512,1536]{1,0:T(8,128)(2,1)}, bf16[512,1536]{1,0:T(8,128)(2,1)}, u32[]{:S(2)}, u32[]{:S(2)}) collective-permute-start(bf16[512,1536]{1,0:T(8,128)(2,1)} %get-tuple-element.27), channel_id=1, source_target_pairs={{0,1},{1,0},{2,3},{3,2},{4,5},{5,4},{6,7},{7,6},{8,9},{9,8},{10,11... | collective-permute-start | bytes 4718600 | tf_op jit(solution)/shard_map/ppermute | solution.py:280
  114.6 34.7 %collective-permute-start.9 = (bf16[512,1536]{1,0:T(8,128)(2,1)}, bf16[512,1536]{1,0:T(8,128)(2,1)}, u32[]{:S(2)}, u32[]{:S(2)}) collective-permute-start(bf16[512,1536]{1,0:T(8,128)(2,1)} %get-tuple-element.26), channel_id=1, source_target_pairs={{0,3},{1,2},{2,1},{3,0},{4,7},{5,6},{6,5},{7,4},{8,11},{9,10},{10,... | collective-permute-start | bytes 4718600 | tf_op jit(solution)/shard_map/ppermute | solution.py:279
  143.6 3.6 %collective-permute-start.11 = (bf16[64,2048]{1,0:T(8,128)(2,1)}, bf16[64,2048]{1,0:T(8,128)(2,1)S(1)}, u32[]{:S(2)}, u32[]{:S(2)}) collective-permute-start(bf16[64,2048]{1,0:T(8,128)(2,1)} %fusion), channel_id=1, source_target_pairs={{64,0},{65,1},{66,2},{67,3},{68,4},{69,5},{70,6},{71,7},{72,8},{73... | collective-permute-start | bytes 786440 | tf_op jit(solution)/shard_map/ppermute | solution.py:294
Sparse Core Ops, SparseCore 0:
  20.9 72.6 all-gather.2
